TPU v7x, 32 devices: a whole 2x2x4 slice. The times are simulated.
32 devices in a mesh: blk: 4 (over y, x), grp: 8 (over z, core).
Axes of the slice: x: 2, y: 2, z: 4, core: 2. Of those that a mesh axis runs over, the one named last changes fastest.
Arguments:
- green_blocks: bfloat16 [96, 65536], P('blk', 'grp'), may hold values from -6 to 6
- chol_slab: bfloat16 [65536, 8192], P('grp', 'blk'), may hold values from -0.09375 to 0.09375
- aux_fields: bfloat16 [96, 8192], P('grp', 'blk'), may hold values from -6 to 6
Outputs:
- force_bias: float32 [96, 8192], P('grp', 'blk')
- field_term: bfloat16 [96, 65536], P('blk', 'grp')
All inputs are finite; a program needn't handle non-finite values.
Results may differ from a plain program's by a relative error of at most 0.0049.
Values may be sent and summed in bfloat16 or wider, within the bound.
No kernel may reach another device: no remote copies, remote signals or barrier semaphores. Data moves between devices by JAX's collectives and lax.ppermute only.
A program may use at most 64 MiB of HBM per device.

v0:
```python
import jax
import jax.numpy as jnp
from jax import lax
from jax.sharding import PartitionSpec as P

tau_root = 0.1


def local(green_blocks, chol_slab, aux_fields):
    partial_value = jnp.dot(
        lax.all_gather(green_blocks, "blk", axis=0, tiled=True),
        chol_slab,
        preferred_element_type=jnp.float32,
    )
    bias_own = lax.psum_scatter(partial_value, "grp", scatter_dimension=0, tiled=True)
    field_own = (aux_fields.astype(jnp.float32) + tau_root * bias_own).astype(jnp.bfloat16)
    field_all = lax.all_gather(field_own, "grp", axis=0, tiled=True)
    summed = lax.psum_scatter(
        lax.dot_general(
            field_all, chol_slab, (((1,), (1,)), ((), ())), preferred_element_type=jnp.float32
        ),
        "blk",
        scatter_dimension=0,
        tiled=True,
    )
    result = summed.astype(jnp.bfloat16)
    return (bias_own, result)


def solution(mesh):
    placed = (P("blk", "grp"), P("grp", "blk"), P("grp", "blk"))
    return jax.shard_map(
        local,
        mesh=mesh,
        in_specs=placed,
        out_specs=(P("grp", "blk"), P("blk", "grp")),
        check_vma=False,
    )
```

profile of v0, /device:TPU:0, one launch (start us, length us, event | category | flops | bytes accessed | tf_op | source)
XLA Modules:
  0.0 169.9 jit_solution(9164907002657391338)
XLA Ops:
  7.2 0.0 copy-start.1
  7.2 0.0 copy-start
  7.2 0.0 all-gather.3.cloned.1.call-start
  7.2 0.7 all-gather.3.cloned.1.call-update
  7.9 0.0 reduce-scatter.6.cloned.1.call-start
  8.0 35.6 %all-gather.3.cloned.1.call-done = bf16[96,8192]{1,0:T(8,128)(2,1)} async-done(((bf16[24,8192]{1,0:T(8,128)(2,1)}), bf16[96,8192]{1,0:T(8,128)(2,1)}) %all-gather.3.cloned.1.call-update) | async-done | bytes 1572880 | tf_op jit(solution)/shard_map/all_gather | solution.py:11
  43.6 13.8 %fusion.2 = f32[96,2048]{1,0:T(8,128)S(1)} fusion(bf16[96,8192]{1,0:T(8,128)(2,1)} %all-gather.3.cloned.1.call-done, bf16[8192,2048]{1,0:T(8,128)(2,1)} %param.4), kind=kOutput, calls=%fused_computation.3 | convolution fusion | flops 3221225472 | bytes 35913728 | tf_op jit(solution)/shard_map/dot_general | solution.py:10
  57.4 21.9 %fusion = f32[16,2048]{1,0:T(8,128)S(1)} fusion(f32[96,2048]{1,0:T(8,128)S(1)} %fusion.2), kind=kCustom, calls=%all-reduce-scatter | all-reduce-scatter fusion | flops 262145 | bytes 918016
  79.2 1.3 collective-permute-start
  80.6 1.3 collective-permute-start.1
  81.9 0.0 copy-done.1
  81.9 0.6 dynamic-slice.6
  83.1 1.7 collective-permute-done.1
  84.8 0.0 collective-permute-done
  84.8 0.4 concatenate
  85.2 0.0 copy-done
  85.2 0.7 fusion.1
  85.8 14.9 %all-gather = bf16[8,12,2048]{2,1,0:T(8,128)(2,1)S(1)} all-gather(bf16[1,12,2048]{2,1,0:T(8,128)(2,1)S(1)} %get-tuple-element.2), channel_id=1, replica_groups=mesh['blk'=4,'grp'=8] {'grp'}, dimensions={0}, use_global_device_ids=true | all-gather | bytes 442368 | tf_op jit(solution)/shard_map/all_gather | solution.py:17
  100.8 0.1 reshape.5
  100.9 16.5 %fusion.3 = f32[96,8192]{1,0:T(8,128)} fusion(bf16[96,2048]{1,0:T(8,128)(2,1)S(1)} %reshape.5, bf16[8192,2048]{1,0:T(8,128)(2,1)} %param.4), kind=kOutput, calls=%fused_computation.4 | convolution fusion | flops 3221225472 | bytes 37093376 | tf_op jit(solution)/shard_map/dot_general | solution.py:19
  117.4 0.0 reduce-scatter.6.cloned.1.call-update
  117.4 43.8 %reduce-scatter.6.cloned.1.call-done = f32[24,8192]{1,0:T(8,128)} async-done(((f32[96,8192]{1,0:T(8,128)}), f32[24,8192]{1,0:T(8,128)}) %reduce-scatter.6.cloned.1.call-update) | async-done | bytes 786448
  161.2 1.9 %convert_element_type.11 = bf16[24,8192]{1,0:T(8,128)(2,1)} convert(f32[24,8192]{1,0:T(8,128)} %reduce-scatter.6.cloned.1.call-done) | non-fusion elementwise | flops 196608 | bytes 1179648 | tf_op jit(solution)/shard_map/convert_element_type | solution.py:26
  (1 shorter events, 0.0 us)
Async XLA Ops:
  7.2 74.7 %copy-start.1 = (u32[32]{0:T(128)S(1)}, u32[32]{0:T(128)}, u32[]{:S(2)}) copy-start(u32[32]{0:T(128)} %constant.5) | copy-start | bytes 388
  7.2 78.0 %copy-start = (bf16[12,2048]{1,0:T(8,128)(2,1)S(1)}, bf16[12,2048]{1,0:T(8,128)(2,1)}, u32[]{:S(2)}) copy-start(bf16[12,2048]{1,0:T(8,128)(2,1)} %param.5) | copy-start | bytes 147460
  7.2 36.4 %all-gather.3.cloned.1.call-start = ((), (), s32[]{:S(2)}) async-start(), calls=%async_computation.1 | async-start | bytes 1966080 | tf_op jit(solution)/shard_map/all_gather | solution.py:11
  7.9 153.3 %reduce-scatter.6.cloned.1.call-start = ((), (), s32[]{:S(2)}) async-start(), calls=%async_computation.2 | async-start | bytes 3932160
  79.2 5.5 %collective-permute-start = (f32[16,2048]{1,0:T(8,128)S(1)}, f32[16,2048]{1,0:T(8,128)S(1)}, u32[]{:S(2)}, u32[]{:S(2)}) collective-permute-start(f32[16,2048]{1,0:T(8,128)S(1)} %fusion), channel_id=1, source_target_pairs={{0,1},{1,2},{2,3},{3,4},{4,5},{5,6},{6,7},{8,9},{9,10},{10,11},{11... | collective-permute-start | bytes 393224
  80.6 4.2 %collective-permute-start.1 = (f32[12,2048]{1,0:T(8,128)S(1)}, f32[12,2048]{1,0:T(8,128)S(1)}, u32[]{:S(2)}, u32[]{:S(2)}) collective-permute-start(f32[12,2048]{1,0:T(8,128)S(1)} %slice), channel_id=1, source_target_pairs={{0,2},{1,3},{2,4},{3,5},{4,6},{5,7},{8,10},{9,11},{10,12},{11,13},... | collective-permute-start | bytes 294920
Sparse Core Ops, SparseCore 0:
  9.9 33.6 all-gather.2
  117.5 43.5 reduce-scatter.5
where the time goes:
time: 170 us
  waiting for transfers between devices  81.7 us (48%)
  blocking collectives  36.8 us (22%)
  matrix products  30.3 us (18%)
  between operations  14.8 us (9%)
  starting transfers between devices  2.67 us (2%)
  other arithmetic  2.6 us (2%)
    unnamed x5, waiting for transfers between devices  46.1 us
    all_gather x1, waiting for transfers between devices, local(): lax.all_gather(green_blocks, 'blk', axis=0, tiled=True)  35.6 us
    unnamed x1, blocking collectives  21.9 us
    dot_general x1, matrix products, local(): lax.dot_general(field_all, chol_slab, (((1,), (1,)), ((), ())), preferred...  16.5 us
    all_gather x1, blocking collectives, local(): field_all = lax.all_gather(field_own, 'grp', axis=0, tiled=True)  14.9 us
    dot_general x1, matrix products, local(): jnp.dot(lax.all_gather(green_blocks, 'blk', axis=0, tiled=True), chol_sla...  13.8 us
  transfers between devices with their start and end apart: 4, of which 3 were waited for; matrix products, arithmetic and copies ran while one was open for 0% of the time, Pallas kernels for 0%

commit v1 on v0

v1 whole, which is shorter than its diff:
```python
import jax
import jax.numpy as jnp
from jax import lax
from jax.experimental import pallas as pl
from jax.experimental.pallas import tpu as pltpu
from jax.sharding import PartitionSpec as P

tau_root = 0.1
f32, bf16 = jnp.float32, jnp.bfloat16
VMEM = pl.BlockSpec(memory_space=pltpu.VMEM)
PAD = 32


def general(green_blocks, chol_slab, aux_fields):
    partial_value = jnp.dot(
        lax.all_gather(green_blocks, "blk", axis=0, tiled=True),
        chol_slab,
        preferred_element_type=f32,
    )
    bias_own = lax.psum_scatter(partial_value, "grp", scatter_dimension=0, tiled=True)
    field_own = (aux_fields.astype(f32) + tau_root * bias_own).astype(bf16)
    field_all = lax.all_gather(field_own, "grp", axis=0, tiled=True)
    summed = lax.psum_scatter(
        lax.dot_general(
            field_all, chol_slab, (((1,), (1,)), ((), ())), preferred_element_type=f32
        ),
        "blk",
        scatter_dimension=0,
        tiled=True,
    )
    return bias_own, summed.astype(bf16)


def swap(x, axis, bit):
    n = lax.axis_size(axis)
    return lax.ppermute(x, axis, [(i, i ^ bit) for i in range(n)])


def call(body, outs, *args, mib=8, flops=0, nbytes=1 << 18, ins=None, scratch=()):
    return pl.pallas_call(
        body,
        out_shape=outs,
        in_specs=ins or [VMEM] * len(args),
        out_specs=jax.tree.map(lambda _: VMEM, outs),
        scratch_shapes=scratch,
        compiler_params=pltpu.CompilerParams(vmem_limit_bytes=mib << 20),
        cost_estimate=pl.CostEstimate(flops=flops, bytes_accessed=nbytes, transcendentals=0),
    )(*args)


def struct(shape, dtype):
    return jax.ShapeDtypeStruct(shape, dtype)


def load_chunk(chol, i, rows):
    cols = chol.shape[1]
    parts = 4
    step = rows // parts

    def body(c_ref, o_ref, sems):
        copies = [
            pltpu.make_async_copy(
                c_ref.at[pl.ds(i * rows + p * step, step)],
                o_ref.at[pl.ds(p * step, step)],
                sems.at[p],
            )
            for p in range(parts)
        ]
        for c in copies:
            c.start()
        for c in copies:
            c.wait()

    return call(
        body,
        pltpu.VMEM((rows, cols), chol.dtype),
        pltpu.with_memory_space_constraint(chol, pltpu.HBM),
        nbytes=2 * rows * cols * 2,
        ins=[pl.BlockSpec(memory_space=pl.ANY)],
        scratch=[pltpu.SemaphoreType.DMA((parts,))],
    )


def ids():
    blk, grp = lax.axis_index("blk"), lax.axis_index("grp")
    return blk, grp // 2, grp % 2


def fast(green, chol, aux):
    wb, depth = green.shape
    width = chol.shape[1]
    wg = aux.shape[0]
    half, hd = width // 2, depth // 2
    n_chunks = depth // width

    def split(g_ref, aux_ref, a_ref, b_ref, sent_ref, sems):
        copies = [
            pltpu.make_async_copy(g_ref.at[:, pl.ds(h * hd, hd)], r, sems.at[h])
            for h, r in enumerate((a_ref, b_ref))
        ]
        for c in copies:
            c.start()
        _, _, core = ids()
        sent_ref[...] = aux_ref[:, pl.ds(pl.multiple_of((1 - core) * half, half), half)]
        for c in copies:
            c.wait()

    ga, gb, aux_sent = call(
        split,
        (struct((wb, hd), bf16), struct((wb, hd), bf16), struct((wg, half), bf16)),
        green, aux,
        ins=[pl.BlockSpec(memory_space=pl.ANY), VMEM],
        scratch=[pltpu.SemaphoreType.DMA((2,))],
    )
    xb, ya = swap(gb, "blk", 1), swap(ga, "blk", 2)
    xa, yb = swap(ga, "blk", 1), swap(gb, "blk", 2)
    da, db = swap(ya, "blk", 1), swap(xb, "blk", 2)
    chunks = [load_chunk(chol, i, width) for i in range(n_chunks)]

    aux_got = swap(aux_sent, "grp", 1)

    def bias_half(all_ref, chunk_refs, offset):
        total = None
        for k, c in enumerate(chunk_refs):
            term = jnp.dot(
                all_ref[:, k * width : (k + 1) * width],
                c[:, pl.ds(pl.multiple_of(offset, half), half)],
                preferred_element_type=f32,
            )
            total = term if total is None else total + term
        return total

    def first(*refs):
        pieces, chunk_refs, (all_ref, sent_ref) = refs[:8], refs[8:-2], refs[-2:]
        blk, _, core = ids()
        for p in range(4):
            rows = pl.ds(p * PAD, wb)
            all_ref[rows, :hd] = pieces[2 * p][...]
            all_ref[rows, hd:] = pieces[2 * p + 1][...]
            all_ref[pl.ds(p * PAD + wb, PAD - wb), :] = jnp.zeros((PAD - wb, depth), bf16)
        total = bias_half(all_ref, chunk_refs, (1 - core) * half)
        for p in range(4):
            sent_ref[blk ^ p] = total[p * PAD : p * PAD + wb].astype(bf16)

    flops1 = 2 * 128 * depth * half
    g_all, sent = call(
        first,
        (struct((4 * PAD, depth), bf16), struct((4, wb, half), bf16)),
        ga, gb, xa, xb, ya, yb, da, db, *chunks,
        flops=flops1,
    )
    other = swap(sent, "grp", 1)

    def second(*refs):
        all_ref, chunk_refs, out_ref = refs[0], refs[1:-1], refs[-1]
        blk, _, core = ids()
        total = bias_half(all_ref, chunk_refs, core * half)
        for p in range(4):
            out_ref[blk ^ p] = total[p * PAD : p * PAD + wb]

    mine = call(second, struct((4, wb, half), f32), g_all, *chunks, flops=flops1)

    def combine(mine_ref, other_ref, keep_ref, *sent_refs):
        _, z, _ = ids()
        keep_ref[...] = mine_ref[z] + other_ref[z].astype(f32)
        for t, s in enumerate(sent_refs, 1):
            s[...] = (mine_ref[z ^ t] + other_ref[z ^ t].astype(f32)).astype(bf16)

    keep, *sums = call(
        combine, (struct((wb, half), f32),) + (struct((wb, half), bf16),) * 3, mine, other
    )
    sums = [swap(s, "grp", 2 * t) for t, s in enumerate(sums, 1)]

    def shift(keep_ref, r1, r2, r3, aux_ref, got_ref, bias_ref, give_ref, out_ref):
        _, _, core = ids()
        bias = keep_ref[...]
        for r in (r1, r2, r3):
            bias = bias + r[...].astype(f32)
        bias_ref[...] = bias
        give_ref[...] = jnp.where(core == 0, bias[wg:], bias[:wg])
        own = aux_ref[:, pl.ds(pl.multiple_of(core * half, half), half)].astype(f32)
        got = got_ref[...].astype(f32)
        top = jnp.where(core == 0, own, got)
        low = jnp.where(core == 0, got, own)
        out_ref[...] = (jnp.concatenate([top, low], 0) + tau_root * bias).astype(bf16)

    bias, give, shifted = call(
        shift,
        (struct((wb, half), f32), struct((wg, half), f32), struct((wb, half), bf16)),
        keep, *sums, aux, aux_got,
    )
    blocks = [shifted] + [swap(shifted, "grp", 2 * t) for t in (1, 2, 3)]
    bias_got = swap(give, "grp", 1)

    def arrange(*refs):
        ins, out_ref = refs[:4], refs[4]
        blk, z, _ = ids()
        for t in range(4):
            out_ref[z ^ t ^ blk, :wb] = ins[t][...]
            out_ref[t, wb:] = jnp.zeros((PAD - wb, half), bf16)

    s_mine = call(arrange, struct((4, PAD, half), bf16), *blocks)
    s_other = swap(s_mine, "grp", 1)

    def field(mine_ref, other_ref, ca, cb, sx, sy, xb_ref, ya_ref, own_a, own_b, all_ref):
        _, _, core = ids()
        for ref, at in ((mine_ref, core), (other_ref, 1 - core)):
            all_ref[:, pl.ds(pl.multiple_of(at * half, half), half)] = ref[...].reshape(4 * PAD, half)
        for c, own, s, two, left in ((ca, own_a, sx, 1, ya_ref), (cb, own_b, sy, 2, xb_ref)):
            total = lax.dot_general(
                all_ref[...], c[...], (((1,), (1,)), ((), ())), preferred_element_type=f32
            )
            block = [total[p * PAD : p * PAD + wb] for p in range(4)]
            own[...] = block[0]
            s[0] = block[3].astype(bf16)
            s[1] = block[two].astype(bf16)
            left[...] = block[3 - two]

    def forward(rx, ry, xb_ref, ya_ref, own_a, own_b, sx, sy, new_a, new_b):
        sx[...] = (xb_ref[...] + ry[0].astype(f32)).astype(bf16)
        sy[...] = (ya_ref[...] + rx[0].astype(f32)).astype(bf16)
        new_a[...] = own_a[...] + rx[1].astype(f32)
        new_b[...] = own_b[...] + ry[1].astype(f32)

    one32, one16 = struct((wb, width), f32), struct((wb, width), bf16)
    two16 = struct((2, wb, width), bf16)
    pairs = range(n_chunks // 2)
    stage = [
        call(
            field,
            (two16, two16, one32, one32, one32, one32),
            s_mine, s_other, chunks[2 * i], chunks[2 * i + 1],
            flops=4 * 128 * width * width,
            scratch=[pltpu.VMEM((4 * PAD, width), bf16)],
        )
        for i in pairs
    ]
    got = [(swap(s[0], "blk", 1), swap(s[1], "blk", 2)) for s in stage]
    stage = [
        call(forward, (one16, one16, one32, one32), *got[i], *stage[i][2:]) for i in pairs
    ]
    got = [(swap(s[0], "blk", 1), swap(s[1], "blk", 2)) for s in stage]

    def final(*refs):
        out_ref = refs[-1]
        for i in pairs:
            own_a, own_b, rx, ry = refs[4 * i : 4 * i + 4]
            at = 2 * i * width
            out_ref[:, at : at + width] = (own_a[...] + ry[...].astype(f32)).astype(bf16)
            at += width
            out_ref[:, at : at + width] = (own_b[...] + rx[...].astype(f32)).astype(bf16)

    result = call(
        final,
        struct((wb, depth), bf16),
        *[r for i in pairs for r in (*stage[i][2:], *got[i])],
    )

    def own_bias(bias_ref, got_ref, out_ref):
        _, _, core = ids()
        b = bias_ref[...]
        out_ref[:, pl.ds(pl.multiple_of(core * half, half), half)] = jnp.where(
            core == 0, b[:wg], b[wg:]
        )
        out_ref[:, pl.ds(pl.multiple_of((1 - core) * half, half), half)] = got_ref[...]

    bias_own = call(own_bias, struct((wg, width), f32), bias, bias_got)
    return bias_own, result


def solution(mesh):
    blk, grp = mesh.shape["blk"], mesh.shape["grp"]

    def local(green, chol, aux):
        plane = blk == 4 and grp == 8
        fits = chol.shape[0] % (2 * chol.shape[1]) == 0 and green.shape[0] == 2 * aux.shape[0]
        return (fast if plane and fits and green.shape[0] <= PAD else general)(green, chol, aux)

    placed = (P("blk", "grp"), P("grp", "blk"), P("grp", "blk"))
    return jax.shard_map(
        local,
        mesh=mesh,
        in_specs=placed,
        out_specs=(P("grp", "blk"), P("blk", "grp")),
        check_vma=False,
    )
```

time: 170 us -> 81.1 us (0.48)
  waiting for transfers between devices: 81.7 us -> 20.4 us
  blocking collectives: 36.8 us -> 0 us
  Pallas kernels: 0 us -> 31.8 us
  matrix products: 30.3 us -> 0 us
  starting transfers between devices: 2.67 us -> 26 us
  between operations: 14.8 us -> 0.82 us
  other arithmetic: 2.6 us -> 0 us
    unnamed x5 -> x0, waiting for transfers between devices: 46.1 us -> none
    all_gather x1 -> x0, waiting for transfers between devices: 35.6 us -> none  [local(): lax.all_gather(green_blocks, 'blk', axis=0, tiled=True)]
    pallas_call x0 -> x16, Pallas kernels: none -> 31.8 us  [call(): pl.pallas_call(body, out_shape=outs, in_specs=ins or [VMEM] * len(args),...]
    dot_general x2 -> x0, matrix products: 30.3 us -> none  [the longest x1 16.5 us: local(): lax.dot_general(field_all, chol_slab, (((1,), (1,)), ((), ())), preferred...]
    ppermute x0 -> x24, starting transfers between devices: none -> 26 us  [swap(): return lax.ppermute(x, axis, [(i, i ^ bit) for i in range(n)])]
    unnamed x1 -> x0, blocking collectives: 21.9 us -> none
    ppermute x0 -> x24, waiting for transfers between devices: none -> 20.4 us  [swap(): return lax.ppermute(x, axis, [(i, i ^ bit) for i in range(n)])]
    all_gather x1 -> x0, blocking collectives: 14.9 us -> none  [local(): field_all = lax.all_gather(field_own, 'grp', axis=0, tiled=True)]
  transfers between devices with their start and end apart: 4 -> 24, of which waited for: 3 -> 13; matrix products, arithmetic and copies ran while one was open for 0% -> 0% of each run, Pallas kernels for 0% -> 28%
where the time goes in v1:
time: 81.1 us; the launch traced here: 80.9 us
  Pallas kernels  31.8 us (39%)
  starting transfers between devices  26 us (32%)
  waiting for transfers between devices  20.4 us (25%)
  local copies, waits for them, and re-layouts  1.83 us (2%)
  between operations  0.82 us (1%)
    pallas_call x16, Pallas kernels, call(): pl.pallas_call(body, out_shape=outs, in_specs=ins or [VMEM] * len(args),...  31.8 us
    ppermute x24, starting transfers between devices, swap(): return lax.ppermute(x, axis, [(i, i ^ bit) for i in range(n)])  26 us
    ppermute x24, waiting for transfers between devices, swap(): return lax.ppermute(x, axis, [(i, i ^ bit) for i in range(n)])  20.4 us
    unnamed x6, local copies, waits for them, and re-layouts  1.83 us
  transfers between devices with their start and end apart: 24, of which 13 were waited for; matrix products, arithmetic and copies ran while one was open for 0% of the time, Pallas kernels for 28%

profile of v1, /device:TPU:0, one launch (start us, length us, event | category | flops | bytes accessed | tf_op | source)
XLA Modules:
  0.0 80.9 jit_solution(9425630798591774993)
XLA Ops:
  2.7 3.0 %collective-permute-start.2 = (bf16[24,4096]{1,0:T(8,128)(2,1)S(1)}, bf16[24,4096]{1,0:T(8,128)(2,1)S(1)}, u32[]{:S(2)}, u32[]{:S(2)}) collective-permute-start(bf16[24,4096]{1,0:T(8,128)(2,1)S(1)} %get-tuple-element.34.refs_0_), channel_id=1, source_target_pairs={{0,16},{8,24},{16,0},{24,8},{1,17},{9,25},{17,1},{25,9},{2,18},{10... | collective-permute-start | bytes 589832 | tf_op jit(solution)/shard_map/ppermute | solution.py:36
  5.7 1.5 %collective-permute-start.1 = (bf16[24,4096]{1,0:T(8,128)(2,1)S(1)}, bf16[24,4096]{1,0:T(8,128)(2,1)S(1)}, u32[]{:S(2)}, u32[]{:S(2)}) collective-permute-start(bf16[24,4096]{1,0:T(8,128)(2,1)S(1)} %get-tuple-element.35.refs_1_), channel_id=1, source_target_pairs={{0,8},{8,0},{16,24},{24,16},{1,9},{9,1},{17,25},{25,17},{2,10},{10... | collective-permute-start | bytes 589832 | tf_op jit(solution)/shard_map/ppermute | solution.py:36
  7.8 3.6 %collective-permute-done.2.refs_4_ = bf16[24,4096]{1,0:T(8,128)(2,1)S(1)} collective-permute-done((bf16[24,4096]{1,0:T(8,128)(2,1)S(1)}, bf16[24,4096]{1,0:T(8,128)(2,1)S(1)}, u32[]{:S(2)}, u32[]{:S(2)}) %collective-permute-start.2) | collective-permute-done | bytes 196640 | tf_op jit(solution)/shard_map/ppermute | solution.py:36
  11.4 2.0 %collective-permute-start.4 = (bf16[24,4096]{1,0:T(8,128)(2,1)S(1)}, bf16[24,4096]{1,0:T(8,128)(2,1)S(1)}, u32[]{:S(2)}, u32[]{:S(2)}) collective-permute-start(bf16[24,4096]{1,0:T(8,128)(2,1)S(1)} %collective-permute-done.2.refs_4_), channel_id=1, source_target_pairs={{0,8},{8,0},{16,24},{24,16},{1,9},{9,1},{17,25},{25,17},{2,10},{10... | collective-permute-start | bytes 589832 | tf_op jit(solution)/shard_map/ppermute | solution.py:36
  15.0 3.5 %shard_map.52.refs_9_.refs_2_.cb = bf16[2048,2048]{1,0:T(8,128)(2,1)S(1)} custom-call(bf16[8192,2048]{1,0:T(8,128)(2,1)} %c_ref.7), custom_call_target="tpu_custom_call" | custom-call | bytes 16777216 | tf_op jit(solution)/shard_map/pallas_call | solution.py:40
  18.5 3.5 %shard_map.51.refs_8_.refs_1_.ca = bf16[2048,2048]{1,0:T(8,128)(2,1)S(1)} custom-call(bf16[8192,2048]{1,0:T(8,128)(2,1)} %c_ref.7), custom_call_target="tpu_custom_call" | custom-call | bytes 16777216 | tf_op jit(solution)/shard_map/pallas_call | solution.py:40
  22.0 3.5 %shard_map.54.refs_11_.refs_4_.cb = bf16[2048,2048]{1,0:T(8,128)(2,1)S(1)} custom-call(bf16[8192,2048]{1,0:T(8,128)(2,1)} %c_ref.7), custom_call_target="tpu_custom_call" | custom-call | bytes 16777216 | tf_op jit(solution)/shard_map/pallas_call | solution.py:40
  25.5 3.5 %shard_map.53.refs_10_.refs_3_.ca = bf16[2048,2048]{1,0:T(8,128)(2,1)S(1)} custom-call(bf16[8192,2048]{1,0:T(8,128)(2,1)} %c_ref.7), custom_call_target="tpu_custom_call" | custom-call | bytes 16777216 | tf_op jit(solution)/shard_map/pallas_call | solution.py:40
  29.1 2.4 %shard_map.55 = (bf16[128,8192]{1,0:T(8,128)(2,1)S(1)}, bf16[4,24,1024]{2,1,0:T(8,128)(2,1)S(1)}) custom-call(bf16[24,4096]{1,0:T(8,128)(2,1)S(1)} %get-tuple-element.34.refs_0_, bf16[24,4096]{1,0:T(8,128)(2,1)S(1)} %get-tuple-element.35.refs_1_, bf16[24,4096]{1,0:T(8,128)(2,1)S(1)} %collective-permute-done.refs_2_, ...), custom_call_target="tpu_custom_call" | custom-call | flops 2147483648 | bytes 262144 | tf_op jit(solution)/shard_map/pallas_call | solution.py:40
  31.5 2.3 %shard_map.56.mine_ref = f32[4,24,1024]{2,1,0:T(8,128)S(1)} custom-call(bf16[128,8192]{1,0:T(8,128)(2,1)S(1)} %get-tuple-element.36.refs_0_, bf16[2048,2048]{1,0:T(8,128)(2,1)S(1)} %shard_map.51.refs_8_.refs_1_.ca, bf16[2048,2048]{1,0:T(8,128)(2,1)S(1)} %shard_map.52.refs_9_.refs_2_.cb, bf16[2048,2048]{1,0:T(8,128)(2,1)S(1)} %shard_map.53.refs_10_.refs_3_.ca, ...), custom_call_target="tpu_custom_call" | custom-call | flops 2147483648 | bytes 262144 | tf_op jit(solution)/shard_map/pallas_call | solution.py:40
  34.0 1.6 %collective-permute-start.7 = (bf16[24,1024]{1,0:T(8,128)(2,1)S(1)}, bf16[24,1024]{1,0:T(8,128)(2,1)S(1)}, u32[]{:S(2)}, u32[]{:S(2)}) collective-permute-start(bf16[24,1024]{1,0:T(8,128)(2,1)S(1)} %get-tuple-element.39), channel_id=1, source_target_pairs={{0,2},{1,3},{2,0},{3,1},{4,6},{5,7},{6,4},{7,5},{8,10},{9,11},{10,... | collective-permute-start | bytes 147464 | tf_op jit(solution)/shard_map/ppermute | solution.py:36
  35.6 2.6 %collective-permute-start.8 = (bf16[24,1024]{1,0:T(8,128)(2,1)S(1)}, bf16[24,1024]{1,0:T(8,128)(2,1)S(1)}, u32[]{:S(2)}, u32[]{:S(2)}) collective-permute-start(bf16[24,1024]{1,0:T(8,128)(2,1)S(1)} %get-tuple-element.40), channel_id=1, source_target_pairs={{0,4},{1,5},{2,6},{3,7},{4,0},{5,1},{6,2},{7,3},{8,12},{9,13},{10,... | collective-permute-start | bytes 147464 | tf_op jit(solution)/shard_map/ppermute | solution.py:36
  39.6 2.1 %collective-permute-done.8.r2 = bf16[24,1024]{1,0:T(8,128)(2,1)S(1)} collective-permute-done((bf16[24,1024]{1,0:T(8,128)(2,1)S(1)}, bf16[24,1024]{1,0:T(8,128)(2,1)S(1)}, u32[]{:S(2)}, u32[]{:S(2)}) %collective-permute-start.8) | collective-permute-done | bytes 49184 | tf_op jit(solution)/shard_map/ppermute | solution.py:36
  41.7 2.3 %collective-permute-done.9.r3 = bf16[24,1024]{1,0:T(8,128)(2,1)S(1)} collective-permute-done((bf16[24,1024]{1,0:T(8,128)(2,1)S(1)}, bf16[24,1024]{1,0:T(8,128)(2,1)S(1)}, u32[]{:S(2)}, u32[]{:S(2)}) %collective-permute-start.9) | collective-permute-done | bytes 49184 | tf_op jit(solution)/shard_map/ppermute | solution.py:36
  45.6 3.0 %collective-permute-start.12 = (bf16[24,1024]{1,0:T(8,128)(2,1)S(1)}, bf16[24,1024]{1,0:T(8,128)(2,1)S(1)}, u32[]{:S(2)}, u32[]{:S(2)}) collective-permute-start(bf16[24,1024]{1,0:T(8,128)(2,1)S(1)} %get-tuple-element.45.refs_0_), channel_id=1, source_target_pairs={{0,2},{1,3},{2,0},{3,1},{4,6},{5,7},{6,4},{7,5},{8,10},{9,11},{10,... | collective-permute-start | bytes 147464 | tf_op jit(solution)/shard_map/ppermute | solution.py:36
  48.6 1.5 %collective-permute-done.14.refs_3_ = bf16[24,1024]{1,0:T(8,128)(2,1)S(1)} collective-permute-done((bf16[24,1024]{1,0:T(8,128)(2,1)S(1)}, bf16[24,1024]{1,0:T(8,128)(2,1)S(1)}, u32[]{:S(2)}, u32[]{:S(2)}) %collective-permute-start.14) | collective-permute-done | bytes 49184 | tf_op jit(solution)/shard_map/ppermute | solution.py:36
  51.3 1.5 %collective-permute-done.15.other_ref = bf16[4,32,1024]{2,1,0:T(8,128)(2,1)S(1)} collective-permute-done((bf16[4,32,1024]{2,1,0:T(8,128)(2,1)S(1)}, bf16[4,32,1024]{2,1,0:T(8,128)(2,1)S(1)}, u32[]{:S(2)}, u32[]{:S(2)}) %collective-permute-start.15) | collective-permute-done | bytes 262176 | tf_op jit(solution)/shard_map/ppermute | solution.py:36
  52.8 5.6 %shard_map.63 = (bf16[2,24,2048]{2,1,0:T(8,128)(2,1)S(1)}, bf16[2,24,2048]{2,1,0:T(8,128)(2,1)S(1)}, f32[24,2048]{1,0:T(8,128)S(1)}, f32[24,2048]{1,0:T(8,128)S(...) custom-call(bf16[4,32,1024]{2,1,0:T(8,128)(2,1)S(1)} %shard_map.60.mine_ref, ...), custom_call_target="tpu_custom_call" | custom-call | flops 2147483648 | bytes 262144 | tf_op jit(solution)/shard_map/pallas_call | solution.py:40
  59.0 1.5 %collective-permute-start.21 = (bf16[2,24,2048]{2,1,0:T(8,128)(2,1)S(1)}, bf16[2,24,2048]{2,1,0:T(8,128)(2,1)S(1)}, u32[]{:S(2)}, u32[]{:S(2)}) collective-permute-start(bf16[2,24,2048]{2,1,0:T(8,128)(2,1)S(1)} %get-tuple-element.57), channel_id=1, source_target_pairs={{0,16},{8,24},{16,0},{24,8},{1,17},{9,25},{17,1},{25,9},{2,18},{10... | collective-permute-start | bytes 589832 | tf_op jit(solution)/shard_map/ppermute | solution.py:36
  60.5 5.5 %shard_map.61 = (bf16[2,24,2048]{2,1,0:T(8,128)(2,1)S(1)}, bf16[2,24,2048]{2,1,0:T(8,128)(2,1)S(1)}, f32[24,2048]{1,0:T(8,128)S(1)}, f32[24,2048]{1,0:T(8,128)S(...) custom-call(bf16[4,32,1024]{2,1,0:T(8,128)(2,1)S(1)} %shard_map.60.mine_ref, ...), custom_call_target="tpu_custom_call" | custom-call | flops 2147483648 | bytes 262144 | tf_op jit(solution)/shard_map/pallas_call | solution.py:40
  68.8 1.5 %collective-permute-start.23 = (bf16[24,2048]{1,0:T(8,128)(2,1)S(1)}, bf16[24,2048]{1,0:T(8,128)(2,1)S(1)}, u32[]{:S(2)}, u32[]{:S(2)}) collective-permute-start(bf16[24,2048]{1,0:T(8,128)(2,1)S(1)} %get-tuple-element.65), channel_id=1, source_target_pairs={{0,16},{8,24},{16,0},{24,8},{1,17},{9,25},{17,1},{25,9},{2,18},{10... | collective-permute-start | bytes 294920 | tf_op jit(solution)/shard_map/ppermute | solution.py:36
  70.3 3.2 %collective-permute-done.16.rx = bf16[2,24,2048]{2,1,0:T(8,128)(2,1)S(1)} collective-permute-done((bf16[2,24,2048]{2,1,0:T(8,128)(2,1)S(1)}, bf16[2,24,2048]{2,1,0:T(8,128)(2,1)S(1)}, u32[]{:S(2)}, u32[]{:S(2)}) %collective-permute-start.16) | collective-permute-done | bytes 196640 | tf_op jit(solution)/shard_map/ppermute | solution.py:36
  73.9 1.5 %collective-permute-start.18 = (bf16[24,2048]{1,0:T(8,128)(2,1)S(1)}, bf16[24,2048]{1,0:T(8,128)(2,1)S(1)}, u32[]{:S(2)}, u32[]{:S(2)}) collective-permute-start(bf16[24,2048]{1,0:T(8,128)(2,1)S(1)} %get-tuple-element.54), channel_id=1, source_target_pairs={{0,8},{8,0},{16,24},{24,16},{1,9},{9,1},{17,25},{25,17},{2,10},{10... | collective-permute-start | bytes 294920 | tf_op jit(solution)/shard_map/ppermute | solution.py:36
  78.6 1.5 %collective-permute-done.19.refs_3_ = bf16[24,2048]{1,0:T(8,128)(2,1)S(1)} collective-permute-done((bf16[24,2048]{1,0:T(8,128)(2,1)S(1)}, bf16[24,2048]{1,0:T(8,128)(2,1)S(1)}, u32[]{:S(2)}, u32[]{:S(2)}) %collective-permute-start.19) | collective-permute-done | bytes 98336 | tf_op jit(solution)/shard_map/ppermute | solution.py:36
  (46 shorter events, 16.0 us)
Async XLA Ops:
  2.7 8.8 %collective-permute-start.2 = (bf16[24,4096]{1,0:T(8,128)(2,1)S(1)}, bf16[24,4096]{1,0:T(8,128)(2,1)S(1)}, u32[]{:S(2)}, u32[]{:S(2)}) collective-permute-start(bf16[24,4096]{1,0:T(8,128)(2,1)S(1)} %get-tuple-element.34.refs_0_), channel_id=1, source_target_pairs={{0,16},{8,24},{16,0},{24,8},{1,17},{9,25},{17,1},{25,9},{2,18},{10... | collective-permute-start | bytes 589832 | tf_op jit(solution)/shard_map/ppermute | solution.py:36
  5.7 7.8 %collective-permute-start.1 = (bf16[24,4096]{1,0:T(8,128)(2,1)S(1)}, bf16[24,4096]{1,0:T(8,128)(2,1)S(1)}, u32[]{:S(2)}, u32[]{:S(2)}) collective-permute-start(bf16[24,4096]{1,0:T(8,128)(2,1)S(1)} %get-tuple-element.35.refs_1_), channel_id=1, source_target_pairs={{0,8},{8,0},{16,24},{24,16},{1,9},{9,1},{17,25},{25,17},{2,10},{10... | collective-permute-start | bytes 589832 | tf_op jit(solution)/shard_map/ppermute | solution.py:36
  7.2 21.8 %collective-permute-start = (bf16[24,4096]{1,0:T(8,128)(2,1)S(1)}, bf16[24,4096]{1,0:T(8,128)(2,1)S(1)}, u32[]{:S(2)}, u32[]{:S(2)}) collective-permute-start(bf16[24,4096]{1,0:T(8,128)(2,1)S(1)} %get-tuple-element.34.refs_0_), channel_id=1, source_target_pairs={{0,8},{8,0},{16,24},{24,16},{1,9},{9,1},{17,25},{25,17},{2,10},{10... | collective-permute-start | bytes 589832 | tf_op jit(solution)/shard_map/ppermute | solution.py:36
  7.7 21.3 %collective-permute-start.3 = (bf16[24,4096]{1,0:T(8,128)(2,1)S(1)}, bf16[24,4096]{1,0:T(8,128)(2,1)S(1)}, u32[]{:S(2)}, u32[]{:S(2)}) collective-permute-start(bf16[24,4096]{1,0:T(8,128)(2,1)S(1)} %get-tuple-element.35.refs_1_), channel_id=1, source_target_pairs={{0,16},{8,24},{16,0},{24,8},{1,17},{9,25},{17,1},{25,9},{2,18},{10... | collective-permute-start | bytes 589832 | tf_op jit(solution)/shard_map/ppermute | solution.py:36
  11.4 17.6 %collective-permute-start.4 = (bf16[24,4096]{1,0:T(8,128)(2,1)S(1)}, bf16[24,4096]{1,0:T(8,128)(2,1)S(1)}, u32[]{:S(2)}, u32[]{:S(2)}) collective-permute-start(bf16[24,4096]{1,0:T(8,128)(2,1)S(1)} %collective-permute-done.2.refs_4_), channel_id=1, source_target_pairs={{0,8},{8,0},{16,24},{24,16},{1,9},{9,1},{17,25},{25,17},{2,10},{10... | collective-permute-start | bytes 589832 | tf_op jit(solution)/shard_map/ppermute | solution.py:36
  13.5 15.5 %collective-permute-start.5 = (bf16[24,4096]{1,0:T(8,128)(2,1)S(1)}, bf16[24,4096]{1,0:T(8,128)(2,1)S(1)}, u32[]{:S(2)}, u32[]{:S(2)}) collective-permute-start(bf16[24,4096]{1,0:T(8,128)(2,1)S(1)} %collective-permute-done.1.refs_3_), channel_id=1, source_target_pairs={{0,16},{8,24},{16,0},{24,8},{1,17},{9,25},{17,1},{25,9},{2,18},{10... | collective-permute-start | bytes 589832 | tf_op jit(solution)/shard_map/ppermute | solution.py:36
  31.4 2.4 %collective-permute-start.6 = (bf16[4,24,1024]{2,1,0:T(8,128)(2,1)S(1)}, bf16[4,24,1024]{2,1,0:T(8,128)(2,1)S(1)}, u32[]{:S(2)}, u32[]{:S(2)}) collective-permute-start(bf16[4,24,1024]{2,1,0:T(8,128)(2,1)S(1)} %get-tuple-element.37), channel_id=1, source_target_pairs={{0,1},{1,0},{2,3},{3,2},{4,5},{5,4},{6,7},{7,6},{8,9},{9,8},{10,11... | collective-permute-start | bytes 589832 | tf_op jit(solution)/shard_map/ppermute | solution.py:36
  34.0 5.7 %collective-permute-start.7 = (bf16[24,1024]{1,0:T(8,128)(2,1)S(1)}, bf16[24,1024]{1,0:T(8,128)(2,1)S(1)}, u32[]{:S(2)}, u32[]{:S(2)}) collective-permute-start(bf16[24,1024]{1,0:T(8,128)(2,1)S(1)} %get-tuple-element.39), channel_id=1, source_target_pairs={{0,2},{1,3},{2,0},{3,1},{4,6},{5,7},{6,4},{7,5},{8,10},{9,11},{10,... | collective-permute-start | bytes 147464 | tf_op jit(solution)/shard_map/ppermute | solution.py:36
  35.6 6.1 %collective-permute-start.8 = (bf16[24,1024]{1,0:T(8,128)(2,1)S(1)}, bf16[24,1024]{1,0:T(8,128)(2,1)S(1)}, u32[]{:S(2)}, u32[]{:S(2)}) collective-permute-start(bf16[24,1024]{1,0:T(8,128)(2,1)S(1)} %get-tuple-element.40), channel_id=1, source_target_pairs={{0,4},{1,5},{2,6},{3,7},{4,0},{5,1},{6,2},{7,3},{8,12},{9,13},{10,... | collective-permute-start | bytes 147464 | tf_op jit(solution)/shard_map/ppermute | solution.py:36
  38.2 5.9 %collective-permute-start.9 = (bf16[24,1024]{1,0:T(8,128)(2,1)S(1)}, bf16[24,1024]{1,0:T(8,128)(2,1)S(1)}, u32[]{:S(2)}, u32[]{:S(2)}) collective-permute-start(bf16[24,1024]{1,0:T(8,128)(2,1)S(1)} %get-tuple-element.41), channel_id=1, source_target_pairs={{0,6},{1,7},{2,4},{3,5},{4,2},{5,3},{6,0},{7,1},{8,14},{9,15},{10,... | collective-permute-start | bytes 147464 | tf_op jit(solution)/shard_map/ppermute | solution.py:36
  38.4 1.2 %collective-permute-start.10 = (bf16[12,1024]{1,0:T(8,128)(2,1)S(1)}, bf16[12,1024]{1,0:T(8,128)(2,1)S(1)}, u32[]{:S(2)}, u32[]{:S(2)}) collective-permute-start(bf16[12,1024]{1,0:T(8,128)(2,1)S(1)} %get-tuple-element.42), channel_id=1, source_target_pairs={{0,1},{1,0},{2,3},{3,2},{4,5},{5,4},{6,7},{7,6},{8,9},{9,8},{10,11... | collective-permute-start | bytes 73736 | tf_op jit(solution)/shard_map/ppermute | solution.py:36
  44.1 6.0 %collective-permute-start.14 = (bf16[24,1024]{1,0:T(8,128)(2,1)S(1)}, bf16[24,1024]{1,0:T(8,128)(2,1)S(1)}, u32[]{:S(2)}, u32[]{:S(2)}) collective-permute-start(bf16[24,1024]{1,0:T(8,128)(2,1)S(1)} %get-tuple-element.45.refs_0_), channel_id=1, source_target_pairs={{0,6},{1,7},{2,4},{3,5},{4,2},{5,3},{6,0},{7,1},{8,14},{9,15},{10,... | collective-permute-start | bytes 147464 | tf_op jit(solution)/shard_map/ppermute | solution.py:36
  45.6 5.6 %collective-permute-start.13 = (bf16[24,1024]{1,0:T(8,128)(2,1)S(1)}, bf16[24,1024]{1,0:T(8,128)(2,1)S(1)}, u32[]{:S(2)}, u32[]{:S(2)}) collective-permute-start(bf16[24,1024]{1,0:T(8,128)(2,1)S(1)} %get-tuple-element.45.refs_0_), channel_id=1, source_target_pairs={{0,4},{1,5},{2,6},{3,7},{4,0},{5,1},{6,2},{7,3},{8,12},{9,13},{10,... | collective-permute-start | bytes 147464 | tf_op jit(solution)/shard_map/ppermute | solution.py:36
  45.6 5.6 %collective-permute-start.12 = (bf16[24,1024]{1,0:T(8,128)(2,1)S(1)}, bf16[24,1024]{1,0:T(8,128)(2,1)S(1)}, u32[]{:S(2)}, u32[]{:S(2)}) collective-permute-start(bf16[24,1024]{1,0:T(8,128)(2,1)S(1)} %get-tuple-element.45.refs_0_), channel_id=1, source_target_pairs={{0,2},{1,3},{2,0},{3,1},{4,6},{5,7},{6,4},{7,5},{8,10},{9,11},{10,... | collective-permute-start | bytes 147464 | tf_op jit(solution)/shard_map/ppermute | solution.py:36
  51.2 1.6 %collective-permute-start.15 = (bf16[4,32,1024]{2,1,0:T(8,128)(2,1)S(1)}, bf16[4,32,1024]{2,1,0:T(8,128)(2,1)S(1)}, u32[]{:S(2)}, u32[]{:S(2)}) collective-permute-start(bf16[4,32,1024]{2,1,0:T(8,128)(2,1)S(1)} %shard_map.60.mine_ref), channel_id=1, source_target_pairs={{0,1},{1,0},{2,3},{3,2},{4,5},{5,4},{6,7},{7,6},{8,9},{9,8},{10,11... | collective-permute-start | bytes 786440 | tf_op jit(solution)/shard_map/ppermute | solution.py:36
  58.4 9.7 %collective-permute-start.20 = (bf16[2,24,2048]{2,1,0:T(8,128)(2,1)S(1)}, bf16[2,24,2048]{2,1,0:T(8,128)(2,1)S(1)}, u32[]{:S(2)}, u32[]{:S(2)}) collective-permute-start(bf16[2,24,2048]{2,1,0:T(8,128)(2,1)S(1)} %get-tuple-element.56), channel_id=1, source_target_pairs={{0,8},{8,0},{16,24},{24,16},{1,9},{9,1},{17,25},{25,17},{2,10},{10... | collective-permute-start | bytes 589832 | tf_op jit(solution)/shard_map/ppermute | solution.py:36
  59.0 9.1 %collective-permute-start.21 = (bf16[2,24,2048]{2,1,0:T(8,128)(2,1)S(1)}, bf16[2,24,2048]{2,1,0:T(8,128)(2,1)S(1)}, u32[]{:S(2)}, u32[]{:S(2)}) collective-permute-start(bf16[2,24,2048]{2,1,0:T(8,128)(2,1)S(1)} %get-tuple-element.57), channel_id=1, source_target_pairs={{0,16},{8,24},{16,0},{24,8},{1,17},{9,25},{17,1},{25,9},{2,18},{10... | collective-permute-start | bytes 589832 | tf_op jit(solution)/shard_map/ppermute | solution.py:36
  66.1 7.5 %collective-permute-start.16 = (bf16[2,24,2048]{2,1,0:T(8,128)(2,1)S(1)}, bf16[2,24,2048]{2,1,0:T(8,128)(2,1)S(1)}, u32[]{:S(2)}, u32[]{:S(2)}) collective-permute-start(bf16[2,24,2048]{2,1,0:T(8,128)(2,1)S(1)} %get-tuple-element.46), channel_id=1, source_target_pairs={{0,8},{8,0},{16,24},{24,16},{1,9},{9,1},{17,25},{25,17},{2,10},{10... | collective-permute-start | bytes 589832 | tf_op jit(solution)/shard_map/ppermute | solution.py:36
  66.7 7.2 %collective-permute-start.17 = (bf16[2,24,2048]{2,1,0:T(8,128)(2,1)S(1)}, bf16[2,24,2048]{2,1,0:T(8,128)(2,1)S(1)}, u32[]{:S(2)}, u32[]{:S(2)}) collective-permute-start(bf16[2,24,2048]{2,1,0:T(8,128)(2,1)S(1)} %get-tuple-element.47), channel_id=1, source_target_pairs={{0,16},{8,24},{16,0},{24,8},{1,17},{9,25},{17,1},{25,9},{2,18},{10... | collective-permute-start | bytes 589832 | tf_op jit(solution)/shard_map/ppermute | solution.py:36
  68.2 9.7 %collective-permute-start.22 = (bf16[24,2048]{1,0:T(8,128)(2,1)S(1)}, bf16[24,2048]{1,0:T(8,128)(2,1)S(1)}, u32[]{:S(2)}, u32[]{:S(2)}) collective-permute-start(bf16[24,2048]{1,0:T(8,128)(2,1)S(1)} %get-tuple-element.64), channel_id=1, source_target_pairs={{0,8},{8,0},{16,24},{24,16},{1,9},{9,1},{17,25},{25,17},{2,10},{10... | collective-permute-start | bytes 294920 | tf_op jit(solution)/shard_map/ppermute | solution.py:36
  68.8 9.1 %collective-permute-start.23 = (bf16[24,2048]{1,0:T(8,128)(2,1)S(1)}, bf16[24,2048]{1,0:T(8,128)(2,1)S(1)}, u32[]{:S(2)}, u32[]{:S(2)}) collective-permute-start(bf16[24,2048]{1,0:T(8,128)(2,1)S(1)} %get-tuple-element.65), channel_id=1, source_target_pairs={{0,16},{8,24},{16,0},{24,8},{1,17},{9,25},{17,1},{25,9},{2,18},{10... | collective-permute-start | bytes 294920 | tf_op jit(solution)/shard_map/ppermute | solution.py:36
  73.9 4.7 %collective-permute-start.18 = (bf16[24,2048]{1,0:T(8,128)(2,1)S(1)}, bf16[24,2048]{1,0:T(8,128)(2,1)S(1)}, u32[]{:S(2)}, u32[]{:S(2)}) collective-permute-start(bf16[24,2048]{1,0:T(8,128)(2,1)S(1)} %get-tuple-element.54), channel_id=1, source_target_pairs={{0,8},{8,0},{16,24},{24,16},{1,9},{9,1},{17,25},{25,17},{2,10},{10... | collective-permute-start | bytes 294920 | tf_op jit(solution)/shard_map/ppermute | solution.py:36
  75.4 4.6 %collective-permute-start.19 = (bf16[24,2048]{1,0:T(8,128)(2,1)S(1)}, bf16[24,2048]{1,0:T(8,128)(2,1)S(1)}, u32[]{:S(2)}, u32[]{:S(2)}) collective-permute-start(bf16[24,2048]{1,0:T(8,128)(2,1)S(1)} %get-tuple-element.55), channel_id=1, source_target_pairs={{0,16},{8,24},{16,0},{24,8},{1,17},{9,25},{17,1},{25,9},{2,18},{10... | collective-permute-start | bytes 294920 | tf_op jit(solution)/shard_map/ppermute | solution.py:36
  76.0 1.3 %collective-permute-start.11 = (f32[12,1024]{1,0:T(8,128)S(1)}, f32[12,1024]{1,0:T(8,128)S(1)}, u32[]{:S(2)}, u32[]{:S(2)}) collective-permute-start(f32[12,1024]{1,0:T(8,128)S(1)} %get-tuple-element.44), channel_id=1, source_target_pairs={{0,1},{1,0},{2,3},{3,2},{4,5},{5,4},{6,7},{7,6},{8,9},{9,8},{10,11... | collective-permute-start | bytes 147464 | tf_op jit(solution)/shard_map/ppermute | solution.py:36
  (3 other events, 14.4 us)

commit v2 on v1

v2 whole, which is shorter than its diff:
```python
import functools

import jax
import jax.numpy as jnp
from jax import lax
from jax.experimental import pallas as pl
from jax.experimental.pallas import tpu as pltpu
from jax.sharding import PartitionSpec as P

tau_root = 0.1
f32, bf16 = jnp.float32, jnp.bfloat16
VMEM = pl.BlockSpec(memory_space=pltpu.VMEM)
PAD = 32


def general(green_blocks, chol_slab, aux_fields):
    partial_value = jnp.dot(
        lax.all_gather(green_blocks, "blk", axis=0, tiled=True),
        chol_slab,
        preferred_element_type=f32,
    )
    bias_own = lax.psum_scatter(partial_value, "grp", scatter_dimension=0, tiled=True)
    field_own = (aux_fields.astype(f32) + tau_root * bias_own).astype(bf16)
    field_all = lax.all_gather(field_own, "grp", axis=0, tiled=True)
    summed = lax.psum_scatter(
        lax.dot_general(
            field_all, chol_slab, (((1,), (1,)), ((), ())), preferred_element_type=f32
        ),
        "blk",
        scatter_dimension=0,
        tiled=True,
    )
    return bias_own, summed.astype(bf16)


def swap(x, axis, bit):
    n = lax.axis_size(axis)
    return lax.ppermute(x, axis, [(i, i ^ bit) for i in range(n)])


def cross(x, turn):
    blks, grps = lax.axis_size("blk"), lax.axis_size("grp")
    pairs = [
        (b * grps + g, (b ^ (1 + (g + turn) % 2)) * grps + g) for b in range(blks) for g in range(grps)
    ]
    return lax.ppermute(x, ("blk", "grp"), pairs)


def call(body, outs, *args, mib=8, flops=0, ins=None, scratch=(), aliases=None):
    return pl.pallas_call(
        body,
        out_shape=outs,
        in_specs=ins or [VMEM] * len(args),
        out_specs=jax.tree.map(lambda _: VMEM, outs),
        scratch_shapes=scratch,
        input_output_aliases=aliases or {},
        compiler_params=pltpu.CompilerParams(vmem_limit_bytes=mib << 20),
        cost_estimate=pl.CostEstimate(flops=flops, bytes_accessed=1 << 18, transcendentals=0),
    )(*args)


def struct(shape, dtype):
    return jax.ShapeDtypeStruct(shape, dtype)


HBM = pl.BlockSpec(memory_space=pl.ANY)


def in_hbm(x):
    return pltpu.with_memory_space_constraint(x, pltpu.HBM)


def in_vmem(x):
    return pltpu.with_memory_space_constraint(x, pltpu.VMEM)


def run(copies):
    for c in copies:
        c.start()
    for c in copies:
        c.wait()


def piece_copies(c_ref, o_ref, sems, i, parts=2):
    rows = o_ref.shape[0]
    step = rows // parts
    return [
        pltpu.make_async_copy(
            c_ref.at[pl.ds(i * rows + p * step, step)],
            o_ref.at[pl.ds(p * step, step)],
            sems.at[p],
        )
        for p in range(parts)
    ]


def load_pieces(chol, first, count, piece, after):
    def body(c_ref, _, *refs):
        run([c for j in range(count) for c in piece_copies(c_ref, refs[j], refs[count].at[j], first + j)])

    return call(
        body,
        [piece] * count,
        in_hbm(chol),
        after,
        flops=count * 2 * 10**9,
        ins=[HBM, HBM],
        scratch=[pltpu.SemaphoreType.DMA((count, 2))],
    )


def transposed(piece, *after):
    rows, cols = piece.shape
    tile = min(512, rows, cols)

    def body(c, *refs):
        o = refs[-1]

        @pl.loop(0, rows // tile)
        def _(r):
            at = pl.ds(pl.multiple_of(r * tile, tile), tile)
            for j in range(cols // tile):
                o[j * tile : (j + 1) * tile, at] = c[at, j * tile : (j + 1) * tile].T

    return call(
        body, pltpu.VMEM((cols, rows), bf16), piece, *after, mib=8, ins=[VMEM] + [HBM] * len(after)
    )


def ids():
    blk, grp = lax.axis_index("blk"), lax.axis_index("grp")
    return blk, grp // 2, grp % 2


def role(p, core):
    return jnp.where(core == 0, p, (p >> 1) | ((p & 1) << 1))


def fast(green, chol, aux):
    wb, depth = green.shape
    width = chol.shape[1]
    wg = aux.shape[0]
    half = width // 2
    n_chunks = depth // width
    n_pieces, rows = 2 * n_chunks, width // 2
    piece = pltpu.VMEM((rows, width), bf16)

    near = cross(green, 0)

    def begin(c_ref, aux_ref, g_ref, c0_ref, c1_ref, kept_ref, sent_ref, own_ref, sems):
        _, _, core = ids()
        at = [pl.ds(pl.multiple_of(c * half, half), half) for c in (core, 1 - core)]
        run(
            [
                pltpu.make_async_copy(aux_ref.at[:, at[0]], kept_ref, sems.at[2, 0]),
                pltpu.make_async_copy(aux_ref.at[:, at[1]], sent_ref, sems.at[2, 1]),
                pltpu.make_async_copy(g_ref, own_ref, sems.at[3, 0]),
            ]
            + piece_copies(c_ref, c0_ref, sems.at[0], 0)
            + piece_copies(c_ref, c1_ref, sems.at[1], 1)
        )

    c0, c1, aux_kept, aux_sent, own = call(
        begin,
        (
            piece,
            piece,
            struct((wg, half), bf16),
            struct((wg, half), bf16),
            pltpu.VMEM((wb, depth), bf16),
        ),
        in_hbm(chol), in_hbm(aux), in_hbm(green),
        flops=4 * 10**9,
        ins=[HBM] * 3,
        scratch=[pltpu.SemaphoreType.DMA((4, 2))],
    )
    side, far = cross(own, 1), cross(near, 1)
    pieces = [c0, c1, *load_pieces(chol, 2, n_pieces - 4, piece, aux_kept)]
    aux_got = swap(aux_sent, "grp", 1)

    def bias_half(all_ref, c_refs, offset, start=0):
        total = None
        for k, c in enumerate(c_refs, start):
            term = jnp.dot(
                all_ref[:, k * rows : (k + 1) * rows],
                c[:, pl.ds(pl.multiple_of(offset, half), half)],
                preferred_element_type=f32,
            )
            total = term if total is None else total + term
        return total

    early = n_chunks
    here = n_pieces - 2

    def first(*refs):
        parts, c_refs, c_ref = refs[:4], refs[4 : 4 + here], refs[4 + here]
        all_ref, sent_ref, part_ref, *last_refs, sems, total_ref = refs[5 + here :]
        copies = [
            c for j, r in enumerate(last_refs) for c in piece_copies(c_ref, r, sems.at[j], here + j)
        ]
        for c in copies:
            c.start()
        blk, _, core = ids()

        @pl.when(core < 2)
        def _():
            for p in range(4):
                at = pl.ds(p * PAD, wb)
                all_ref[at, :] = parts[p][...]
                all_ref[pl.ds(p * PAD + wb, PAD - wb), :] = jnp.zeros((PAD - wb, depth), bf16)
            part_ref[...] = bias_half(all_ref, c_refs[:early], core * half)
            total_ref[...] = bias_half(all_ref, c_refs, (1 - core) * half)

        for c in copies:
            c.wait()
        total = total_ref[...] + bias_half(all_ref, last_refs, (1 - core) * half, here)
        for p in range(4):
            sent_ref[blk ^ role(p, core)] = total[p * PAD : p * PAD + wb].astype(bf16)

    flops1 = 2 * 128 * depth * half
    g_all, sent, part, *last = call(
        first,
        (
            struct((4 * PAD, depth), bf16),
            struct((4, wb, half), bf16),
            struct((4 * PAD, half), f32),
            piece,
            piece,
        ),
        own, near, side, far, *pieces, in_hbm(chol),
        flops=flops1,
        ins=[VMEM] * (4 + here) + [HBM],
        scratch=[pltpu.SemaphoreType.DMA((2, 2)), pltpu.VMEM((4 * PAD, half), f32)],
    )
    pieces += last
    other = swap(sent, "grp", 1)

    def second(all_ref, part_ref, *refs):
        c_refs, out_ref = refs[:-1], refs[-1]
        blk, _, core = ids()
        total = part_ref[...] + bias_half(all_ref, c_refs, core * half, early)
        for p in range(4):
            out_ref[blk ^ role(p, core)] = total[p * PAD : p * PAD + wb]

    mine = call(second, struct((4, wb, half), f32), g_all, part, *pieces[early:], flops=flops1)

    def combine(mine_ref, other_ref, keep_ref, *sent_refs):
        _, z, _ = ids()
        keep_ref[...] = mine_ref[z] + other_ref[z].astype(f32)
        for t, s in enumerate(sent_refs, 1):
            s[...] = (mine_ref[z ^ t] + other_ref[z ^ t].astype(f32)).astype(bf16)

    keep, *sums = call(
        combine, (struct((wb, half), f32),) + (struct((wb, half), bf16),) * 3, mine, other
    )
    sums = [swap(s, "grp", 2 * t) for t, s in enumerate(sums, 1)]
    turned = []
    for k in range(4):
        turned.append(
            transposed(pieces[k], turned[-1] if turned else sums[0], *pieces[k + 1 :])
        )

    def shift(keep_ref, r1, r2, r3, aux_ref, got_ref, _, bias_ref, give_ref, out_ref):
        _, _, core = ids()
        bias = keep_ref[...]
        for r in (r1, r2, r3):
            bias = bias + r[...].astype(f32)
        bias_ref[...] = bias
        give_ref[...] = jnp.where(core == 0, bias[wg:], bias[:wg])
        own = aux_ref[...].astype(f32)
        got = got_ref[...].astype(f32)
        top = jnp.where(core == 0, own, got)
        low = jnp.where(core == 0, got, own)
        out_ref[...] = (jnp.concatenate([top, low], 0) + tau_root * bias).astype(bf16)

    bias, give, shifted = call(
        shift,
        (struct((wb, half), f32), struct((wg, half), f32), struct((wb, half), bf16)),
        keep, *sums, aux_kept, aux_got, turned[-1],
        ins=[VMEM] * 6 + [HBM],
    )
    turned.append(transposed(pieces[4], shifted, *pieces[5:]))
    turned.append(transposed(pieces[5], turned[-1], *pieces[6:]))
    turned.append(transposed(pieces[6], turned[-1], *pieces[7:]))
    blocks = [shifted] + [swap(shifted, "grp", 2 * t) for t in (1, 2, 3)]
    bias_got = swap(give, "grp", 1)

    def arrange(*refs):
        ins, out_ref = refs[:4], refs[5]
        blk, z, _ = ids()
        for t in range(4):
            out_ref[z ^ t ^ blk, :wb] = ins[t][...]
            out_ref[t, wb:] = jnp.zeros((PAD - wb, half), bf16)

    s_mine = call(arrange, struct((4, PAD, half), bf16), *blocks, turned[-1], ins=[VMEM] * 4 + [HBM])
    s_other = swap(s_mine, "grp", 1)
    turned.append(transposed(pieces[7], s_mine))
    n_turned = len(turned)

    groups = [range(n_pieces - 2, n_pieces), range(n_pieces // 2, n_pieces - 2), range(n_pieces // 2)]

    def field(group, mine_ref, other_ref, *refs):
        c_refs, (s_ref, pass_ref, own_ref, all_ref) = refs[: len(group)], refs[-4:]
        _, _, core = ids()
        for ref, at in ((mine_ref, core), (other_ref, 1 - core)):
            cols = pl.ds(pl.multiple_of(at * half, half), half)
            for p in range(4):
                all_ref[p * PAD : (p + 1) * PAD, cols] = ref[role(p, core)]
        for j, (k, c) in enumerate(zip(group, c_refs)):
            if k < n_turned:
                total = jnp.dot(all_ref[...], c[...], preferred_element_type=f32)
            else:
                total = lax.dot_general(
                    c[...], all_ref[...], (((1,), (1,)), ((), ())), preferred_element_type=f32
                ).T
            block = [total[p * PAD : p * PAD + wb] for p in range(4)]
            at = pl.ds(j * rows, rows)
            own_ref[:, at] = block[0]
            pass_ref[:, at] = block[1]
            s_ref[0, :, at] = block[3].astype(bf16)
            s_ref[1, :, at] = block[2].astype(bf16)

    def forward(*refs):
        out_ref, new_ref = refs[-2:]
        start = 0
        for j in range(len(refs) // 3):
            got_ref, pass_ref, own_ref = refs[3 * j : 3 * j + 3]
            at = pl.ds(start, own_ref.shape[1])
            start += own_ref.shape[1]
            out_ref[:, at] = (pass_ref[...] + got_ref[0].astype(f32)).astype(bf16)
            new_ref[:, at] = own_ref[...] + got_ref[1].astype(f32)

    right = turned + pieces[n_turned:]
    stage = []
    for group in groups:
        n = len(group) * rows
        sent, passed, mine = call(
            functools.partial(field, group),
            (struct((2, wb, n), bf16), struct((wb, n), f32), struct((wb, n), f32)),
            s_mine, s_other, *right[group.start : group.stop], turned[-1],
            flops=4 * 128 * width * width,
            ins=[VMEM] * (2 + len(group)) + [HBM],
            scratch=[pltpu.VMEM((4 * PAD, width), bf16)],
        )
        stage.append((cross(sent, 1), passed, mine))
    done = []
    for part in (stage[1:][::-1], stage[:1]):
        n = sum(s[2].shape[1] for s in part)
        sent, mine = call(
            forward, (struct((wb, n), bf16), struct((wb, n), f32)), *[r for s in part for r in s]
        )
        done += [mine, cross(sent, 0)]

    def final(mine_ref, got_ref, last_ref, last_got_ref, out_ref):
        n = mine_ref.shape[1]
        out_ref[:, :n] = (mine_ref[...] + got_ref[...].astype(f32)).astype(bf16)
        out_ref[:, n:] = (last_ref[...] + last_got_ref[...].astype(f32)).astype(bf16)

    result = call(final, struct((wb, depth), bf16), *done)

    def own_bias(bias_ref, got_ref, out_ref):
        _, _, core = ids()
        b = bias_ref[...]
        out_ref[:, pl.ds(pl.multiple_of(core * half, half), half)] = jnp.where(
            core == 0, b[:wg], b[wg:]
        )
        out_ref[:, pl.ds(pl.multiple_of((1 - core) * half, half), half)] = got_ref[...]

    bias_own = call(own_bias, struct((wg, width), f32), bias, bias_got)
    return bias_own, result


def solution(mesh):
    blk, grp = mesh.shape["blk"], mesh.shape["grp"]

    def local(green, chol, aux):
        plane = blk == 4 and grp == 8
        fits = chol.shape[0] % (2 * chol.shape[1]) == 0 and green.shape[0] == 2 * aux.shape[0]
        return (fast if plane and fits and green.shape[0] <= PAD else general)(green, chol, aux)

    placed = (P("blk", "grp"), P("grp", "blk"), P("grp", "blk"))
    return jax.shard_map(
        local,
        mesh=mesh,
        in_specs=placed,
        out_specs=(P("grp", "blk"), P("blk", "grp")),
        check_vma=False,
    )
```

time: 81.1 us -> 75.1 us (0.926)
  waiting for transfers between devices: 20.4 us -> 10.2 us
  local copies, waits for them, and re-layouts: 1.83 us -> 7.32 us
  starting transfers between devices: 26 us -> 23.1 us
  Pallas kernels: 31.8 us -> 33.4 us
    ppermute x24 -> x10, waiting for transfers between devices: 20.4 us -> 1.91 us  [swap(): return lax.ppermute(x, axis, [(i, i ^ bit) for i in range(n)])]
    ppermute x24 -> x10, starting transfers between devices: 26 us -> 9.07 us  [swap(): return lax.ppermute(x, axis, [(i, i ^ bit) for i in range(n)])]
    ppermute x0 -> x8, starting transfers between devices: none -> 14 us  [cross(): return lax.ppermute(x, ('blk', 'grp'), pairs)]
    ppermute x0 -> x8, waiting for transfers between devices: none -> 8.33 us  [cross(): return lax.ppermute(x, ('blk', 'grp'), pairs)]
    unnamed x6 -> x16, local copies, waits for them, and re-layouts: 1.83 us -> 7.32 us
    pallas_call x16 -> x22, Pallas kernels: 31.8 us -> 33.4 us  [call(): pl.pallas_call(body, out_shape=outs, in_specs=ins or [VMEM] * len(args),...]
  transfers between devices with their start and end apart: 24 -> 18, of which waited for: 13 -> 9; matrix products, arithmetic and copies ran while one was open for 0% -> 0% of each run, Pallas kernels for 28% -> 33%
where the time goes in v2:
time: 75.1 us; the launch traced here: 75 us
  Pallas kernels  33.4 us (44%)
  starting transfers between devices  23.1 us (31%)
  waiting for transfers between devices  10.2 us (14%)
  local copies, waits for them, and re-layouts  7.32 us (10%)
  between operations  0.87 us (1%)
    pallas_call x22, Pallas kernels, call(): pl.pallas_call(body, out_shape=outs, in_specs=ins or [VMEM] * len(args),...  33.4 us
    ppermute x8, starting transfers between devices, cross(): return lax.ppermute(x, ('blk', 'grp'), pairs)  14 us
    ppermute x10, starting transfers between devices, swap(): return lax.ppermute(x, axis, [(i, i ^ bit) for i in range(n)])  9.07 us
    ppermute x8, waiting for transfers between devices, cross(): return lax.ppermute(x, ('blk', 'grp'), pairs)  8.33 us
    unnamed x16, local copies, waits for them, and re-layouts  7.32 us
    ppermute x10, waiting for transfers between devices, swap(): return lax.ppermute(x, axis, [(i, i ^ bit) for i in range(n)])  1.91 us
  transfers between devices with their start and end apart: 18, of which 9 were waited for; matrix products, arithmetic and copies ran while one was open for 0% of the time, Pallas kernels for 33%

profile of v2, /device:TPU:0, one launch (start us, length us, event | category | flops | bytes accessed | tf_op | source)
XLA Modules:
  0.0 75.0 jit_solution(1699539203182479744)
XLA Ops:
  0.6 3.0 %collective-permute-start = (bf16[24,8192]{1,0:T(8,128)(2,1)}, bf16[24,8192]{1,0:T(8,128)(2,1)S(1)}, u32[]{:S(2)}, u32[]{:S(2)}) collective-permute-start(bf16[24,8192]{1,0:T(8,128)(2,1)} %g_ref.1), channel_id=1, source_target_pairs={{0,8},{1,17},{2,10},{3,19},{4,12},{5,21},{6,14},{7,23},{8,0},{9,25... | collective-permute-start | bytes 1179656 | tf_op jit(solution)/shard_map/ppermute | solution.py:46
  3.6 3.7 %shard_map.50 = (bf16[1024,2048]{1,0:T(8,128)(2,1)S(1)}, bf16[1024,2048]{1,0:T(8,128)(2,1)S(1)}, bf16[12,1024]{1,0:T(8,128)(2,1)S(1)}, bf16[12,1024]{1,0:T(8,128)(2,1)S(1)}, bf16[24,8192]{1,0:T(8,128)(2,1)S(1)}) custom-call(bf16[8192,2048]{1,0:T(8,128)(2,1)} %refs_10_.1, bf16[12,2048]{1,0:T(8,128)(2,1)} %aux_ref.1, bf16[24,8192]{1,0:T(8,128)(2,1)} %g_ref.1), custom_call_target="tpu_custom_call" | custom-call | flops 4000000000 | bytes 262144 | tf_op jit(solution)/shard_map/pallas_call | solution.py:50
  7.3 1.6 %collective-permute-start.1 = (bf16[24,8192]{1,0:T(8,128)(2,1)S(1)}, bf16[24,8192]{1,0:T(8,128)(2,1)S(1)}, u32[]{:S(2)}, u32[]{:S(2)}) collective-permute-start(bf16[24,8192]{1,0:T(8,128)(2,1)S(1)} %get-tuple-element.36.refs_0_), channel_id=1, source_target_pairs={{0,16},{1,9},{2,18},{3,11},{4,20},{5,13},{6,22},{7,15},{8,24},{9,1... | collective-permute-start | bytes 1179656 | tf_op jit(solution)/shard_map/ppermute | solution.py:46
  9.7 3.6 %collective-permute-start.2 = (bf16[24,8192]{1,0:T(8,128)(2,1)S(1)}, bf16[24,8192]{1,0:T(8,128)(2,1)S(1)}, u32[]{:S(2)}, u32[]{:S(2)}) collective-permute-start(bf16[24,8192]{1,0:T(8,128)(2,1)S(1)} %collective-permute-done.refs_1_), channel_id=1, source_target_pairs={{0,16},{1,9},{2,18},{3,11},{4,20},{5,13},{6,22},{7,15},{8,24},{9,1... | collective-permute-start | bytes 1179656 | tf_op jit(solution)/shard_map/ppermute | solution.py:46
  13.3 5.9 %shard_map.51 = (bf16[1024,2048]{1,0:T(8,128)(2,1)S(1)}, bf16[1024,2048]{1,0:T(8,128)(2,1)S(1)}, bf16[1024,2048]{1,0:T(8,128)(2,1)S(1)}, bf16[1024,2048]{1,0:T(8,128)(2,1)S(1)}) custom-call(bf16[8192,2048]{1,0:T(8,128)(2,1)} %refs_10_.1, bf16[12,1024]{1,0:T(8,128)(2,1)S(1)} %get-tuple-element.39._.aux_ref), custom_call_target="tpu_custom_call" | custom-call | flops 8000000000 | bytes 262144 | tf_op jit(solution)/shard_map/pallas_call | solution.py:50
  19.4 5.6 %shard_map.52 = (bf16[128,8192]{1,0:T(8,128)(2,1)S(1)}, bf16[4,24,1024]{2,1,0:T(8,128)(2,1)S(1)}, f32[128,1024]{1,0:T(8,128)S(1)}, bf16[1024,2048]{1,0:T(8,128)(2,1)S(1)}, bf16[1024,2048]{1,0:T(8,128)(2,1)S(1)}) custom-call(bf16[24,8192]{1,0:T(8,128)(2,1)S(1)} %get-tuple-element.36.refs_0_, bf16[24,8192]{1,0:T(8,128)(2,1)S(1)} %collective-permute-done.refs_1_, ...), custom_call_target="tpu_custom_call" | custom-call | flops 2147483648 | bytes 262144 | tf_op jit(solution)/shard_map/pallas_call | solution.py:50
  25.1 1.3 %shard_map.53.mine_ref = f32[4,24,1024]{2,1,0:T(8,128)S(1)} custom-call(bf16[128,8192]{1,0:T(8,128)(2,1)S(1)} %get-tuple-element.44.all_ref, f32[128,1024]{1,0:T(8,128)S(1)} %get-tuple-element.45.part_ref, bf16[1024,2048]{1,0:T(8,128)(2,1)S(1)} %get-tuple-element.42.refs_8_.refs_0_.refs_4_.refs_3_.refs_2_.refs_1_.c, ...), custom_call_target="tpu_custom_call" | custom-call | flops 2147483648 | bytes 262144 | tf_op jit(solution)/shard_map/pallas_call | solution.py:50
  26.6 1.4 %collective-permute-start.4 = (bf16[24,1024]{1,0:T(8,128)(2,1)S(1)}, bf16[24,1024]{1,0:T(8,128)(2,1)S(1)}, u32[]{:S(2)}, u32[]{:S(2)}) collective-permute-start(bf16[24,1024]{1,0:T(8,128)(2,1)S(1)} %get-tuple-element.50), channel_id=1, source_target_pairs={{0,2},{1,3},{2,0},{3,1},{4,6},{5,7},{6,4},{7,5},{8,10},{9,11},{10,... | collective-permute-start | bytes 147464 | tf_op jit(solution)/shard_map/ppermute | solution.py:38
  28.0 2.6 %collective-permute-start.5 = (bf16[24,1024]{1,0:T(8,128)(2,1)S(1)}, bf16[24,1024]{1,0:T(8,128)(2,1)S(1)}, u32[]{:S(2)}, u32[]{:S(2)}) collective-permute-start(bf16[24,1024]{1,0:T(8,128)(2,1)S(1)} %get-tuple-element.51), channel_id=1, source_target_pairs={{0,4},{1,5},{2,6},{3,7},{4,0},{5,1},{6,2},{7,3},{8,12},{9,13},{10,... | collective-permute-start | bytes 147464 | tf_op jit(solution)/shard_map/ppermute | solution.py:38
  31.1 1.3 %shard_map.55.refs_0_ = bf16[2048,1024]{1,0:T(8,128)(2,1)S(1)} custom-call(bf16[1024,2048]{1,0:T(8,128)(2,1)S(1)} %get-tuple-element.37.refs_4_.c, bf16[24,1024]{1,0:T(8,128)(2,1)S(1)} %collective-permute-done.4.refs_0_.r1, bf16[1024,2048]{1,0:T(8,128)(2,1)S(1)} %get-tuple-element.38.refs_5_.refs_1_.c, ...), custom_call_target="tpu_custom_call" | custom-call | bytes 262144 | tf_op jit(solution)/shard_map/pallas_call | solution.py:50
  32.4 1.3 %shard_map.56.refs_0_.refs_1_ = bf16[2048,1024]{1,0:T(8,128)(2,1)S(1)} custom-call(bf16[1024,2048]{1,0:T(8,128)(2,1)S(1)} %get-tuple-element.38.refs_5_.refs_1_.c, bf16[2048,1024]{1,0:T(8,128)(2,1)S(1)} %shard_map.55.refs_0_, bf16[1024,2048]{1,0:T(8,128)(2,1)S(1)} %get-tuple-element.40.refs_6_.refs_2_.refs_1_.c, ...), custom_call_target="tpu_custom_call" | custom-call | bytes 262144 | tf_op jit(solution)/shard_map/pallas_call | solution.py:50
  36.3 2.2 %copy-done.1 = bf16[1024,2048]{1,0:T(8,128)(2,1)S(1)} copy-done((bf16[1024,2048]{1,0:T(8,128)(2,1)S(1)}, bf16[1024,2048]{1,0:T(8,128)(2,1)}, u32[]{:S(2)}) %copy-start.1) | copy-done | bytes 4194328
  40.6 3.4 %collective-permute-start.11 = (bf16[24,1024]{1,0:T(8,128)(2,1)S(1)}, bf16[24,1024]{1,0:T(8,128)(2,1)S(1)}, u32[]{:S(2)}, u32[]{:S(2)}) collective-permute-start(bf16[24,1024]{1,0:T(8,128)(2,1)S(1)} %get-tuple-element.56.refs_0_), channel_id=1, source_target_pairs={{0,6},{1,7},{2,4},{3,5},{4,2},{5,3},{6,0},{7,1},{8,14},{9,15},{10,... | collective-permute-start | bytes 147464 | tf_op jit(solution)/shard_map/ppermute | solution.py:38
  46.3 1.3 %shard_map.62.refs_0_.refs_1_ = bf16[2048,1024]{1,0:T(8,128)(2,1)S(1)} custom-call(bf16[1024,2048]{1,0:T(8,128)(2,1)S(1)} %get-tuple-element.43.refs_9_.refs_1_.refs_5_.refs_4_.refs_3_.refs_2_.c, bf16[2048,1024]{1,0:T(8,128)(2,1)S(1)} %shard_map.61.refs_0_, bf16[1024,2048]{1,0:T(8,128)(2,1)S(1)} %get-tuple-element.46.refs_2_.refs_6_.refs_5_.refs_4_.refs_3_.refs_1_.c, ...), custom_call_target="tpu_custom_call" | custom-call | bytes 262144 | tf_op jit(solution)/shard_map/pallas_call | solution.py:50
  47.6 1.3 %shard_map.63.refs_4_.refs_0_ = bf16[2048,1024]{1,0:T(8,128)(2,1)S(1)} custom-call(bf16[1024,2048]{1,0:T(8,128)(2,1)S(1)} %get-tuple-element.46.refs_2_.refs_6_.refs_5_.refs_4_.refs_3_.refs_1_.c, bf16[2048,1024]{1,0:T(8,128)(2,1)S(1)} %shard_map.62.refs_0_.refs_1_, ...), custom_call_target="tpu_custom_call" | custom-call | bytes 262144 | tf_op jit(solution)/shard_map/pallas_call | solution.py:50
  49.4 1.3 %shard_map.65.refs_4_.refs_2_.refs_1_ = bf16[2048,1024]{1,0:T(8,128)(2,1)S(1)} custom-call(bf16[1024,2048]{1,0:T(8,128)(2,1)S(1)} %get-tuple-element.47.refs_3_.refs_7_.refs_6_.refs_5_.refs_4_.refs_2_.refs_1_.c, bf16[4,32,1024]{2,1,0:T(8,128)(2,1)S(1)} %shard_map.64.refs_0_.mine_ref), custom_call_target="tpu_custom_call" | custom-call | bytes 262144 | tf_op jit(solution)/shard_map/pallas_call | solution.py:50
  51.4 1.3 %copy-done.3 = bf16[2048,1024]{1,0:T(8,128)(2,1)S(1)} copy-done((bf16[2048,1024]{1,0:T(8,128)(2,1)S(1)}, bf16[2048,1024]{1,0:T(8,128)(2,1)}, u32[]{:S(2)}) %copy-start.3) | copy-done | bytes 4194328
  53.9 2.4 %shard_map.66 = (bf16[2,24,4096]{2,1,0:T(8,128)(2,1)S(1)}, f32[24,4096]{1,0:T(8,128)S(1)}, f32[24,4096]{1,0:T(8,128)S(1)}) custom-call(bf16[4,32,1024]{2,1,0:T(8,128)(2,1)S(1)} %shard_map.64.refs_0_.mine_ref, bf16[4,32,1024]{2,1,0:T(8,128)(2,1)S(1)} %collective-permute-done.12.other_ref, bf16[2048,1024]{1,0:T(8,128)(2,1)S(1)} %copy-done.3, ...), custom_call_target="tpu_custom_call" | custom-call | flops 2147483648 | bytes 262144 | tf_op jit(solution)/shard_map/pallas_call | solution.py:50
  58.0 1.7 %collective-permute-start.14 = (bf16[2,24,2048]{2,1,0:T(8,128)(2,1)S(1)}, bf16[2,24,2048]{2,1,0:T(8,128)(2,1)S(1)}, u32[]{:S(2)}, u32[]{:S(2)}) collective-permute-start(bf16[2,24,2048]{2,1,0:T(8,128)(2,1)S(1)} %get-tuple-element.60), channel_id=1, source_target_pairs={{0,16},{1,9},{2,18},{3,11},{4,20},{5,13},{6,22},{7,15},{8,24},{9,1... | collective-permute-start | bytes 589832 | tf_op jit(solution)/shard_map/ppermute | solution.py:46
  59.7 1.3 %shard_map.69 = (bf16[2,24,2048]{2,1,0:T(8,128)(2,1)S(1)}, f32[24,2048]{1,0:T(8,128)S(1)}, f32[24,2048]{1,0:T(8,128)S(1)}) custom-call(bf16[4,32,1024]{2,1,0:T(8,128)(2,1)S(1)} %shard_map.64.refs_0_.mine_ref, bf16[4,32,1024]{2,1,0:T(8,128)(2,1)S(1)} %collective-permute-done.12.other_ref, bf16[2048,1024]{1,0:T(8,128)(2,1)S(1)} %shard_map.63.refs_4_.refs_0_, ...), custom_call_target="tpu_custom_call" | custom-call | flops 2147483648 | bytes 262144 | tf_op jit(solution)/shard_map/pallas_call | solution.py:50
  61.4 4.8 %collective-permute-done.14.refs_3_ = bf16[2,24,2048]{2,1,0:T(8,128)(2,1)S(1)} collective-permute-done((bf16[2,24,2048]{2,1,0:T(8,128)(2,1)S(1)}, bf16[2,24,2048]{2,1,0:T(8,128)(2,1)S(1)}, u32[]{:S(2)}, u32[]{:S(2)}) %collective-permute-start.14) | collective-permute-done | bytes 196640 | tf_op jit(solution)/shard_map/ppermute | solution.py:46
  66.3 1.6 %collective-permute-start.15 = (bf16[24,6144]{1,0:T(8,128)(2,1)S(1)}, bf16[24,6144]{1,0:T(8,128)(2,1)S(1)}, u32[]{:S(2)}, u32[]{:S(2)}) collective-permute-start(bf16[24,6144]{1,0:T(8,128)(2,1)S(1)} %get-tuple-element.64), channel_id=1, source_target_pairs={{0,8},{1,17},{2,10},{3,19},{4,12},{5,21},{6,14},{7,23},{8,0},{9,25... | collective-permute-start | bytes 884744 | tf_op jit(solution)/shard_map/ppermute | solution.py:46
  68.7 1.7 %collective-permute-start.17 = (bf16[24,2048]{1,0:T(8,128)(2,1)S(1)}, bf16[24,2048]{1,0:T(8,128)(2,1)S(1)}, u32[]{:S(2)}, u32[]{:S(2)}) collective-permute-start(bf16[24,2048]{1,0:T(8,128)(2,1)S(1)} %get-tuple-element.69), channel_id=1, source_target_pairs={{0,8},{1,17},{2,10},{3,19},{4,12},{5,21},{6,14},{7,23},{8,0},{9,25... | collective-permute-start | bytes 294920 | tf_op jit(solution)/shard_map/ppermute | solution.py:46
  72.3 1.9 %collective-permute-done.17.last_got_ref = bf16[24,2048]{1,0:T(8,128)(2,1)S(1)} collective-permute-done((bf16[24,2048]{1,0:T(8,128)(2,1)S(1)}, bf16[24,2048]{1,0:T(8,128)(2,1)S(1)}, u32[]{:S(2)}, u32[]{:S(2)}) %collective-permute-start.17) | collective-permute-done | bytes 98336 | tf_op jit(solution)/shard_map/ppermute | solution.py:46
  (50 shorter events, 16.7 us)
Async XLA Ops:
  0.6 9.1 %collective-permute-start = (bf16[24,8192]{1,0:T(8,128)(2,1)}, bf16[24,8192]{1,0:T(8,128)(2,1)S(1)}, u32[]{:S(2)}, u32[]{:S(2)}) collective-permute-start(bf16[24,8192]{1,0:T(8,128)(2,1)} %g_ref.1), channel_id=1, source_target_pairs={{0,8},{1,17},{2,10},{3,19},{4,12},{5,21},{6,14},{7,23},{8,0},{9,25... | collective-permute-start | bytes 1179656 | tf_op jit(solution)/shard_map/ppermute | solution.py:46
  7.3 11.9 %collective-permute-start.1 = (bf16[24,8192]{1,0:T(8,128)(2,1)S(1)}, bf16[24,8192]{1,0:T(8,128)(2,1)S(1)}, u32[]{:S(2)}, u32[]{:S(2)}) collective-permute-start(bf16[24,8192]{1,0:T(8,128)(2,1)S(1)} %get-tuple-element.36.refs_0_), channel_id=1, source_target_pairs={{0,16},{1,9},{2,18},{3,11},{4,20},{5,13},{6,22},{7,15},{8,24},{9,1... | collective-permute-start | bytes 1179656 | tf_op jit(solution)/shard_map/ppermute | solution.py:46
  9.7 9.7 %collective-permute-start.2 = (bf16[24,8192]{1,0:T(8,128)(2,1)S(1)}, bf16[24,8192]{1,0:T(8,128)(2,1)S(1)}, u32[]{:S(2)}, u32[]{:S(2)}) collective-permute-start(bf16[24,8192]{1,0:T(8,128)(2,1)S(1)} %collective-permute-done.refs_1_), channel_id=1, source_target_pairs={{0,16},{1,9},{2,18},{3,11},{4,20},{5,13},{6,22},{7,15},{8,24},{9,1... | collective-permute-start | bytes 1179656 | tf_op jit(solution)/shard_map/ppermute | solution.py:46
  19.3 14.4 %copy-start = (bf16[1024,2048]{1,0:T(8,128)(2,1)}, bf16[1024,2048]{1,0:T(8,128)(2,1)S(1)}, u32[]{:S(2)}) copy-start(bf16[1024,2048]{1,0:T(8,128)(2,1)S(1)} %get-tuple-element.41.refs_7_.refs_3_.refs_2_.refs_1_.c) | copy-start | bytes 12582916
  25.0 1.5 %collective-permute-start.3 = (bf16[4,24,1024]{2,1,0:T(8,128)(2,1)S(1)}, bf16[4,24,1024]{2,1,0:T(8,128)(2,1)S(1)}, u32[]{:S(2)}, u32[]{:S(2)}) collective-permute-start(bf16[4,24,1024]{2,1,0:T(8,128)(2,1)S(1)} %get-tuple-element.48), channel_id=1, source_target_pairs={{0,1},{1,0},{2,3},{3,2},{4,5},{5,4},{6,7},{7,6},{8,9},{9,8},{10,11... | collective-permute-start | bytes 589832 | tf_op jit(solution)/shard_map/ppermute | solution.py:38
  26.6 4.5 %collective-permute-start.4 = (bf16[24,1024]{1,0:T(8,128)(2,1)S(1)}, bf16[24,1024]{1,0:T(8,128)(2,1)S(1)}, u32[]{:S(2)}, u32[]{:S(2)}) collective-permute-start(bf16[24,1024]{1,0:T(8,128)(2,1)S(1)} %get-tuple-element.50), channel_id=1, source_target_pairs={{0,2},{1,3},{2,0},{3,1},{4,6},{5,7},{6,4},{7,5},{8,10},{9,11},{10,... | collective-permute-start | bytes 147464 | tf_op jit(solution)/shard_map/ppermute | solution.py:38
  28.0 12.5 %collective-permute-start.5 = (bf16[24,1024]{1,0:T(8,128)(2,1)S(1)}, bf16[24,1024]{1,0:T(8,128)(2,1)S(1)}, u32[]{:S(2)}, u32[]{:S(2)}) collective-permute-start(bf16[24,1024]{1,0:T(8,128)(2,1)S(1)} %get-tuple-element.51), channel_id=1, source_target_pairs={{0,4},{1,5},{2,6},{3,7},{4,0},{5,1},{6,2},{7,3},{8,12},{9,13},{10,... | collective-permute-start | bytes 147464 | tf_op jit(solution)/shard_map/ppermute | solution.py:38
  30.6 9.9 %collective-permute-start.6 = (bf16[24,1024]{1,0:T(8,128)(2,1)S(1)}, bf16[24,1024]{1,0:T(8,128)(2,1)S(1)}, u32[]{:S(2)}, u32[]{:S(2)}) collective-permute-start(bf16[24,1024]{1,0:T(8,128)(2,1)S(1)} %get-tuple-element.52), channel_id=1, source_target_pairs={{0,6},{1,7},{2,4},{3,5},{4,2},{5,3},{6,0},{7,1},{8,14},{9,15},{10,... | collective-permute-start | bytes 147464 | tf_op jit(solution)/shard_map/ppermute | solution.py:38
  31.1 9.5 %collective-permute-start.7 = (bf16[12,1024]{1,0:T(8,128)(2,1)S(1)}, bf16[12,1024]{1,0:T(8,128)(2,1)S(1)}, u32[]{:S(2)}, u32[]{:S(2)}) collective-permute-start(bf16[12,1024]{1,0:T(8,128)(2,1)S(1)} %get-tuple-element.53), channel_id=1, source_target_pairs={{0,1},{1,0},{2,3},{3,2},{4,5},{5,4},{6,7},{7,6},{8,9},{9,8},{10,11... | collective-permute-start | bytes 73736 | tf_op jit(solution)/shard_map/ppermute | solution.py:38
  34.3 2.0 %copy-start.4 = (bf16[2048,1024]{1,0:T(8,128)(2,1)}, bf16[2048,1024]{1,0:T(8,128)(2,1)S(1)}, u32[]{:S(2)}) copy-start(bf16[2048,1024]{1,0:T(8,128)(2,1)S(1)} %shard_map.56.refs_0_.refs_1_) | copy-start | bytes 12582916
  36.3 2.2 %copy-start.1 = (bf16[1024,2048]{1,0:T(8,128)(2,1)S(1)}, bf16[1024,2048]{1,0:T(8,128)(2,1)}, u32[]{:S(2)}) copy-start(bf16[1024,2048]{1,0:T(8,128)(2,1)} %copy-done) | copy-start | bytes 12582916
  40.6 8.3 %collective-permute-start.11 = (bf16[24,1024]{1,0:T(8,128)(2,1)S(1)}, bf16[24,1024]{1,0:T(8,128)(2,1)S(1)}, u32[]{:S(2)}, u32[]{:S(2)}) collective-permute-start(bf16[24,1024]{1,0:T(8,128)(2,1)S(1)} %get-tuple-element.56.refs_0_), channel_id=1, source_target_pairs={{0,6},{1,7},{2,4},{3,5},{4,2},{5,3},{6,0},{7,1},{8,14},{9,15},{10,... | collective-permute-start | bytes 147464 | tf_op jit(solution)/shard_map/ppermute | solution.py:38
  44.0 5.2 %collective-permute-start.10 = (bf16[24,1024]{1,0:T(8,128)(2,1)S(1)}, bf16[24,1024]{1,0:T(8,128)(2,1)S(1)}, u32[]{:S(2)}, u32[]{:S(2)}) collective-permute-start(bf16[24,1024]{1,0:T(8,128)(2,1)S(1)} %get-tuple-element.56.refs_0_), channel_id=1, source_target_pairs={{0,4},{1,5},{2,6},{3,7},{4,0},{5,1},{6,2},{7,3},{8,12},{9,13},{10,... | collective-permute-start | bytes 147464 | tf_op jit(solution)/shard_map/ppermute | solution.py:38
  44.0 5.2 %collective-permute-start.9 = (bf16[24,1024]{1,0:T(8,128)(2,1)S(1)}, bf16[24,1024]{1,0:T(8,128)(2,1)S(1)}, u32[]{:S(2)}, u32[]{:S(2)}) collective-permute-start(bf16[24,1024]{1,0:T(8,128)(2,1)S(1)} %get-tuple-element.56.refs_0_), channel_id=1, source_target_pairs={{0,2},{1,3},{2,0},{3,1},{4,6},{5,7},{6,4},{7,5},{8,10},{9,11},{10,... | collective-permute-start | bytes 147464 | tf_op jit(solution)/shard_map/ppermute | solution.py:38
  49.2 2.2 %copy-start.7 = (bf16[2048,1024]{1,0:T(8,128)(2,1)S(1)}, bf16[2048,1024]{1,0:T(8,128)(2,1)}, u32[]{:S(2)}) copy-start(bf16[2048,1024]{1,0:T(8,128)(2,1)} %copy-done.6) | copy-start | bytes 12582916
  49.3 3.4 %copy-start.3 = (bf16[2048,1024]{1,0:T(8,128)(2,1)S(1)}, bf16[2048,1024]{1,0:T(8,128)(2,1)}, u32[]{:S(2)}) copy-start(bf16[2048,1024]{1,0:T(8,128)(2,1)} %copy-done.2) | copy-start | bytes 12582916
  49.3 4.6 %copy-start.5 = (bf16[2048,1024]{1,0:T(8,128)(2,1)S(1)}, bf16[2048,1024]{1,0:T(8,128)(2,1)}, u32[]{:S(2)}) copy-start(bf16[2048,1024]{1,0:T(8,128)(2,1)} %copy-done.4) | copy-start | bytes 12582916
  49.3 1.6 %collective-permute-start.12 = (bf16[4,32,1024]{2,1,0:T(8,128)(2,1)S(1)}, bf16[4,32,1024]{2,1,0:T(8,128)(2,1)S(1)}, u32[]{:S(2)}, u32[]{:S(2)}) collective-permute-start(bf16[4,32,1024]{2,1,0:T(8,128)(2,1)S(1)} %shard_map.64.refs_0_.mine_ref), channel_id=1, source_target_pairs={{0,1},{1,0},{2,3},{3,2},{4,5},{5,4},{6,7},{7,6},{8,9},{9,8},{10,11... | collective-permute-start | bytes 786440 | tf_op jit(solution)/shard_map/ppermute | solution.py:38
  56.3 10.0 %collective-permute-start.13 = (bf16[2,24,4096]{2,1,0:T(8,128)(2,1)S(1)}, bf16[2,24,4096]{2,1,0:T(8,128)(2,1)S(1)}, u32[]{:S(2)}, u32[]{:S(2)}) collective-permute-start(bf16[2,24,4096]{2,1,0:T(8,128)(2,1)S(1)} %get-tuple-element.57), channel_id=1, source_target_pairs={{0,16},{1,9},{2,18},{3,11},{4,20},{5,13},{6,22},{7,15},{8,24},{9,1... | collective-permute-start | bytes 1179656 | tf_op jit(solution)/shard_map/ppermute | solution.py:46
  58.0 8.3 %collective-permute-start.14 = (bf16[2,24,2048]{2,1,0:T(8,128)(2,1)S(1)}, bf16[2,24,2048]{2,1,0:T(8,128)(2,1)S(1)}, u32[]{:S(2)}, u32[]{:S(2)}) collective-permute-start(bf16[2,24,2048]{2,1,0:T(8,128)(2,1)S(1)} %get-tuple-element.60), channel_id=1, source_target_pairs={{0,16},{1,9},{2,18},{3,11},{4,20},{5,13},{6,22},{7,15},{8,24},{9,1... | collective-permute-start | bytes 589832 | tf_op jit(solution)/shard_map/ppermute | solution.py:46
  61.0 7.7 %collective-permute-start.16 = (bf16[2,24,2048]{2,1,0:T(8,128)(2,1)S(1)}, bf16[2,24,2048]{2,1,0:T(8,128)(2,1)S(1)}, u32[]{:S(2)}, u32[]{:S(2)}) collective-permute-start(bf16[2,24,2048]{2,1,0:T(8,128)(2,1)S(1)} %get-tuple-element.65), channel_id=1, source_target_pairs={{0,16},{1,9},{2,18},{3,11},{4,20},{5,13},{6,22},{7,15},{8,24},{9,1... | collective-permute-start | bytes 589832 | tf_op jit(solution)/shard_map/ppermute | solution.py:46
  66.3 7.8 %collective-permute-start.15 = (bf16[24,6144]{1,0:T(8,128)(2,1)S(1)}, bf16[24,6144]{1,0:T(8,128)(2,1)S(1)}, u32[]{:S(2)}, u32[]{:S(2)}) collective-permute-start(bf16[24,6144]{1,0:T(8,128)(2,1)S(1)} %get-tuple-element.64), channel_id=1, source_target_pairs={{0,8},{1,17},{2,10},{3,19},{4,12},{5,21},{6,14},{7,23},{8,0},{9,25... | collective-permute-start | bytes 884744 | tf_op jit(solution)/shard_map/ppermute | solution.py:46
  68.7 5.5 %collective-permute-start.17 = (bf16[24,2048]{1,0:T(8,128)(2,1)S(1)}, bf16[24,2048]{1,0:T(8,128)(2,1)S(1)}, u32[]{:S(2)}, u32[]{:S(2)}) collective-permute-start(bf16[24,2048]{1,0:T(8,128)(2,1)S(1)} %get-tuple-element.69), channel_id=1, source_target_pairs={{0,8},{1,17},{2,10},{3,19},{4,12},{5,21},{6,14},{7,23},{8,0},{9,25... | collective-permute-start | bytes 294920 | tf_op jit(solution)/shard_map/ppermute | solution.py:46
  70.3 1.3 %collective-permute-start.8 = (f32[12,1024]{1,0:T(8,128)S(1)}, f32[12,1024]{1,0:T(8,128)S(1)}, u32[]{:S(2)}, u32[]{:S(2)}) collective-permute-start(f32[12,1024]{1,0:T(8,128)S(1)} %get-tuple-element.55), channel_id=1, source_target_pairs={{0,1},{1,0},{2,3},{3,2},{4,5},{5,4},{6,7},{7,6},{8,9},{9,8},{10,11... | collective-permute-start | bytes 147464 | tf_op jit(solution)/shard_map/ppermute | solution.py:38
  (2 other events, 4.0 us)

commit v3 on v2

--- a/solution.py
+++ b/solution.py
@@ -46,7 +46,7 @@
     return lax.ppermute(x, ("blk", "grp"), pairs)
 
 
-def call(body, outs, *args, mib=8, flops=0, ins=None, scratch=(), aliases=None):
+def call(body, outs, *args, mib=4, flops=0, ins=None, scratch=(), aliases=None):
     return pl.pallas_call(
         body,
         out_shape=outs,
@@ -123,7 +123,7 @@
                 o[j * tile : (j + 1) * tile, at] = c[at, j * tile : (j + 1) * tile].T
 
     return call(
-        body, pltpu.VMEM((cols, rows), bf16), piece, *after, mib=8, ins=[VMEM] + [HBM] * len(after)
+        body, pltpu.VMEM((cols, rows), bf16), piece, *after, mib=2, ins=[VMEM] + [HBM] * len(after)
     )
 
 
@@ -144,6 +144,7 @@
     n_chunks = depth // width
     n_pieces, rows = 2 * n_chunks, width // 2
     piece = pltpu.VMEM((rows, width), bf16)
+    tile = min(256, half)
 
     near = cross(green, 0)
 
@@ -179,15 +180,16 @@
     aux_got = swap(aux_sent, "grp", 1)
 
     def bias_half(all_ref, c_refs, offset, start=0):
-        total = None
-        for k, c in enumerate(c_refs, start):
-            term = jnp.dot(
-                all_ref[:, k * rows : (k + 1) * rows],
-                c[:, pl.ds(pl.multiple_of(offset, half), half)],
-                preferred_element_type=f32,
-            )
-            total = term if total is None else total + term
-        return total
+        for n in range(0, half, tile):
+            total = None
+            for k, c in enumerate(c_refs, start):
+                term = jnp.dot(
+                    all_ref[:, k * rows : (k + 1) * rows],
+                    c[:, pl.ds(pl.multiple_of(offset + n, tile), tile)],
+                    preferred_element_type=f32,
+                )
+                total = term if total is None else total + term
+            yield slice(n, n + tile), total
 
     early = n_chunks
     here = n_pieces - 2
@@ -208,14 +210,17 @@
                 at = pl.ds(p * PAD, wb)
                 all_ref[at, :] = parts[p][...]
                 all_ref[pl.ds(p * PAD + wb, PAD - wb), :] = jnp.zeros((PAD - wb, depth), bf16)
-            part_ref[...] = bias_half(all_ref, c_refs[:early], core * half)
-            total_ref[...] = bias_half(all_ref, c_refs, (1 - core) * half)
+            for at, total in bias_half(all_ref, c_refs[:early], core * half):
+                part_ref[:, at] = total
+            for at, total in bias_half(all_ref, c_refs, (1 - core) * half):
+                total_ref[:, at] = total
 
         for c in copies:
             c.wait()
-        total = total_ref[...] + bias_half(all_ref, last_refs, (1 - core) * half, here)
-        for p in range(4):
-            sent_ref[blk ^ role(p, core)] = total[p * PAD : p * PAD + wb].astype(bf16)
+        for at, total in bias_half(all_ref, last_refs, (1 - core) * half, here):
+            total += total_ref[:, at]
+            for p in range(4):
+                sent_ref[blk ^ role(p, core), :, at] = total[p * PAD : p * PAD + wb].astype(bf16)
 
     flops1 = 2 * 128 * depth * half
     g_all, sent, part, *last = call(
@@ -238,9 +243,10 @@
     def second(all_ref, part_ref, *refs):
         c_refs, out_ref = refs[:-1], refs[-1]
         blk, _, core = ids()
-        total = part_ref[...] + bias_half(all_ref, c_refs, core * half, early)
-        for p in range(4):
-            out_ref[blk ^ role(p, core)] = total[p * PAD : p * PAD + wb]
+        for at, total in bias_half(all_ref, c_refs, core * half, early):
+            total += part_ref[:, at]
+            for p in range(4):
+                out_ref[blk ^ role(p, core), :, at] = total[p * PAD : p * PAD + wb]
 
     mine = call(second, struct((4, wb, half), f32), g_all, part, *pieces[early:], flops=flops1)
 
@@ -295,7 +301,6 @@
     s_mine = call(arrange, struct((4, PAD, half), bf16), *blocks, turned[-1], ins=[VMEM] * 4 + [HBM])
     s_other = swap(s_mine, "grp", 1)
     turned.append(transposed(pieces[7], s_mine))
-    n_turned = len(turned)
 
     groups = [range(n_pieces - 2, n_pieces), range(n_pieces // 2, n_pieces - 2), range(n_pieces // 2)]
 
@@ -306,19 +311,15 @@
             cols = pl.ds(pl.multiple_of(at * half, half), half)
             for p in range(4):
                 all_ref[p * PAD : (p + 1) * PAD, cols] = ref[role(p, core)]
-        for j, (k, c) in enumerate(zip(group, c_refs)):
-            if k < n_turned:
-                total = jnp.dot(all_ref[...], c[...], preferred_element_type=f32)
-            else:
-                total = lax.dot_general(
-                    c[...], all_ref[...], (((1,), (1,)), ((), ())), preferred_element_type=f32
-                ).T
-            block = [total[p * PAD : p * PAD + wb] for p in range(4)]
-            at = pl.ds(j * rows, rows)
-            own_ref[:, at] = block[0]
-            pass_ref[:, at] = block[1]
-            s_ref[0, :, at] = block[3].astype(bf16)
-            s_ref[1, :, at] = block[2].astype(bf16)
+        for j, c in enumerate(c_refs):
+            for n in range(0, rows, tile):
+                total = jnp.dot(all_ref[...], c[:, n : n + tile], preferred_element_type=f32)
+                block = [total[p * PAD : p * PAD + wb] for p in range(4)]
+                at = slice(j * rows + n, j * rows + n + tile)
+                own_ref[:, at] = block[0]
+                pass_ref[:, at] = block[1]
+                s_ref[0, :, at] = block[3].astype(bf16)
+                s_ref[1, :, at] = block[2].astype(bf16)
 
     def forward(*refs):
         out_ref, new_ref = refs[-2:]
@@ -330,14 +331,13 @@
             out_ref[:, at] = (pass_ref[...] + got_ref[0].astype(f32)).astype(bf16)
             new_ref[:, at] = own_ref[...] + got_ref[1].astype(f32)
 
-    right = turned + pieces[n_turned:]
     stage = []
     for group in groups:
         n = len(group) * rows
         sent, passed, mine = call(
             functools.partial(field, group),
             (struct((2, wb, n), bf16), struct((wb, n), f32), struct((wb, n), f32)),
-            s_mine, s_other, *right[group.start : group.stop], turned[-1],
+            s_mine, s_other, *turned[group.start : group.stop], turned[-1],
             flops=4 * 128 * width * width,
             ins=[VMEM] * (2 + len(group)) + [HBM],
             scratch=[pltpu.VMEM((4 * PAD, width), bf16)],

time: 75.1 us -> 66.7 us (0.89)
  local copies, waits for them, and re-layouts: 7.32 us -> 0 us
  Pallas kernels: 33.4 us -> 32.2 us
    unnamed x16 -> x0, local copies, waits for them, and re-layouts: 7.32 us -> none
    pallas_call x22, Pallas kernels: 33.4 us -> 32.2 us  [call(): pl.pallas_call(body, out_shape=outs, in_specs=ins or [VMEM] * len(args),...]
  transfers between devices with their start and end apart: 18 -> 18, of which waited for: 9 -> 9; matrix products, arithmetic and copies ran while one was open for 0% -> 0% of each run, Pallas kernels for 33% -> 37%
where the time goes in v3:
time: 66.7 us; the launch traced here: 66.5 us
  Pallas kernels  32.2 us (48%)
  starting transfers between devices  23.5 us (35%)
  waiting for transfers between devices  9.96 us (15%)
  between operations  0.84 us (1%)
    pallas_call x22, Pallas kernels, call(): pl.pallas_call(body, out_shape=outs, in_specs=ins or [VMEM] * len(args),...  32.2 us
    ppermute x8, starting transfers between devices, cross(): return lax.ppermute(x, ('blk', 'grp'), pairs)  14.5 us
    ppermute x10, starting transfers between devices, swap(): return lax.ppermute(x, axis, [(i, i ^ bit) for i in range(n)])  9.05 us
    ppermute x8, waiting for transfers between devices, cross(): return lax.ppermute(x, ('blk', 'grp'), pairs)  7.93 us
    ppermute x10, waiting for transfers between devices, swap(): return lax.ppermute(x, axis, [(i, i ^ bit) for i in range(n)])  2.03 us
  transfers between devices with their start and end apart: 18, of which 9 were waited for; matrix products, arithmetic and copies ran while one was open for 0% of the time, Pallas kernels for 37%

profile of v3, /device:TPU:0, one launch (start us, length us, event | category | flops | bytes accessed | tf_op | source)
XLA Modules:
  0.0 66.5 jit_solution(1712638434212380925)
XLA Ops:
  0.6 3.0 %collective-permute-start = (bf16[24,8192]{1,0:T(8,128)(2,1)}, bf16[24,8192]{1,0:T(8,128)(2,1)S(1)}, u32[]{:S(2)}, u32[]{:S(2)}) collective-permute-start(bf16[24,8192]{1,0:T(8,128)(2,1)} %g_ref.1), channel_id=1, source_target_pairs={{0,8},{1,17},{2,10},{3,19},{4,12},{5,21},{6,14},{7,23},{8,0},{9,25... | collective-permute-start | bytes 1179656 | tf_op jit(solution)/shard_map/ppermute | solution.py:46
  3.6 3.7 %shard_map.50 = (bf16[1024,2048]{1,0:T(8,128)(2,1)S(1)}, bf16[1024,2048]{1,0:T(8,128)(2,1)S(1)}, bf16[12,1024]{1,0:T(8,128)(2,1)S(1)}, bf16[12,1024]{1,0:T(8,128)(2,1)S(1)}, bf16[24,8192]{1,0:T(8,128)(2,1)S(1)}) custom-call(bf16[8192,2048]{1,0:T(8,128)(2,1)} %refs_10_.1, bf16[12,2048]{1,0:T(8,128)(2,1)} %aux_ref.1, bf16[24,8192]{1,0:T(8,128)(2,1)} %g_ref.1), custom_call_target="tpu_custom_call" | custom-call | flops 4000000000 | bytes 262144 | tf_op jit(solution)/shard_map/pallas_call | solution.py:50
  7.3 1.6 %collective-permute-start.1 = (bf16[24,8192]{1,0:T(8,128)(2,1)S(1)}, bf16[24,8192]{1,0:T(8,128)(2,1)S(1)}, u32[]{:S(2)}, u32[]{:S(2)}) collective-permute-start(bf16[24,8192]{1,0:T(8,128)(2,1)S(1)} %get-tuple-element.36.refs_0_), channel_id=1, source_target_pairs={{0,16},{1,9},{2,18},{3,11},{4,20},{5,13},{6,22},{7,15},{8,24},{9,1... | collective-permute-start | bytes 1179656 | tf_op jit(solution)/shard_map/ppermute | solution.py:46
  9.7 3.6 %collective-permute-start.2 = (bf16[24,8192]{1,0:T(8,128)(2,1)S(1)}, bf16[24,8192]{1,0:T(8,128)(2,1)S(1)}, u32[]{:S(2)}, u32[]{:S(2)}) collective-permute-start(bf16[24,8192]{1,0:T(8,128)(2,1)S(1)} %collective-permute-done.refs_1_), channel_id=1, source_target_pairs={{0,16},{1,9},{2,18},{3,11},{4,20},{5,13},{6,22},{7,15},{8,24},{9,1... | collective-permute-start | bytes 1179656 | tf_op jit(solution)/shard_map/ppermute | solution.py:46
  13.3 5.9 %shard_map.51 = (bf16[1024,2048]{1,0:T(8,128)(2,1)S(1)}, bf16[1024,2048]{1,0:T(8,128)(2,1)S(1)}, bf16[1024,2048]{1,0:T(8,128)(2,1)S(1)}, bf16[1024,2048]{1,0:T(8,128)(2,1)S(1)}) custom-call(bf16[8192,2048]{1,0:T(8,128)(2,1)} %refs_10_.1, bf16[12,1024]{1,0:T(8,128)(2,1)S(1)} %get-tuple-element.39._.aux_ref), custom_call_target="tpu_custom_call" | custom-call | flops 8000000000 | bytes 262144 | tf_op jit(solution)/shard_map/pallas_call | solution.py:50
  19.4 4.3 %shard_map.52 = (bf16[128,8192]{1,0:T(8,128)(2,1)S(1)}, bf16[4,24,1024]{2,1,0:T(8,128)(2,1)S(1)}, f32[128,1024]{1,0:T(8,128)S(1)}, bf16[1024,2048]{1,0:T(8,128)(2,1)S(1)}, bf16[1024,2048]{1,0:T(8,128)(2,1)S(1)}) custom-call(bf16[24,8192]{1,0:T(8,128)(2,1)S(1)} %get-tuple-element.36.refs_0_, bf16[24,8192]{1,0:T(8,128)(2,1)S(1)} %collective-permute-done.refs_1_, ...), custom_call_target="tpu_custom_call" | custom-call | flops 2147483648 | bytes 262144 | tf_op jit(solution)/shard_map/pallas_call | solution.py:50
  23.8 1.4 %shard_map.53.mine_ref = f32[4,24,1024]{2,1,0:T(8,128)S(1)} custom-call(bf16[128,8192]{1,0:T(8,128)(2,1)S(1)} %get-tuple-element.44.all_ref, f32[128,1024]{1,0:T(8,128)S(1)} %get-tuple-element.45.part_ref, bf16[1024,2048]{1,0:T(8,128)(2,1)S(1)} %get-tuple-element.42.refs_8_.refs_0_.refs_4_.refs_3_.refs_2_.refs_1_.c, ...), custom_call_target="tpu_custom_call" | custom-call | flops 2147483648 | bytes 262144 | tf_op jit(solution)/shard_map/pallas_call | solution.py:50
  25.3 1.6 %collective-permute-start.4 = (bf16[24,1024]{1,0:T(8,128)(2,1)S(1)}, bf16[24,1024]{1,0:T(8,128)(2,1)S(1)}, u32[]{:S(2)}, u32[]{:S(2)}) collective-permute-start(bf16[24,1024]{1,0:T(8,128)(2,1)S(1)} %get-tuple-element.50), channel_id=1, source_target_pairs={{0,2},{1,3},{2,0},{3,1},{4,6},{5,7},{6,4},{7,5},{8,10},{9,11},{10,... | collective-permute-start | bytes 147464 | tf_op jit(solution)/shard_map/ppermute | solution.py:38
  26.9 2.6 %collective-permute-start.5 = (bf16[24,1024]{1,0:T(8,128)(2,1)S(1)}, bf16[24,1024]{1,0:T(8,128)(2,1)S(1)}, u32[]{:S(2)}, u32[]{:S(2)}) collective-permute-start(bf16[24,1024]{1,0:T(8,128)(2,1)S(1)} %get-tuple-element.51), channel_id=1, source_target_pairs={{0,4},{1,5},{2,6},{3,7},{4,0},{5,1},{6,2},{7,3},{8,12},{9,13},{10,... | collective-permute-start | bytes 147464 | tf_op jit(solution)/shard_map/ppermute | solution.py:38
  29.7 1.3 %shard_map.55.refs_0_ = bf16[2048,1024]{1,0:T(8,128)(2,1)S(1)} custom-call(bf16[1024,2048]{1,0:T(8,128)(2,1)S(1)} %get-tuple-element.37.refs_4_.c, bf16[24,1024]{1,0:T(8,128)(2,1)S(1)} %collective-permute-done.4.refs_0_.r1, bf16[1024,2048]{1,0:T(8,128)(2,1)S(1)} %get-tuple-element.38.refs_5_.refs_1_.c, ...), custom_call_target="tpu_custom_call" | custom-call | bytes 262144 | tf_op jit(solution)/shard_map/pallas_call | solution.py:50
  31.0 1.3 %shard_map.56.refs_0_.refs_1_ = bf16[2048,1024]{1,0:T(8,128)(2,1)S(1)} custom-call(bf16[1024,2048]{1,0:T(8,128)(2,1)S(1)} %get-tuple-element.38.refs_5_.refs_1_.c, bf16[2048,1024]{1,0:T(8,128)(2,1)S(1)} %shard_map.55.refs_0_, bf16[1024,2048]{1,0:T(8,128)(2,1)S(1)} %get-tuple-element.40.refs_6_.refs_2_.refs_1_.c, ...), custom_call_target="tpu_custom_call" | custom-call | bytes 262144 | tf_op jit(solution)/shard_map/pallas_call | solution.py:50
  32.3 1.3 %shard_map.57.refs_0_.refs_2_ = bf16[2048,1024]{1,0:T(8,128)(2,1)S(1)} custom-call(bf16[1024,2048]{1,0:T(8,128)(2,1)S(1)} %get-tuple-element.40.refs_6_.refs_2_.refs_1_.c, bf16[2048,1024]{1,0:T(8,128)(2,1)S(1)} %shard_map.56.refs_0_.refs_1_, bf16[1024,2048]{1,0:T(8,128)(2,1)S(1)} %get-tuple-element.41.refs_7_.refs_3_.refs_2_.refs_1_.c, ...), custom_call_target="tpu_custom_call" | custom-call | bytes 262144 | tf_op jit(solution)/shard_map/pallas_call | solution.py:50
  33.6 1.3 %shard_map.58._.refs_3_ = bf16[2048,1024]{1,0:T(8,128)(2,1)S(1)} custom-call(bf16[1024,2048]{1,0:T(8,128)(2,1)S(1)} %get-tuple-element.41.refs_7_.refs_3_.refs_2_.refs_1_.c, bf16[2048,1024]{1,0:T(8,128)(2,1)S(1)} %shard_map.57.refs_0_.refs_2_, bf16[1024,2048]{1,0:T(8,128)(2,1)S(1)} %get-tuple-element.42.refs_8_.refs_0_.refs_4_.refs_3_.refs_2_.refs_1_.c, ...), custom_call_target="tpu_custom_call" | custom-call | bytes 262144 | tf_op jit(solution)/shard_map/pallas_call | solution.py:50
  35.4 3.2 %collective-permute-start.11 = (bf16[24,1024]{1,0:T(8,128)(2,1)S(1)}, bf16[24,1024]{1,0:T(8,128)(2,1)S(1)}, u32[]{:S(2)}, u32[]{:S(2)}) collective-permute-start(bf16[24,1024]{1,0:T(8,128)(2,1)S(1)} %get-tuple-element.56.refs_0_), channel_id=1, source_target_pairs={{0,6},{1,7},{2,4},{3,5},{4,2},{5,3},{6,0},{7,1},{8,14},{9,15},{10,... | collective-permute-start | bytes 147464 | tf_op jit(solution)/shard_map/ppermute | solution.py:38
  39.9 1.3 %shard_map.61.refs_0_ = bf16[2048,1024]{1,0:T(8,128)(2,1)S(1)} custom-call(bf16[1024,2048]{1,0:T(8,128)(2,1)S(1)} %get-tuple-element.42.refs_8_.refs_0_.refs_4_.refs_3_.refs_2_.refs_1_.c, bf16[24,1024]{1,0:T(8,128)(2,1)S(1)} %get-tuple-element.56.refs_0_, bf16[1024,2048]{1,0:T(8,128)(2,1)S(1)} %get-tuple-element.43.refs_9_.refs_1_.refs_5_.refs_4_.refs_3_.refs_2_.c, ...), custom_call_target="tpu_custom_call" | custom-call | bytes 262144 | tf_op jit(solution)/shard_map/pallas_call | solution.py:50
  41.2 1.3 %shard_map.62.refs_0_.refs_1_ = bf16[2048,1024]{1,0:T(8,128)(2,1)S(1)} custom-call(bf16[1024,2048]{1,0:T(8,128)(2,1)S(1)} %get-tuple-element.43.refs_9_.refs_1_.refs_5_.refs_4_.refs_3_.refs_2_.c, bf16[2048,1024]{1,0:T(8,128)(2,1)S(1)} %shard_map.61.refs_0_, bf16[1024,2048]{1,0:T(8,128)(2,1)S(1)} %get-tuple-element.46.refs_2_.refs_6_.refs_5_.refs_4_.refs_3_.refs_1_.c, ...), custom_call_target="tpu_custom_call" | custom-call | bytes 262144 | tf_op jit(solution)/shard_map/pallas_call | solution.py:50
  42.5 1.3 %shard_map.63.refs_4_.refs_0_ = bf16[2048,1024]{1,0:T(8,128)(2,1)S(1)} custom-call(bf16[1024,2048]{1,0:T(8,128)(2,1)S(1)} %get-tuple-element.46.refs_2_.refs_6_.refs_5_.refs_4_.refs_3_.refs_1_.c, bf16[2048,1024]{1,0:T(8,128)(2,1)S(1)} %shard_map.62.refs_0_.refs_1_, ...), custom_call_target="tpu_custom_call" | custom-call | bytes 262144 | tf_op jit(solution)/shard_map/pallas_call | solution.py:50
  43.9 1.3 %shard_map.65.refs_4_.refs_2_.refs_1_ = bf16[2048,1024]{1,0:T(8,128)(2,1)S(1)} custom-call(bf16[1024,2048]{1,0:T(8,128)(2,1)S(1)} %get-tuple-element.47.refs_3_.refs_7_.refs_6_.refs_5_.refs_4_.refs_2_.refs_1_.c, bf16[4,32,1024]{2,1,0:T(8,128)(2,1)S(1)} %shard_map.64.refs_0_.mine_ref), custom_call_target="tpu_custom_call" | custom-call | bytes 262144 | tf_op jit(solution)/shard_map/pallas_call | solution.py:50
  45.5 2.4 %shard_map.66 = (bf16[2,24,4096]{2,1,0:T(8,128)(2,1)S(1)}, f32[24,4096]{1,0:T(8,128)S(1)}, f32[24,4096]{1,0:T(8,128)S(1)}) custom-call(bf16[4,32,1024]{2,1,0:T(8,128)(2,1)S(1)} %shard_map.64.refs_0_.mine_ref, bf16[4,32,1024]{2,1,0:T(8,128)(2,1)S(1)} %collective-permute-done.12.other_ref, bf16[2048,1024]{1,0:T(8,128)(2,1)S(1)} %shard_map.55.refs_0_, ...), custom_call_target="tpu_custom_call" | custom-call | flops 2147483648 | bytes 262144 | tf_op jit(solution)/shard_map/pallas_call | solution.py:50
  47.8 1.6 %collective-permute-start.13 = (bf16[2,24,4096]{2,1,0:T(8,128)(2,1)S(1)}, bf16[2,24,4096]{2,1,0:T(8,128)(2,1)S(1)}, u32[]{:S(2)}, u32[]{:S(2)}) collective-permute-start(bf16[2,24,4096]{2,1,0:T(8,128)(2,1)S(1)} %get-tuple-element.57), channel_id=1, source_target_pairs={{0,16},{1,9},{2,18},{3,11},{4,20},{5,13},{6,22},{7,15},{8,24},{9,1... | collective-permute-start | bytes 1179656 | tf_op jit(solution)/shard_map/ppermute | solution.py:46
  49.4 1.3 %shard_map.67 = (bf16[2,24,2048]{2,1,0:T(8,128)(2,1)S(1)}, f32[24,2048]{1,0:T(8,128)S(1)}, f32[24,2048]{1,0:T(8,128)S(1)}) custom-call(bf16[4,32,1024]{2,1,0:T(8,128)(2,1)S(1)} %shard_map.64.refs_0_.mine_ref, bf16[4,32,1024]{2,1,0:T(8,128)(2,1)S(1)} %collective-permute-done.12.other_ref, bf16[2048,1024]{1,0:T(8,128)(2,1)S(1)} %shard_map.61.refs_0_, ...), custom_call_target="tpu_custom_call" | custom-call | flops 2147483648 | bytes 262144 | tf_op jit(solution)/shard_map/pallas_call | solution.py:50
  52.6 1.6 %collective-permute-start.16 = (bf16[2,24,2048]{2,1,0:T(8,128)(2,1)S(1)}, bf16[2,24,2048]{2,1,0:T(8,128)(2,1)S(1)}, u32[]{:S(2)}, u32[]{:S(2)}) collective-permute-start(bf16[2,24,2048]{2,1,0:T(8,128)(2,1)S(1)} %get-tuple-element.65), channel_id=1, source_target_pairs={{0,16},{1,9},{2,18},{3,11},{4,20},{5,13},{6,22},{7,15},{8,24},{9,1... | collective-permute-start | bytes 589832 | tf_op jit(solution)/shard_map/ppermute | solution.py:46
  54.1 3.6 %collective-permute-done.14.refs_3_ = bf16[2,24,2048]{2,1,0:T(8,128)(2,1)S(1)} collective-permute-done((bf16[2,24,2048]{2,1,0:T(8,128)(2,1)S(1)}, bf16[2,24,2048]{2,1,0:T(8,128)(2,1)S(1)}, u32[]{:S(2)}, u32[]{:S(2)}) %collective-permute-start.14) | collective-permute-done | bytes 196640 | tf_op jit(solution)/shard_map/ppermute | solution.py:46
  63.1 2.6 %collective-permute-done.17.last_got_ref = bf16[24,2048]{1,0:T(8,128)(2,1)S(1)} collective-permute-done((bf16[24,2048]{1,0:T(8,128)(2,1)S(1)}, bf16[24,2048]{1,0:T(8,128)(2,1)S(1)}, u32[]{:S(2)}, u32[]{:S(2)}) %collective-permute-start.17) | collective-permute-done | bytes 98336 | tf_op jit(solution)/shard_map/ppermute | solution.py:46
  (34 shorter events, 11.4 us)
Async XLA Ops:
  0.6 9.1 %collective-permute-start = (bf16[24,8192]{1,0:T(8,128)(2,1)}, bf16[24,8192]{1,0:T(8,128)(2,1)S(1)}, u32[]{:S(2)}, u32[]{:S(2)}) collective-permute-start(bf16[24,8192]{1,0:T(8,128)(2,1)} %g_ref.1), channel_id=1, source_target_pairs={{0,8},{1,17},{2,10},{3,19},{4,12},{5,21},{6,14},{7,23},{8,0},{9,25... | collective-permute-start | bytes 1179656 | tf_op jit(solution)/shard_map/ppermute | solution.py:46
  7.3 11.9 %collective-permute-start.1 = (bf16[24,8192]{1,0:T(8,128)(2,1)S(1)}, bf16[24,8192]{1,0:T(8,128)(2,1)S(1)}, u32[]{:S(2)}, u32[]{:S(2)}) collective-permute-start(bf16[24,8192]{1,0:T(8,128)(2,1)S(1)} %get-tuple-element.36.refs_0_), channel_id=1, source_target_pairs={{0,16},{1,9},{2,18},{3,11},{4,20},{5,13},{6,22},{7,15},{8,24},{9,1... | collective-permute-start | bytes 1179656 | tf_op jit(solution)/shard_map/ppermute | solution.py:46
  9.7 9.7 %collective-permute-start.2 = (bf16[24,8192]{1,0:T(8,128)(2,1)S(1)}, bf16[24,8192]{1,0:T(8,128)(2,1)S(1)}, u32[]{:S(2)}, u32[]{:S(2)}) collective-permute-start(bf16[24,8192]{1,0:T(8,128)(2,1)S(1)} %collective-permute-done.refs_1_), channel_id=1, source_target_pairs={{0,16},{1,9},{2,18},{3,11},{4,20},{5,13},{6,22},{7,15},{8,24},{9,1... | collective-permute-start | bytes 1179656 | tf_op jit(solution)/shard_map/ppermute | solution.py:46
  23.7 1.5 %collective-permute-start.3 = (bf16[4,24,1024]{2,1,0:T(8,128)(2,1)S(1)}, bf16[4,24,1024]{2,1,0:T(8,128)(2,1)S(1)}, u32[]{:S(2)}, u32[]{:S(2)}) collective-permute-start(bf16[4,24,1024]{2,1,0:T(8,128)(2,1)S(1)} %get-tuple-element.48), channel_id=1, source_target_pairs={{0,1},{1,0},{2,3},{3,2},{4,5},{5,4},{6,7},{7,6},{8,9},{9,8},{10,11... | collective-permute-start | bytes 589832 | tf_op jit(solution)/shard_map/ppermute | solution.py:38
  25.3 4.5 %collective-permute-start.4 = (bf16[24,1024]{1,0:T(8,128)(2,1)S(1)}, bf16[24,1024]{1,0:T(8,128)(2,1)S(1)}, u32[]{:S(2)}, u32[]{:S(2)}) collective-permute-start(bf16[24,1024]{1,0:T(8,128)(2,1)S(1)} %get-tuple-element.50), channel_id=1, source_target_pairs={{0,2},{1,3},{2,0},{3,1},{4,6},{5,7},{6,4},{7,5},{8,10},{9,11},{10,... | collective-permute-start | bytes 147464 | tf_op jit(solution)/shard_map/ppermute | solution.py:38
  26.9 8.0 %collective-permute-start.5 = (bf16[24,1024]{1,0:T(8,128)(2,1)S(1)}, bf16[24,1024]{1,0:T(8,128)(2,1)S(1)}, u32[]{:S(2)}, u32[]{:S(2)}) collective-permute-start(bf16[24,1024]{1,0:T(8,128)(2,1)S(1)} %get-tuple-element.51), channel_id=1, source_target_pairs={{0,4},{1,5},{2,6},{3,7},{4,0},{5,1},{6,2},{7,3},{8,12},{9,13},{10,... | collective-permute-start | bytes 147464 | tf_op jit(solution)/shard_map/ppermute | solution.py:38
  29.5 5.9 %collective-permute-start.6 = (bf16[24,1024]{1,0:T(8,128)(2,1)S(1)}, bf16[24,1024]{1,0:T(8,128)(2,1)S(1)}, u32[]{:S(2)}, u32[]{:S(2)}) collective-permute-start(bf16[24,1024]{1,0:T(8,128)(2,1)S(1)} %get-tuple-element.52), channel_id=1, source_target_pairs={{0,6},{1,7},{2,4},{3,5},{4,2},{5,3},{6,0},{7,1},{8,14},{9,15},{10,... | collective-permute-start | bytes 147464 | tf_op jit(solution)/shard_map/ppermute | solution.py:38
  29.7 5.2 %collective-permute-start.7 = (bf16[12,1024]{1,0:T(8,128)(2,1)S(1)}, bf16[12,1024]{1,0:T(8,128)(2,1)S(1)}, u32[]{:S(2)}, u32[]{:S(2)}) collective-permute-start(bf16[12,1024]{1,0:T(8,128)(2,1)S(1)} %get-tuple-element.53), channel_id=1, source_target_pairs={{0,1},{1,0},{2,3},{3,2},{4,5},{5,4},{6,7},{7,6},{8,9},{9,8},{10,11... | collective-permute-start | bytes 73736 | tf_op jit(solution)/shard_map/ppermute | solution.py:38
  35.4 8.3 %collective-permute-start.11 = (bf16[24,1024]{1,0:T(8,128)(2,1)S(1)}, bf16[24,1024]{1,0:T(8,128)(2,1)S(1)}, u32[]{:S(2)}, u32[]{:S(2)}) collective-permute-start(bf16[24,1024]{1,0:T(8,128)(2,1)S(1)} %get-tuple-element.56.refs_0_), channel_id=1, source_target_pairs={{0,6},{1,7},{2,4},{3,5},{4,2},{5,3},{6,0},{7,1},{8,14},{9,15},{10,... | collective-permute-start | bytes 147464 | tf_op jit(solution)/shard_map/ppermute | solution.py:38
  38.7 5.2 %collective-permute-start.10 = (bf16[24,1024]{1,0:T(8,128)(2,1)S(1)}, bf16[24,1024]{1,0:T(8,128)(2,1)S(1)}, u32[]{:S(2)}, u32[]{:S(2)}) collective-permute-start(bf16[24,1024]{1,0:T(8,128)(2,1)S(1)} %get-tuple-element.56.refs_0_), channel_id=1, source_target_pairs={{0,4},{1,5},{2,6},{3,7},{4,0},{5,1},{6,2},{7,3},{8,12},{9,13},{10,... | collective-permute-start | bytes 147464 | tf_op jit(solution)/shard_map/ppermute | solution.py:38
  38.7 5.2 %collective-permute-start.9 = (bf16[24,1024]{1,0:T(8,128)(2,1)S(1)}, bf16[24,1024]{1,0:T(8,128)(2,1)S(1)}, u32[]{:S(2)}, u32[]{:S(2)}) collective-permute-start(bf16[24,1024]{1,0:T(8,128)(2,1)S(1)} %get-tuple-element.56.refs_0_), channel_id=1, source_target_pairs={{0,2},{1,3},{2,0},{3,1},{4,6},{5,7},{6,4},{7,5},{8,10},{9,11},{10,... | collective-permute-start | bytes 147464 | tf_op jit(solution)/shard_map/ppermute | solution.py:38
  43.9 1.6 %collective-permute-start.12 = (bf16[4,32,1024]{2,1,0:T(8,128)(2,1)S(1)}, bf16[4,32,1024]{2,1,0:T(8,128)(2,1)S(1)}, u32[]{:S(2)}, u32[]{:S(2)}) collective-permute-start(bf16[4,32,1024]{2,1,0:T(8,128)(2,1)S(1)} %shard_map.64.refs_0_.mine_ref), channel_id=1, source_target_pairs={{0,1},{1,0},{2,3},{3,2},{4,5},{5,4},{6,7},{7,6},{8,9},{9,8},{10,11... | collective-permute-start | bytes 786440 | tf_op jit(solution)/shard_map/ppermute | solution.py:38
  47.8 10.0 %collective-permute-start.13 = (bf16[2,24,4096]{2,1,0:T(8,128)(2,1)S(1)}, bf16[2,24,4096]{2,1,0:T(8,128)(2,1)S(1)}, u32[]{:S(2)}, u32[]{:S(2)}) collective-permute-start(bf16[2,24,4096]{2,1,0:T(8,128)(2,1)S(1)} %get-tuple-element.57), channel_id=1, source_target_pairs={{0,16},{1,9},{2,18},{3,11},{4,20},{5,13},{6,22},{7,15},{8,24},{9,1... | collective-permute-start | bytes 1179656 | tf_op jit(solution)/shard_map/ppermute | solution.py:46
  50.7 7.1 %collective-permute-start.14 = (bf16[2,24,2048]{2,1,0:T(8,128)(2,1)S(1)}, bf16[2,24,2048]{2,1,0:T(8,128)(2,1)S(1)}, u32[]{:S(2)}, u32[]{:S(2)}) collective-permute-start(bf16[2,24,2048]{2,1,0:T(8,128)(2,1)S(1)} %get-tuple-element.60), channel_id=1, source_target_pairs={{0,16},{1,9},{2,18},{3,11},{4,20},{5,13},{6,22},{7,15},{8,24},{9,1... | collective-permute-start | bytes 589832 | tf_op jit(solution)/shard_map/ppermute | solution.py:46
  52.6 7.3 %collective-permute-start.16 = (bf16[2,24,2048]{2,1,0:T(8,128)(2,1)S(1)}, bf16[2,24,2048]{2,1,0:T(8,128)(2,1)S(1)}, u32[]{:S(2)}, u32[]{:S(2)}) collective-permute-start(bf16[2,24,2048]{2,1,0:T(8,128)(2,1)S(1)} %get-tuple-element.65), channel_id=1, source_target_pairs={{0,16},{1,9},{2,18},{3,11},{4,20},{5,13},{6,22},{7,15},{8,24},{9,1... | collective-permute-start | bytes 589832 | tf_op jit(solution)/shard_map/ppermute | solution.py:46
  57.9 7.8 %collective-permute-start.15 = (bf16[24,6144]{1,0:T(8,128)(2,1)S(1)}, bf16[24,6144]{1,0:T(8,128)(2,1)S(1)}, u32[]{:S(2)}, u32[]{:S(2)}) collective-permute-start(bf16[24,6144]{1,0:T(8,128)(2,1)S(1)} %get-tuple-element.64), channel_id=1, source_target_pairs={{0,8},{1,17},{2,10},{3,19},{4,12},{5,21},{6,14},{7,23},{8,0},{9,25... | collective-permute-start | bytes 884744 | tf_op jit(solution)/shard_map/ppermute | solution.py:46
  59.9 5.8 %collective-permute-start.17 = (bf16[24,2048]{1,0:T(8,128)(2,1)S(1)}, bf16[24,2048]{1,0:T(8,128)(2,1)S(1)}, u32[]{:S(2)}, u32[]{:S(2)}) collective-permute-start(bf16[24,2048]{1,0:T(8,128)(2,1)S(1)} %get-tuple-element.69), channel_id=1, source_target_pairs={{0,8},{1,17},{2,10},{3,19},{4,12},{5,21},{6,14},{7,23},{8,0},{9,25... | collective-permute-start | bytes 294920 | tf_op jit(solution)/shard_map/ppermute | solution.py:46
  61.2 1.3 %collective-permute-start.8 = (f32[12,1024]{1,0:T(8,128)S(1)}, f32[12,1024]{1,0:T(8,128)S(1)}, u32[]{:S(2)}, u32[]{:S(2)}) collective-permute-start(f32[12,1024]{1,0:T(8,128)S(1)} %get-tuple-element.55), channel_id=1, source_target_pairs={{0,1},{1,0},{2,3},{3,2},{4,5},{5,4},{6,7},{7,6},{8,9},{9,8},{10,11... | collective-permute-start | bytes 147464 | tf_op jit(solution)/shard_map/ppermute | solution.py:38

commit v4 on v3

--- a/solution.py
+++ b/solution.py
@@ -46,7 +46,7 @@
     return lax.ppermute(x, ("blk", "grp"), pairs)
 
 
-def call(body, outs, *args, mib=4, flops=0, ins=None, scratch=(), aliases=None):
+def call(body, outs, *args, mib=3, flops=0, ins=None, scratch=(), aliases=None):
     return pl.pallas_call(
         body,
         out_shape=outs,
@@ -253,17 +253,17 @@
     def combine(mine_ref, other_ref, keep_ref, *sent_refs):
         _, z, _ = ids()
         keep_ref[...] = mine_ref[z] + other_ref[z].astype(f32)
-        for t, s in enumerate(sent_refs, 1):
+        for t, s in zip((2, 3, 1), sent_refs):
             s[...] = (mine_ref[z ^ t] + other_ref[z ^ t].astype(f32)).astype(bf16)
 
     keep, *sums = call(
         combine, (struct((wb, half), f32),) + (struct((wb, half), bf16),) * 3, mine, other
     )
-    sums = [swap(s, "grp", 2 * t) for t, s in enumerate(sums, 1)]
+    sums = [swap(s, "grp", 2 * t) for t, s in zip((2, 3, 1), sums)]
     turned = []
-    for k in range(4):
+    for k in range(3):
         turned.append(
-            transposed(pieces[k], turned[-1] if turned else sums[0], *pieces[k + 1 :])
+            transposed(pieces[k], turned[-1] if turned else keep, *pieces[k + 1 :])
         )
 
     def shift(keep_ref, r1, r2, r3, aux_ref, got_ref, _, bias_ref, give_ref, out_ref):
@@ -285,9 +285,8 @@
         keep, *sums, aux_kept, aux_got, turned[-1],
         ins=[VMEM] * 6 + [HBM],
     )
-    turned.append(transposed(pieces[4], shifted, *pieces[5:]))
-    turned.append(transposed(pieces[5], turned[-1], *pieces[6:]))
-    turned.append(transposed(pieces[6], turned[-1], *pieces[7:]))
+    for k in range(3, 6):
+        turned.append(transposed(pieces[k], shifted if k == 3 else turned[-1], *pieces[k + 1 :]))
     blocks = [shifted] + [swap(shifted, "grp", 2 * t) for t in (1, 2, 3)]
     bias_got = swap(give, "grp", 1)
 
@@ -300,26 +299,92 @@
 
     s_mine = call(arrange, struct((4, PAD, half), bf16), *blocks, turned[-1], ins=[VMEM] * 4 + [HBM])
     s_other = swap(s_mine, "grp", 1)
-    turned.append(transposed(pieces[7], s_mine))
-
-    groups = [range(n_pieces - 2, n_pieces), range(n_pieces // 2, n_pieces - 2), range(n_pieces // 2)]
+
+    n_first = n_pieces // 2
+    groups = [range(n_first), range(n_first, n_pieces - 2), range(n_pieces - 2, n_pieces)]
+
+    def placed(all_ref, ref, start):
+        _, _, core = ids()
+        for p in range(4):
+            all_ref[p * PAD : (p + 1) * PAD, pl.ds(start, half)] = ref[role(p, core)]
+
+    def tiles(c_refs):
+        return [(c, n, slice(j * rows + n, j * rows + n + tile)) for j, c in enumerate(c_refs) for n in range(0, rows, tile)]
+
+    def stored(total, at, s_ref, pass_ref, own_ref):
+        block = [total[p * PAD : p * PAD + wb] for p in range(4)]
+        own_ref[:, at] = block[0]
+        pass_ref[:, at] = block[1]
+        s_ref[0, :, at] = block[3].astype(bf16)
+        s_ref[1, :, at] = block[2].astype(bf16)
+
+    def field_mine(mine_ref, *refs):
+        c_refs, (part_ref, all_ref) = refs[:-2], refs[-2:]
+        _, _, core = ids()
+        placed(all_ref, mine_ref, 0)
+        k = pl.ds(pl.multiple_of(core * half, half), half)
+        for c, n, at in tiles(c_refs):
+            part_ref[:, at] = jnp.dot(all_ref[...], c[k, n : n + tile], preferred_element_type=f32)
+
+    def field_other(other_ref, part_ref, *refs):
+        c_refs, (*outs, all_ref) = refs[:-4], refs[-4:]
+        _, _, core = ids()
+        placed(all_ref, other_ref, 0)
+        k = pl.ds(pl.multiple_of((1 - core) * half, half), half)
+        for c, n, at in tiles(c_refs):
+            total = jnp.dot(all_ref[...], c[k, n : n + tile], preferred_element_type=f32)
+            stored(part_ref[:, at] + total, at, *outs)
 
     def field(group, mine_ref, other_ref, *refs):
-        c_refs, (s_ref, pass_ref, own_ref, all_ref) = refs[: len(group)], refs[-4:]
-        _, _, core = ids()
-        for ref, at in ((mine_ref, core), (other_ref, 1 - core)):
-            cols = pl.ds(pl.multiple_of(at * half, half), half)
-            for p in range(4):
-                all_ref[p * PAD : (p + 1) * PAD, cols] = ref[role(p, core)]
-        for j, c in enumerate(c_refs):
-            for n in range(0, rows, tile):
+        c_refs, (*outs, all_ref) = refs[: len(group)], refs[-4:]
+        _, _, core = ids()
+        placed(all_ref, mine_ref, pl.multiple_of(core * half, half))
+        placed(all_ref, other_ref, pl.multiple_of((1 - core) * half, half))
+        for c, n, at in tiles(c_refs):
+            if group.start < len(turned):
                 total = jnp.dot(all_ref[...], c[:, n : n + tile], preferred_element_type=f32)
-                block = [total[p * PAD : p * PAD + wb] for p in range(4)]
-                at = slice(j * rows + n, j * rows + n + tile)
-                own_ref[:, at] = block[0]
-                pass_ref[:, at] = block[1]
-                s_ref[0, :, at] = block[3].astype(bf16)
-                s_ref[1, :, at] = block[2].astype(bf16)
+            else:
+                total = lax.dot_general(
+                    c[n : n + tile, :], all_ref[...], (((1,), (1,)), ((), ())), preferred_element_type=f32
+                ).T
+            stored(total, at, *outs)
+
+    def outs(group):
+        n = len(group) * rows
+        return struct((2, wb, n), bf16), struct((wb, n), f32), struct((wb, n), f32)
+
+    some = [pltpu.VMEM((4 * PAD, half), bf16)]
+    whole = [pltpu.VMEM((4 * PAD, width), bf16)]
+    part = call(
+        field_mine,
+        struct((4 * PAD, n_first * rows), f32),
+        s_mine, *turned[:n_first],
+        scratch=some,
+    )
+
+    def later(group, after):
+        n = len(group)
+        return call(
+            functools.partial(field, group),
+            outs(group),
+            s_mine, s_other, *(turned + pieces[len(turned) :])[group.start : group.stop], after,
+            flops=4 * 128 * width * width,
+            ins=[VMEM] * (2 + n) + [HBM],
+            scratch=whole,
+        )
+
+    middle = later(groups[1], s_mine)
+    last = later(groups[2], middle[2])
+    opening = call(
+        field_other,
+        outs(groups[0]),
+        s_other, part, *turned[:n_first],
+        flops=4 * 128 * width * width,
+        scratch=some,
+    )
+    stage = []
+    for sent, passed, mine in (last, middle, opening):
+        stage.append((cross(sent, 1), passed, mine))
 
     def forward(*refs):
         out_ref, new_ref = refs[-2:]
@@ -331,18 +396,6 @@
             out_ref[:, at] = (pass_ref[...] + got_ref[0].astype(f32)).astype(bf16)
             new_ref[:, at] = own_ref[...] + got_ref[1].astype(f32)
 
-    stage = []
-    for group in groups:
-        n = len(group) * rows
-        sent, passed, mine = call(
-            functools.partial(field, group),
-            (struct((2, wb, n), bf16), struct((wb, n), f32), struct((wb, n), f32)),
-            s_mine, s_other, *turned[group.start : group.stop], turned[-1],
-            flops=4 * 128 * width * width,
-            ins=[VMEM] * (2 + len(group)) + [HBM],
-            scratch=[pltpu.VMEM((4 * PAD, width), bf16)],
-        )
-        stage.append((cross(sent, 1), passed, mine))
     done = []
     for part in (stage[1:][::-1], stage[:1]):
         n = sum(s[2].shape[1] for s in part)

time: 66.7 us -> 64.4 us (0.966)
  Pallas kernels: 32.2 us -> 31 us
  waiting for transfers between devices: 9.96 us -> 9.08 us
    pallas_call x22 -> x21, Pallas kernels: 32.2 us -> 31 us  [call(): pl.pallas_call(body, out_shape=outs, in_specs=ins or [VMEM] * len(args),...]
    ppermute x8, waiting for transfers between devices: 7.93 us -> 6.76 us  [cross(): return lax.ppermute(x, ('blk', 'grp'), pairs)]
  transfers between devices with their start and end apart: 18 -> 18, of which waited for: 9 -> 9; matrix products, arithmetic and copies ran while one was open for 0% -> 0% of each run, Pallas kernels for 37% -> 38%
where the time goes in v4:
time: 64.4 us; the launch traced here: 64.2 us
  Pallas kernels  31 us (48%)
  starting transfers between devices  23.3 us (36%)
  waiting for transfers between devices  9.08 us (14%)
  between operations  0.84 us (1%)
    pallas_call x21, Pallas kernels, call(): pl.pallas_call(body, out_shape=outs, in_specs=ins or [VMEM] * len(args),...  31 us
    ppermute x8, starting transfers between devices, cross(): return lax.ppermute(x, ('blk', 'grp'), pairs)  14.4 us
    ppermute x10, starting transfers between devices, swap(): return lax.ppermute(x, axis, [(i, i ^ bit) for i in range(n)])  8.83 us
    ppermute x8, waiting for transfers between devices, cross(): return lax.ppermute(x, ('blk', 'grp'), pairs)  6.76 us
    ppermute x10, waiting for transfers between devices, swap(): return lax.ppermute(x, axis, [(i, i ^ bit) for i in range(n)])  2.32 us
  transfers between devices with their start and end apart: 18, of which 9 were waited for; matrix products, arithmetic and copies ran while one was open for 0% of the time, Pallas kernels for 38%

profile of v4, /device:TPU:0, one launch (start us, length us, event | category | flops | bytes accessed | tf_op | source)
XLA Modules:
  0.0 64.2 jit_solution(11857940718597241210)
XLA Ops:
  0.6 3.0 %collective-permute-start = (bf16[24,8192]{1,0:T(8,128)(2,1)}, bf16[24,8192]{1,0:T(8,128)(2,1)S(1)}, u32[]{:S(2)}, u32[]{:S(2)}) collective-permute-start(bf16[24,8192]{1,0:T(8,128)(2,1)} %g_ref.1), channel_id=1, source_target_pairs={{0,8},{1,17},{2,10},{3,19},{4,12},{5,21},{6,14},{7,23},{8,0},{9,25... | collective-permute-start | bytes 1179656 | tf_op jit(solution)/shard_map/ppermute | solution.py:46
  3.6 3.7 %shard_map.50 = (bf16[1024,2048]{1,0:T(8,128)(2,1)S(1)}, bf16[1024,2048]{1,0:T(8,128)(2,1)S(1)}, bf16[12,1024]{1,0:T(8,128)(2,1)S(1)}, bf16[12,1024]{1,0:T(8,128)(2,1)S(1)}, bf16[24,8192]{1,0:T(8,128)(2,1)S(1)}) custom-call(bf16[8192,2048]{1,0:T(8,128)(2,1)} %refs_10_.1, bf16[12,2048]{1,0:T(8,128)(2,1)} %aux_ref.1, bf16[24,8192]{1,0:T(8,128)(2,1)} %g_ref.1), custom_call_target="tpu_custom_call" | custom-call | flops 4000000000 | bytes 262144 | tf_op jit(solution)/shard_map/pallas_call | solution.py:50
  7.3 1.6 %collective-permute-start.1 = (bf16[24,8192]{1,0:T(8,128)(2,1)S(1)}, bf16[24,8192]{1,0:T(8,128)(2,1)S(1)}, u32[]{:S(2)}, u32[]{:S(2)}) collective-permute-start(bf16[24,8192]{1,0:T(8,128)(2,1)S(1)} %get-tuple-element.36.refs_0_), channel_id=1, source_target_pairs={{0,16},{1,9},{2,18},{3,11},{4,20},{5,13},{6,22},{7,15},{8,24},{9,1... | collective-permute-start | bytes 1179656 | tf_op jit(solution)/shard_map/ppermute | solution.py:46
  9.7 3.6 %collective-permute-start.2 = (bf16[24,8192]{1,0:T(8,128)(2,1)S(1)}, bf16[24,8192]{1,0:T(8,128)(2,1)S(1)}, u32[]{:S(2)}, u32[]{:S(2)}) collective-permute-start(bf16[24,8192]{1,0:T(8,128)(2,1)S(1)} %collective-permute-done.refs_1_), channel_id=1, source_target_pairs={{0,16},{1,9},{2,18},{3,11},{4,20},{5,13},{6,22},{7,15},{8,24},{9,1... | collective-permute-start | bytes 1179656 | tf_op jit(solution)/shard_map/ppermute | solution.py:46
  13.3 5.9 %shard_map.51 = (bf16[1024,2048]{1,0:T(8,128)(2,1)S(1)}, bf16[1024,2048]{1,0:T(8,128)(2,1)S(1)}, bf16[1024,2048]{1,0:T(8,128)(2,1)S(1)}, bf16[1024,2048]{1,0:T(8,128)(2,1)S(1)}) custom-call(bf16[8192,2048]{1,0:T(8,128)(2,1)} %refs_10_.1, bf16[12,1024]{1,0:T(8,128)(2,1)S(1)} %get-tuple-element.39._.aux_ref), custom_call_target="tpu_custom_call" | custom-call | flops 8000000000 | bytes 262144 | tf_op jit(solution)/shard_map/pallas_call | solution.py:50
  19.4 4.3 %shard_map.52 = (bf16[128,8192]{1,0:T(8,128)(2,1)S(1)}, bf16[4,24,1024]{2,1,0:T(8,128)(2,1)S(1)}, f32[128,1024]{1,0:T(8,128)S(1)}, bf16[1024,2048]{1,0:T(8,128)(2,1)S(1)}, bf16[1024,2048]{1,0:T(8,128)(2,1)S(1)}) custom-call(bf16[24,8192]{1,0:T(8,128)(2,1)S(1)} %get-tuple-element.36.refs_0_, bf16[24,8192]{1,0:T(8,128)(2,1)S(1)} %collective-permute-done.refs_1_, ...), custom_call_target="tpu_custom_call" | custom-call | flops 2147483648 | bytes 262144 | tf_op jit(solution)/shard_map/pallas_call | solution.py:50
  23.8 1.4 %shard_map.53.mine_ref = f32[4,24,1024]{2,1,0:T(8,128)S(1)} custom-call(bf16[128,8192]{1,0:T(8,128)(2,1)S(1)} %get-tuple-element.44.all_ref, f32[128,1024]{1,0:T(8,128)S(1)} %get-tuple-element.45.part_ref, bf16[1024,2048]{1,0:T(8,128)(2,1)S(1)} %get-tuple-element.42.refs_8_.refs_0_.refs_4_.refs_3_.refs_2_.refs_1_.c, ...), custom_call_target="tpu_custom_call" | custom-call | flops 2147483648 | bytes 262144 | tf_op jit(solution)/shard_map/pallas_call | solution.py:50
  25.3 2.7 %collective-permute-start.4 = (bf16[24,1024]{1,0:T(8,128)(2,1)S(1)}, bf16[24,1024]{1,0:T(8,128)(2,1)S(1)}, u32[]{:S(2)}, u32[]{:S(2)}) collective-permute-start(bf16[24,1024]{1,0:T(8,128)(2,1)S(1)} %get-tuple-element.50), channel_id=1, source_target_pairs={{0,4},{1,5},{2,6},{3,7},{4,0},{5,1},{6,2},{7,3},{8,12},{9,13},{10,... | collective-permute-start | bytes 147464 | tf_op jit(solution)/shard_map/ppermute | solution.py:38
  27.9 1.3 %collective-permute-start.5 = (bf16[24,1024]{1,0:T(8,128)(2,1)S(1)}, bf16[24,1024]{1,0:T(8,128)(2,1)S(1)}, u32[]{:S(2)}, u32[]{:S(2)}) collective-permute-start(bf16[24,1024]{1,0:T(8,128)(2,1)S(1)} %get-tuple-element.51), channel_id=1, source_target_pairs={{0,6},{1,7},{2,4},{3,5},{4,2},{5,3},{6,0},{7,1},{8,14},{9,15},{10,... | collective-permute-start | bytes 147464 | tf_op jit(solution)/shard_map/ppermute | solution.py:38
  29.5 1.3 %shard_map.55.refs_0_ = bf16[2048,1024]{1,0:T(8,128)(2,1)S(1)} custom-call(bf16[1024,2048]{1,0:T(8,128)(2,1)S(1)} %get-tuple-element.37.refs_4_.c, f32[24,1024]{1,0:T(8,128)S(1)} %get-tuple-element.49.refs_0_.keep_ref, bf16[1024,2048]{1,0:T(8,128)(2,1)S(1)} %get-tuple-element.38.refs_5_.refs_1_.c, ...), custom_call_target="tpu_custom_call" | custom-call | bytes 262144 | tf_op jit(solution)/shard_map/pallas_call | solution.py:50
  30.8 1.3 %shard_map.56.refs_0_.refs_1_ = bf16[2048,1024]{1,0:T(8,128)(2,1)S(1)} custom-call(bf16[1024,2048]{1,0:T(8,128)(2,1)S(1)} %get-tuple-element.38.refs_5_.refs_1_.c, bf16[2048,1024]{1,0:T(8,128)(2,1)S(1)} %shard_map.55.refs_0_, bf16[1024,2048]{1,0:T(8,128)(2,1)S(1)} %get-tuple-element.40.refs_6_.refs_2_.refs_1_.c, ...), custom_call_target="tpu_custom_call" | custom-call | bytes 262144 | tf_op jit(solution)/shard_map/pallas_call | solution.py:50
  32.1 1.3 %shard_map.57._.refs_2_ = bf16[2048,1024]{1,0:T(8,128)(2,1)S(1)} custom-call(bf16[1024,2048]{1,0:T(8,128)(2,1)S(1)} %get-tuple-element.40.refs_6_.refs_2_.refs_1_.c, bf16[2048,1024]{1,0:T(8,128)(2,1)S(1)} %shard_map.56.refs_0_.refs_1_, bf16[1024,2048]{1,0:T(8,128)(2,1)S(1)} %get-tuple-element.41.refs_7_.refs_3_.refs_2_.refs_1_.c, ...), custom_call_target="tpu_custom_call" | custom-call | bytes 262144 | tf_op jit(solution)/shard_map/pallas_call | solution.py:50
  34.3 2.9 %collective-permute-start.11 = (bf16[24,1024]{1,0:T(8,128)(2,1)S(1)}, bf16[24,1024]{1,0:T(8,128)(2,1)S(1)}, u32[]{:S(2)}, u32[]{:S(2)}) collective-permute-start(bf16[24,1024]{1,0:T(8,128)(2,1)S(1)} %get-tuple-element.56.refs_0_), channel_id=1, source_target_pairs={{0,6},{1,7},{2,4},{3,5},{4,2},{5,3},{6,0},{7,1},{8,14},{9,15},{10,... | collective-permute-start | bytes 147464 | tf_op jit(solution)/shard_map/ppermute | solution.py:38
  37.1 1.6 %collective-permute-start.9 = (bf16[24,1024]{1,0:T(8,128)(2,1)S(1)}, bf16[24,1024]{1,0:T(8,128)(2,1)S(1)}, u32[]{:S(2)}, u32[]{:S(2)}) collective-permute-start(bf16[24,1024]{1,0:T(8,128)(2,1)S(1)} %get-tuple-element.56.refs_0_), channel_id=1, source_target_pairs={{0,2},{1,3},{2,0},{3,1},{4,6},{5,7},{6,4},{7,5},{8,10},{9,11},{10,... | collective-permute-start | bytes 147464 | tf_op jit(solution)/shard_map/ppermute | solution.py:38
  38.7 1.3 %shard_map.60.refs_0_.refs_3_ = bf16[2048,1024]{1,0:T(8,128)(2,1)S(1)} custom-call(bf16[1024,2048]{1,0:T(8,128)(2,1)S(1)} %get-tuple-element.41.refs_7_.refs_3_.refs_2_.refs_1_.c, bf16[24,1024]{1,0:T(8,128)(2,1)S(1)} %get-tuple-element.56.refs_0_, bf16[1024,2048]{1,0:T(8,128)(2,1)S(1)} %get-tuple-element.42.refs_8_.refs_0_.refs_4_.refs_3_.refs_2_.refs_1_.c, ...), custom_call_target="tpu_custom_call" | custom-call | bytes 262144 | tf_op jit(solution)/shard_map/pallas_call | solution.py:50
  40.0 1.3 %shard_map.61.refs_0_ = bf16[2048,1024]{1,0:T(8,128)(2,1)S(1)} custom-call(bf16[1024,2048]{1,0:T(8,128)(2,1)S(1)} %get-tuple-element.42.refs_8_.refs_0_.refs_4_.refs_3_.refs_2_.refs_1_.c, bf16[2048,1024]{1,0:T(8,128)(2,1)S(1)} %shard_map.60.refs_0_.refs_3_, bf16[1024,2048]{1,0:T(8,128)(2,1)S(1)} %get-tuple-element.43.refs_9_.refs_1_.refs_5_.refs_4_.refs_3_.refs_2_.c, ...), custom_call_target="tpu_custom_call" | custom-call | bytes 262144 | tf_op jit(solution)/shard_map/pallas_call | solution.py:50
  41.3 1.3 %shard_map.62.refs_4_.refs_1_ = bf16[2048,1024]{1,0:T(8,128)(2,1)S(1)} custom-call(bf16[1024,2048]{1,0:T(8,128)(2,1)S(1)} %get-tuple-element.43.refs_9_.refs_1_.refs_5_.refs_4_.refs_3_.refs_2_.c, bf16[2048,1024]{1,0:T(8,128)(2,1)S(1)} %shard_map.61.refs_0_, bf16[1024,2048]{1,0:T(8,128)(2,1)S(1)} %get-tuple-element.46.refs_2_.refs_6_.refs_5_.refs_4_.refs_3_.refs_1_.refs_0_, ...), custom_call_target="tpu_custom_call" | custom-call | bytes 262144 | tf_op jit(solution)/shard_map/pallas_call | solution.py:50
  42.7 1.3 %shard_map.64.part_ref = f32[128,4096]{1,0:T(8,128)S(1)} custom-call(bf16[4,32,1024]{2,1,0:T(8,128)(2,1)S(1)} %shard_map.63.mine_ref.refs_2_, bf16[2048,1024]{1,0:T(8,128)(2,1)S(1)} %shard_map.55.refs_0_, bf16[2048,1024]{1,0:T(8,128)(2,1)S(1)} %shard_map.56.refs_0_.refs_1_, bf16[2048,1024]{1,0:T(8,128)(2,1)S(1)} %shard_map.57._.refs_2_, ...), custom_call_target="tpu_custom_call" | custom-call | bytes 262144 | tf_op jit(solution)/shard_map/pallas_call | solution.py:50
  44.3 1.3 %shard_map.65 = (bf16[2,24,4096]{2,1,0:T(8,128)(2,1)S(1)}, f32[24,4096]{1,0:T(8,128)S(1)}, f32[24,4096]{1,0:T(8,128)S(1)}) custom-call(bf16[4,32,1024]{2,1,0:T(8,128)(2,1)S(1)} %collective-permute-done.12.other_ref, f32[128,4096]{1,0:T(8,128)S(1)} %shard_map.64.part_ref, bf16[2048,1024]{1,0:T(8,128)(2,1)S(1)} %shard_map.55.refs_0_, ...), custom_call_target="tpu_custom_call" | custom-call | flops 2147483648 | bytes 262144 | tf_op jit(solution)/shard_map/pallas_call | solution.py:50
  45.5 1.6 %collective-permute-start.13 = (bf16[2,24,4096]{2,1,0:T(8,128)(2,1)S(1)}, bf16[2,24,4096]{2,1,0:T(8,128)(2,1)S(1)}, u32[]{:S(2)}, u32[]{:S(2)}) collective-permute-start(bf16[2,24,4096]{2,1,0:T(8,128)(2,1)S(1)} %get-tuple-element.57), channel_id=1, source_target_pairs={{0,16},{1,9},{2,18},{3,11},{4,20},{5,13},{6,22},{7,15},{8,24},{9,1... | collective-permute-start | bytes 1179656 | tf_op jit(solution)/shard_map/ppermute | solution.py:46
  49.0 2.5 %shard_map.68 = (bf16[2,24,2048]{2,1,0:T(8,128)(2,1)S(1)}, f32[24,2048]{1,0:T(8,128)S(1)}, f32[24,2048]{1,0:T(8,128)S(1)}) custom-call(bf16[4,32,1024]{2,1,0:T(8,128)(2,1)S(1)} %shard_map.63.mine_ref.refs_2_, bf16[4,32,1024]{2,1,0:T(8,128)(2,1)S(1)} %collective-permute-done.12.other_ref, ...), custom_call_target="tpu_custom_call" | custom-call | flops 2147483648 | bytes 262144 | tf_op jit(solution)/shard_map/pallas_call | solution.py:50
  51.4 1.6 %collective-permute-start.16 = (bf16[2,24,2048]{2,1,0:T(8,128)(2,1)S(1)}, bf16[2,24,2048]{2,1,0:T(8,128)(2,1)S(1)}, u32[]{:S(2)}, u32[]{:S(2)}) collective-permute-start(bf16[2,24,2048]{2,1,0:T(8,128)(2,1)S(1)} %get-tuple-element.65), channel_id=1, source_target_pairs={{0,16},{1,9},{2,18},{3,11},{4,20},{5,13},{6,22},{7,15},{8,24},{9,1... | collective-permute-start | bytes 589832 | tf_op jit(solution)/shard_map/ppermute | solution.py:46
  53.0 2.5 %collective-permute-done.14.refs_3_ = bf16[2,24,2048]{2,1,0:T(8,128)(2,1)S(1)} collective-permute-done((bf16[2,24,2048]{2,1,0:T(8,128)(2,1)S(1)}, bf16[2,24,2048]{2,1,0:T(8,128)(2,1)S(1)}, u32[]{:S(2)}, u32[]{:S(2)}) %collective-permute-start.14) | collective-permute-done | bytes 196640 | tf_op jit(solution)/shard_map/ppermute | solution.py:46
  60.8 2.6 %collective-permute-done.17.last_got_ref = bf16[24,2048]{1,0:T(8,128)(2,1)S(1)} collective-permute-done((bf16[24,2048]{1,0:T(8,128)(2,1)S(1)}, bf16[24,2048]{1,0:T(8,128)(2,1)S(1)}, u32[]{:S(2)}, u32[]{:S(2)}) %collective-permute-start.17) | collective-permute-done | bytes 98336 | tf_op jit(solution)/shard_map/ppermute | solution.py:46
  (33 shorter events, 10.5 us)
Async XLA Ops:
  0.6 9.1 %collective-permute-start = (bf16[24,8192]{1,0:T(8,128)(2,1)}, bf16[24,8192]{1,0:T(8,128)(2,1)S(1)}, u32[]{:S(2)}, u32[]{:S(2)}) collective-permute-start(bf16[24,8192]{1,0:T(8,128)(2,1)} %g_ref.1), channel_id=1, source_target_pairs={{0,8},{1,17},{2,10},{3,19},{4,12},{5,21},{6,14},{7,23},{8,0},{9,25... | collective-permute-start | bytes 1179656 | tf_op jit(solution)/shard_map/ppermute | solution.py:46
  7.3 11.9 %collective-permute-start.1 = (bf16[24,8192]{1,0:T(8,128)(2,1)S(1)}, bf16[24,8192]{1,0:T(8,128)(2,1)S(1)}, u32[]{:S(2)}, u32[]{:S(2)}) collective-permute-start(bf16[24,8192]{1,0:T(8,128)(2,1)S(1)} %get-tuple-element.36.refs_0_), channel_id=1, source_target_pairs={{0,16},{1,9},{2,18},{3,11},{4,20},{5,13},{6,22},{7,15},{8,24},{9,1... | collective-permute-start | bytes 1179656 | tf_op jit(solution)/shard_map/ppermute | solution.py:46
  9.7 9.7 %collective-permute-start.2 = (bf16[24,8192]{1,0:T(8,128)(2,1)S(1)}, bf16[24,8192]{1,0:T(8,128)(2,1)S(1)}, u32[]{:S(2)}, u32[]{:S(2)}) collective-permute-start(bf16[24,8192]{1,0:T(8,128)(2,1)S(1)} %collective-permute-done.refs_1_), channel_id=1, source_target_pairs={{0,16},{1,9},{2,18},{3,11},{4,20},{5,13},{6,22},{7,15},{8,24},{9,1... | collective-permute-start | bytes 1179656 | tf_op jit(solution)/shard_map/ppermute | solution.py:46
  23.7 1.5 %collective-permute-start.3 = (bf16[4,24,1024]{2,1,0:T(8,128)(2,1)S(1)}, bf16[4,24,1024]{2,1,0:T(8,128)(2,1)S(1)}, u32[]{:S(2)}, u32[]{:S(2)}) collective-permute-start(bf16[4,24,1024]{2,1,0:T(8,128)(2,1)S(1)} %get-tuple-element.48), channel_id=1, source_target_pairs={{0,1},{1,0},{2,3},{3,2},{4,5},{5,4},{6,7},{7,6},{8,9},{9,8},{10,11... | collective-permute-start | bytes 589832 | tf_op jit(solution)/shard_map/ppermute | solution.py:38
  25.3 8.1 %collective-permute-start.4 = (bf16[24,1024]{1,0:T(8,128)(2,1)S(1)}, bf16[24,1024]{1,0:T(8,128)(2,1)S(1)}, u32[]{:S(2)}, u32[]{:S(2)}) collective-permute-start(bf16[24,1024]{1,0:T(8,128)(2,1)S(1)} %get-tuple-element.50), channel_id=1, source_target_pairs={{0,4},{1,5},{2,6},{3,7},{4,0},{5,1},{6,2},{7,3},{8,12},{9,13},{10,... | collective-permute-start | bytes 147464 | tf_op jit(solution)/shard_map/ppermute | solution.py:38
  27.9 6.2 %collective-permute-start.5 = (bf16[24,1024]{1,0:T(8,128)(2,1)S(1)}, bf16[24,1024]{1,0:T(8,128)(2,1)S(1)}, u32[]{:S(2)}, u32[]{:S(2)}) collective-permute-start(bf16[24,1024]{1,0:T(8,128)(2,1)S(1)} %get-tuple-element.51), channel_id=1, source_target_pairs={{0,6},{1,7},{2,4},{3,5},{4,2},{5,3},{6,0},{7,1},{8,14},{9,15},{10,... | collective-permute-start | bytes 147464 | tf_op jit(solution)/shard_map/ppermute | solution.py:38
  29.3 4.9 %collective-permute-start.6 = (bf16[24,1024]{1,0:T(8,128)(2,1)S(1)}, bf16[24,1024]{1,0:T(8,128)(2,1)S(1)}, u32[]{:S(2)}, u32[]{:S(2)}) collective-permute-start(bf16[24,1024]{1,0:T(8,128)(2,1)S(1)} %get-tuple-element.52), channel_id=1, source_target_pairs={{0,2},{1,3},{2,0},{3,1},{4,6},{5,7},{6,4},{7,5},{8,10},{9,11},{10,... | collective-permute-start | bytes 147464 | tf_op jit(solution)/shard_map/ppermute | solution.py:38
  29.5 3.9 %collective-permute-start.7 = (bf16[12,1024]{1,0:T(8,128)(2,1)S(1)}, bf16[12,1024]{1,0:T(8,128)(2,1)S(1)}, u32[]{:S(2)}, u32[]{:S(2)}) collective-permute-start(bf16[12,1024]{1,0:T(8,128)(2,1)S(1)} %get-tuple-element.53), channel_id=1, source_target_pairs={{0,1},{1,0},{2,3},{3,2},{4,5},{5,4},{6,7},{7,6},{8,9},{9,8},{10,11... | collective-permute-start | bytes 73736 | tf_op jit(solution)/shard_map/ppermute | solution.py:38
  34.3 8.3 %collective-permute-start.11 = (bf16[24,1024]{1,0:T(8,128)(2,1)S(1)}, bf16[24,1024]{1,0:T(8,128)(2,1)S(1)}, u32[]{:S(2)}, u32[]{:S(2)}) collective-permute-start(bf16[24,1024]{1,0:T(8,128)(2,1)S(1)} %get-tuple-element.56.refs_0_), channel_id=1, source_target_pairs={{0,6},{1,7},{2,4},{3,5},{4,2},{5,3},{6,0},{7,1},{8,14},{9,15},{10,... | collective-permute-start | bytes 147464 | tf_op jit(solution)/shard_map/ppermute | solution.py:38
  37.1 5.5 %collective-permute-start.10 = (bf16[24,1024]{1,0:T(8,128)(2,1)S(1)}, bf16[24,1024]{1,0:T(8,128)(2,1)S(1)}, u32[]{:S(2)}, u32[]{:S(2)}) collective-permute-start(bf16[24,1024]{1,0:T(8,128)(2,1)S(1)} %get-tuple-element.56.refs_0_), channel_id=1, source_target_pairs={{0,4},{1,5},{2,6},{3,7},{4,0},{5,1},{6,2},{7,3},{8,12},{9,13},{10,... | collective-permute-start | bytes 147464 | tf_op jit(solution)/shard_map/ppermute | solution.py:38
  37.1 5.5 %collective-permute-start.9 = (bf16[24,1024]{1,0:T(8,128)(2,1)S(1)}, bf16[24,1024]{1,0:T(8,128)(2,1)S(1)}, u32[]{:S(2)}, u32[]{:S(2)}) collective-permute-start(bf16[24,1024]{1,0:T(8,128)(2,1)S(1)} %get-tuple-element.56.refs_0_), channel_id=1, source_target_pairs={{0,2},{1,3},{2,0},{3,1},{4,6},{5,7},{6,4},{7,5},{8,10},{9,11},{10,... | collective-permute-start | bytes 147464 | tf_op jit(solution)/shard_map/ppermute | solution.py:38
  42.7 1.6 %collective-permute-start.12 = (bf16[4,32,1024]{2,1,0:T(8,128)(2,1)S(1)}, bf16[4,32,1024]{2,1,0:T(8,128)(2,1)S(1)}, u32[]{:S(2)}, u32[]{:S(2)}) collective-permute-start(bf16[4,32,1024]{2,1,0:T(8,128)(2,1)S(1)} %shard_map.63.mine_ref.refs_2_), channel_id=1, source_target_pairs={{0,1},{1,0},{2,3},{3,2},{4,5},{5,4},{6,7},{7,6},{8,9},{9,8},{10,11... | collective-permute-start | bytes 786440 | tf_op jit(solution)/shard_map/ppermute | solution.py:38
  45.5 10.0 %collective-permute-start.13 = (bf16[2,24,4096]{2,1,0:T(8,128)(2,1)S(1)}, bf16[2,24,4096]{2,1,0:T(8,128)(2,1)S(1)}, u32[]{:S(2)}, u32[]{:S(2)}) collective-permute-start(bf16[2,24,4096]{2,1,0:T(8,128)(2,1)S(1)} %get-tuple-element.57), channel_id=1, source_target_pairs={{0,16},{1,9},{2,18},{3,11},{4,20},{5,13},{6,22},{7,15},{8,24},{9,1... | collective-permute-start | bytes 1179656 | tf_op jit(solution)/shard_map/ppermute | solution.py:46
  48.4 7.1 %collective-permute-start.14 = (bf16[2,24,2048]{2,1,0:T(8,128)(2,1)S(1)}, bf16[2,24,2048]{2,1,0:T(8,128)(2,1)S(1)}, u32[]{:S(2)}, u32[]{:S(2)}) collective-permute-start(bf16[2,24,2048]{2,1,0:T(8,128)(2,1)S(1)} %get-tuple-element.60), channel_id=1, source_target_pairs={{0,16},{1,9},{2,18},{3,11},{4,20},{5,13},{6,22},{7,15},{8,24},{9,1... | collective-permute-start | bytes 589832 | tf_op jit(solution)/shard_map/ppermute | solution.py:46
  51.4 6.2 %collective-permute-start.16 = (bf16[2,24,2048]{2,1,0:T(8,128)(2,1)S(1)}, bf16[2,24,2048]{2,1,0:T(8,128)(2,1)S(1)}, u32[]{:S(2)}, u32[]{:S(2)}) collective-permute-start(bf16[2,24,2048]{2,1,0:T(8,128)(2,1)S(1)} %get-tuple-element.65), channel_id=1, source_target_pairs={{0,16},{1,9},{2,18},{3,11},{4,20},{5,13},{6,22},{7,15},{8,24},{9,1... | collective-permute-start | bytes 589832 | tf_op jit(solution)/shard_map/ppermute | solution.py:46
  55.6 7.8 %collective-permute-start.15 = (bf16[24,6144]{1,0:T(8,128)(2,1)S(1)}, bf16[24,6144]{1,0:T(8,128)(2,1)S(1)}, u32[]{:S(2)}, u32[]{:S(2)}) collective-permute-start(bf16[24,6144]{1,0:T(8,128)(2,1)S(1)} %get-tuple-element.64), channel_id=1, source_target_pairs={{0,8},{1,17},{2,10},{3,19},{4,12},{5,21},{6,14},{7,23},{8,0},{9,25... | collective-permute-start | bytes 884744 | tf_op jit(solution)/shard_map/ppermute | solution.py:46
  57.6 5.8 %collective-permute-start.17 = (bf16[24,2048]{1,0:T(8,128)(2,1)S(1)}, bf16[24,2048]{1,0:T(8,128)(2,1)S(1)}, u32[]{:S(2)}, u32[]{:S(2)}) collective-permute-start(bf16[24,2048]{1,0:T(8,128)(2,1)S(1)} %get-tuple-element.69), channel_id=1, source_target_pairs={{0,8},{1,17},{2,10},{3,19},{4,12},{5,21},{6,14},{7,23},{8,0},{9,25... | collective-permute-start | bytes 294920 | tf_op jit(solution)/shard_map/ppermute | solution.py:46
  58.9 1.3 %collective-permute-start.8 = (f32[12,1024]{1,0:T(8,128)S(1)}, f32[12,1024]{1,0:T(8,128)S(1)}, u32[]{:S(2)}, u32[]{:S(2)}) collective-permute-start(f32[12,1024]{1,0:T(8,128)S(1)} %get-tuple-element.55), channel_id=1, source_target_pairs={{0,1},{1,0},{2,3},{3,2},{4,5},{5,4},{6,7},{7,6},{8,9},{9,8},{10,11... | collective-permute-start | bytes 147464 | tf_op jit(solution)/shard_map/ppermute | solution.py:38

commit v5 on v4

--- a/solution.py
+++ b/solution.py
@@ -285,7 +285,7 @@
         keep, *sums, aux_kept, aux_got, turned[-1],
         ins=[VMEM] * 6 + [HBM],
     )
-    for k in range(3, 6):
+    for k in range(3, 5):
         turned.append(transposed(pieces[k], shifted if k == 3 else turned[-1], *pieces[k + 1 :]))
     blocks = [shifted] + [swap(shifted, "grp", 2 * t) for t in (1, 2, 3)]
     bias_got = swap(give, "grp", 1)
@@ -309,7 +309,11 @@
             all_ref[p * PAD : (p + 1) * PAD, pl.ds(start, half)] = ref[role(p, core)]
 
     def tiles(c_refs):
-        return [(c, n, slice(j * rows + n, j * rows + n + tile)) for j, c in enumerate(c_refs) for n in range(0, rows, tile)]
+        return [
+            (c, n, slice(j * rows + n, j * rows + n + tile))
+            for j, c in enumerate(c_refs)
+            for n in range(0, rows, tile)
+        ]
 
     def stored(total, at, s_ref, pass_ref, own_ref):
         block = [total[p * PAD : p * PAD + wb] for p in range(4)]
@@ -341,7 +345,7 @@
         placed(all_ref, mine_ref, pl.multiple_of(core * half, half))
         placed(all_ref, other_ref, pl.multiple_of((1 - core) * half, half))
         for c, n, at in tiles(c_refs):
-            if group.start < len(turned):
+            if group.start + at.start // rows < len(turned):
                 total = jnp.dot(all_ref[...], c[:, n : n + tile], preferred_element_type=f32)
             else:
                 total = lax.dot_general(

time: 64.4 us -> 64.1 us (level)
    ppermute x10, waiting for transfers between devices: 2.32 us -> 3.34 us  [swap(): return lax.ppermute(x, axis, [(i, i ^ bit) for i in range(n)])]
    pallas_call x21 -> x20, Pallas kernels: 31 us -> 30.4 us  [call(): pl.pallas_call(body, out_shape=outs, in_specs=ins or [VMEM] * len(args),...]
  transfers between devices with their start and end apart: 18 -> 18, of which waited for: 9 -> 10; matrix products, arithmetic and copies ran while one was open for 0% -> 0% of each run, Pallas kernels for 38% -> 37%
where the time goes in v5:
time: 64.1 us; the launch traced here: 63.9 us
  Pallas kernels  30.4 us (47%)
  starting transfers between devices  23.2 us (36%)
  waiting for transfers between devices  9.52 us (15%)
  between operations  0.82 us (1%)
    pallas_call x20, Pallas kernels, call(): pl.pallas_call(body, out_shape=outs, in_specs=ins or [VMEM] * len(args),...  30.4 us
    ppermute x8, starting transfers between devices, cross(): return lax.ppermute(x, ('blk', 'grp'), pairs)  14.4 us
    ppermute x10, starting transfers between devices, swap(): return lax.ppermute(x, axis, [(i, i ^ bit) for i in range(n)])  8.83 us
    ppermute x8, waiting for transfers between devices, cross(): return lax.ppermute(x, ('blk', 'grp'), pairs)  6.19 us
    ppermute x10, waiting for transfers between devices, swap(): return lax.ppermute(x, axis, [(i, i ^ bit) for i in range(n)])  3.34 us
  transfers between devices with their start and end apart: 18, of which 10 were waited for; matrix products, arithmetic and copies ran while one was open for 0% of the time, Pallas kernels for 37%

profile of v5, /device:TPU:0, one launch (start us, length us, event | category | flops | bytes accessed | tf_op | source)
XLA Modules:
  0.0 63.9 jit_solution(10321279221843812976)
XLA Ops:
  0.6 3.0 %collective-permute-start = (bf16[24,8192]{1,0:T(8,128)(2,1)}, bf16[24,8192]{1,0:T(8,128)(2,1)S(1)}, u32[]{:S(2)}, u32[]{:S(2)}) collective-permute-start(bf16[24,8192]{1,0:T(8,128)(2,1)} %g_ref.1), channel_id=1, source_target_pairs={{0,8},{1,17},{2,10},{3,19},{4,12},{5,21},{6,14},{7,23},{8,0},{9,25... | collective-permute-start | bytes 1179656 | tf_op jit(solution)/shard_map/ppermute | solution.py:46
  3.6 3.7 %shard_map.50 = (bf16[1024,2048]{1,0:T(8,128)(2,1)S(1)}, bf16[1024,2048]{1,0:T(8,128)(2,1)S(1)}, bf16[12,1024]{1,0:T(8,128)(2,1)S(1)}, bf16[12,1024]{1,0:T(8,128)(2,1)S(1)}, bf16[24,8192]{1,0:T(8,128)(2,1)S(1)}) custom-call(bf16[8192,2048]{1,0:T(8,128)(2,1)} %refs_10_.1, bf16[12,2048]{1,0:T(8,128)(2,1)} %aux_ref.1, bf16[24,8192]{1,0:T(8,128)(2,1)} %g_ref.1), custom_call_target="tpu_custom_call" | custom-call | flops 4000000000 | bytes 262144 | tf_op jit(solution)/shard_map/pallas_call | solution.py:50
  7.3 1.6 %collective-permute-start.1 = (bf16[24,8192]{1,0:T(8,128)(2,1)S(1)}, bf16[24,8192]{1,0:T(8,128)(2,1)S(1)}, u32[]{:S(2)}, u32[]{:S(2)}) collective-permute-start(bf16[24,8192]{1,0:T(8,128)(2,1)S(1)} %get-tuple-element.36.refs_0_), channel_id=1, source_target_pairs={{0,16},{1,9},{2,18},{3,11},{4,20},{5,13},{6,22},{7,15},{8,24},{9,1... | collective-permute-start | bytes 1179656 | tf_op jit(solution)/shard_map/ppermute | solution.py:46
  9.7 3.6 %collective-permute-start.2 = (bf16[24,8192]{1,0:T(8,128)(2,1)S(1)}, bf16[24,8192]{1,0:T(8,128)(2,1)S(1)}, u32[]{:S(2)}, u32[]{:S(2)}) collective-permute-start(bf16[24,8192]{1,0:T(8,128)(2,1)S(1)} %collective-permute-done.refs_1_), channel_id=1, source_target_pairs={{0,16},{1,9},{2,18},{3,11},{4,20},{5,13},{6,22},{7,15},{8,24},{9,1... | collective-permute-start | bytes 1179656 | tf_op jit(solution)/shard_map/ppermute | solution.py:46
  13.3 5.9 %shard_map.51 = (bf16[1024,2048]{1,0:T(8,128)(2,1)S(1)}, bf16[1024,2048]{1,0:T(8,128)(2,1)S(1)}, bf16[1024,2048]{1,0:T(8,128)(2,1)S(1)}, bf16[1024,2048]{1,0:T(8,128)(2,1)S(1)}) custom-call(bf16[8192,2048]{1,0:T(8,128)(2,1)} %refs_10_.1, bf16[12,1024]{1,0:T(8,128)(2,1)S(1)} %get-tuple-element.39._.aux_ref), custom_call_target="tpu_custom_call" | custom-call | flops 8000000000 | bytes 262144 | tf_op jit(solution)/shard_map/pallas_call | solution.py:50
  19.4 4.3 %shard_map.52 = (bf16[128,8192]{1,0:T(8,128)(2,1)S(1)}, bf16[4,24,1024]{2,1,0:T(8,128)(2,1)S(1)}, f32[128,1024]{1,0:T(8,128)S(1)}, bf16[1024,2048]{1,0:T(8,128)(2,1)S(1)}, bf16[1024,2048]{1,0:T(8,128)(2,1)S(1)}) custom-call(bf16[24,8192]{1,0:T(8,128)(2,1)S(1)} %get-tuple-element.36.refs_0_, bf16[24,8192]{1,0:T(8,128)(2,1)S(1)} %collective-permute-done.refs_1_, ...), custom_call_target="tpu_custom_call" | custom-call | flops 2147483648 | bytes 262144 | tf_op jit(solution)/shard_map/pallas_call | solution.py:50
  23.8 1.4 %shard_map.53.mine_ref = f32[4,24,1024]{2,1,0:T(8,128)S(1)} custom-call(bf16[128,8192]{1,0:T(8,128)(2,1)S(1)} %get-tuple-element.44.all_ref, f32[128,1024]{1,0:T(8,128)S(1)} %get-tuple-element.45.part_ref, bf16[1024,2048]{1,0:T(8,128)(2,1)S(1)} %get-tuple-element.42.refs_8_.refs_0_.refs_4_.refs_3_.refs_2_.refs_1_.c, ...), custom_call_target="tpu_custom_call" | custom-call | flops 2147483648 | bytes 262144 | tf_op jit(solution)/shard_map/pallas_call | solution.py:50
  25.3 2.7 %collective-permute-start.4 = (bf16[24,1024]{1,0:T(8,128)(2,1)S(1)}, bf16[24,1024]{1,0:T(8,128)(2,1)S(1)}, u32[]{:S(2)}, u32[]{:S(2)}) collective-permute-start(bf16[24,1024]{1,0:T(8,128)(2,1)S(1)} %get-tuple-element.50), channel_id=1, source_target_pairs={{0,4},{1,5},{2,6},{3,7},{4,0},{5,1},{6,2},{7,3},{8,12},{9,13},{10,... | collective-permute-start | bytes 147464 | tf_op jit(solution)/shard_map/ppermute | solution.py:38
  27.9 1.3 %collective-permute-start.5 = (bf16[24,1024]{1,0:T(8,128)(2,1)S(1)}, bf16[24,1024]{1,0:T(8,128)(2,1)S(1)}, u32[]{:S(2)}, u32[]{:S(2)}) collective-permute-start(bf16[24,1024]{1,0:T(8,128)(2,1)S(1)} %get-tuple-element.51), channel_id=1, source_target_pairs={{0,6},{1,7},{2,4},{3,5},{4,2},{5,3},{6,0},{7,1},{8,14},{9,15},{10,... | collective-permute-start | bytes 147464 | tf_op jit(solution)/shard_map/ppermute | solution.py:38
  29.5 1.3 %shard_map.55.refs_0_ = bf16[2048,1024]{1,0:T(8,128)(2,1)S(1)} custom-call(bf16[1024,2048]{1,0:T(8,128)(2,1)S(1)} %get-tuple-element.37.refs_4_.c, f32[24,1024]{1,0:T(8,128)S(1)} %get-tuple-element.49.refs_0_.keep_ref, bf16[1024,2048]{1,0:T(8,128)(2,1)S(1)} %get-tuple-element.38.refs_5_.refs_1_.c, ...), custom_call_target="tpu_custom_call" | custom-call | bytes 262144 | tf_op jit(solution)/shard_map/pallas_call | solution.py:50
  30.8 1.3 %shard_map.56.refs_0_.refs_1_ = bf16[2048,1024]{1,0:T(8,128)(2,1)S(1)} custom-call(bf16[1024,2048]{1,0:T(8,128)(2,1)S(1)} %get-tuple-element.38.refs_5_.refs_1_.c, bf16[2048,1024]{1,0:T(8,128)(2,1)S(1)} %shard_map.55.refs_0_, bf16[1024,2048]{1,0:T(8,128)(2,1)S(1)} %get-tuple-element.40.refs_6_.refs_2_.refs_1_.c, ...), custom_call_target="tpu_custom_call" | custom-call | bytes 262144 | tf_op jit(solution)/shard_map/pallas_call | solution.py:50
  32.1 1.3 %shard_map.57._.refs_2_ = bf16[2048,1024]{1,0:T(8,128)(2,1)S(1)} custom-call(bf16[1024,2048]{1,0:T(8,128)(2,1)S(1)} %get-tuple-element.40.refs_6_.refs_2_.refs_1_.c, bf16[2048,1024]{1,0:T(8,128)(2,1)S(1)} %shard_map.56.refs_0_.refs_1_, bf16[1024,2048]{1,0:T(8,128)(2,1)S(1)} %get-tuple-element.41.refs_7_.refs_3_.refs_2_.refs_1_.c, ...), custom_call_target="tpu_custom_call" | custom-call | bytes 262144 | tf_op jit(solution)/shard_map/pallas_call | solution.py:50
  34.3 2.9 %collective-permute-start.11 = (bf16[24,1024]{1,0:T(8,128)(2,1)S(1)}, bf16[24,1024]{1,0:T(8,128)(2,1)S(1)}, u32[]{:S(2)}, u32[]{:S(2)}) collective-permute-start(bf16[24,1024]{1,0:T(8,128)(2,1)S(1)} %get-tuple-element.56.refs_0_), channel_id=1, source_target_pairs={{0,6},{1,7},{2,4},{3,5},{4,2},{5,3},{6,0},{7,1},{8,14},{9,15},{10,... | collective-permute-start | bytes 147464 | tf_op jit(solution)/shard_map/ppermute | solution.py:38
  37.1 1.6 %collective-permute-start.9 = (bf16[24,1024]{1,0:T(8,128)(2,1)S(1)}, bf16[24,1024]{1,0:T(8,128)(2,1)S(1)}, u32[]{:S(2)}, u32[]{:S(2)}) collective-permute-start(bf16[24,1024]{1,0:T(8,128)(2,1)S(1)} %get-tuple-element.56.refs_0_), channel_id=1, source_target_pairs={{0,2},{1,3},{2,0},{3,1},{4,6},{5,7},{6,4},{7,5},{8,10},{9,11},{10,... | collective-permute-start | bytes 147464 | tf_op jit(solution)/shard_map/ppermute | solution.py:38
  38.7 1.3 %shard_map.60.refs_0_.refs_3_ = bf16[2048,1024]{1,0:T(8,128)(2,1)S(1)} custom-call(bf16[1024,2048]{1,0:T(8,128)(2,1)S(1)} %get-tuple-element.41.refs_7_.refs_3_.refs_2_.refs_1_.c, bf16[24,1024]{1,0:T(8,128)(2,1)S(1)} %get-tuple-element.56.refs_0_, bf16[1024,2048]{1,0:T(8,128)(2,1)S(1)} %get-tuple-element.42.refs_8_.refs_0_.refs_4_.refs_3_.refs_2_.refs_1_.c, ...), custom_call_target="tpu_custom_call" | custom-call | bytes 262144 | tf_op jit(solution)/shard_map/pallas_call | solution.py:50
  40.0 1.3 %shard_map.61.refs_4_.refs_0_ = bf16[2048,1024]{1,0:T(8,128)(2,1)S(1)} custom-call(bf16[1024,2048]{1,0:T(8,128)(2,1)S(1)} %get-tuple-element.42.refs_8_.refs_0_.refs_4_.refs_3_.refs_2_.refs_1_.c, bf16[2048,1024]{1,0:T(8,128)(2,1)S(1)} %shard_map.60.refs_0_.refs_3_, bf16[1024,2048]{1,0:T(8,128)(2,1)S(1)} %get-tuple-element.43.refs_9_.refs_1_.refs_5_.refs_4_.refs_3_.refs_2_, ...), custom_call_target="tpu_custom_call" | custom-call | bytes 262144 | tf_op jit(solution)/shard_map/pallas_call | solution.py:50
  42.4 1.3 %shard_map.63.part_ref = f32[128,4096]{1,0:T(8,128)S(1)} custom-call(bf16[4,32,1024]{2,1,0:T(8,128)(2,1)S(1)} %shard_map.62.mine_ref.refs_2_, bf16[2048,1024]{1,0:T(8,128)(2,1)S(1)} %shard_map.55.refs_0_, bf16[2048,1024]{1,0:T(8,128)(2,1)S(1)} %shard_map.56.refs_0_.refs_1_, bf16[2048,1024]{1,0:T(8,128)(2,1)S(1)} %shard_map.57._.refs_2_, ...), custom_call_target="tpu_custom_call" | custom-call | bytes 262144 | tf_op jit(solution)/shard_map/pallas_call | solution.py:50
  44.0 1.3 %shard_map.64 = (bf16[2,24,4096]{2,1,0:T(8,128)(2,1)S(1)}, f32[24,4096]{1,0:T(8,128)S(1)}, f32[24,4096]{1,0:T(8,128)S(1)}) custom-call(bf16[4,32,1024]{2,1,0:T(8,128)(2,1)S(1)} %collective-permute-done.12.other_ref, f32[128,4096]{1,0:T(8,128)S(1)} %shard_map.63.part_ref, bf16[2048,1024]{1,0:T(8,128)(2,1)S(1)} %shard_map.55.refs_0_, ...), custom_call_target="tpu_custom_call" | custom-call | flops 2147483648 | bytes 262144 | tf_op jit(solution)/shard_map/pallas_call | solution.py:50
  45.2 1.6 %collective-permute-start.13 = (bf16[2,24,4096]{2,1,0:T(8,128)(2,1)S(1)}, bf16[2,24,4096]{2,1,0:T(8,128)(2,1)S(1)}, u32[]{:S(2)}, u32[]{:S(2)}) collective-permute-start(bf16[2,24,4096]{2,1,0:T(8,128)(2,1)S(1)} %get-tuple-element.57), channel_id=1, source_target_pairs={{0,16},{1,9},{2,18},{3,11},{4,20},{5,13},{6,22},{7,15},{8,24},{9,1... | collective-permute-start | bytes 1179656 | tf_op jit(solution)/shard_map/ppermute | solution.py:46
  46.8 1.9 %shard_map.65 = (bf16[2,24,2048]{2,1,0:T(8,128)(2,1)S(1)}, f32[24,2048]{1,0:T(8,128)S(1)}, f32[24,2048]{1,0:T(8,128)S(1)}) custom-call(bf16[4,32,1024]{2,1,0:T(8,128)(2,1)S(1)} %shard_map.62.mine_ref.refs_2_, bf16[4,32,1024]{2,1,0:T(8,128)(2,1)S(1)} %collective-permute-done.12.other_ref, bf16[2048,1024]{1,0:T(8,128)(2,1)S(1)} %shard_map.61.refs_4_.refs_0_, ...), custom_call_target="tpu_custom_call" | custom-call | flops 2147483648 | bytes 262144 | tf_op jit(solution)/shard_map/pallas_call | solution.py:50
  49.3 2.5 %shard_map.67 = (bf16[2,24,2048]{2,1,0:T(8,128)(2,1)S(1)}, f32[24,2048]{1,0:T(8,128)S(1)}, f32[24,2048]{1,0:T(8,128)S(1)}) custom-call(bf16[4,32,1024]{2,1,0:T(8,128)(2,1)S(1)} %shard_map.62.mine_ref.refs_2_, bf16[4,32,1024]{2,1,0:T(8,128)(2,1)S(1)} %collective-permute-done.12.other_ref, ...), custom_call_target="tpu_custom_call" | custom-call | flops 2147483648 | bytes 262144 | tf_op jit(solution)/shard_map/pallas_call | solution.py:50
  51.8 1.6 %collective-permute-start.16 = (bf16[2,24,2048]{2,1,0:T(8,128)(2,1)S(1)}, bf16[2,24,2048]{2,1,0:T(8,128)(2,1)S(1)}, u32[]{:S(2)}, u32[]{:S(2)}) collective-permute-start(bf16[2,24,2048]{2,1,0:T(8,128)(2,1)S(1)} %get-tuple-element.65), channel_id=1, source_target_pairs={{0,16},{1,9},{2,18},{3,11},{4,20},{5,13},{6,22},{7,15},{8,24},{9,1... | collective-permute-start | bytes 589832 | tf_op jit(solution)/shard_map/ppermute | solution.py:46
  53.4 1.8 %collective-permute-done.14.refs_3_ = bf16[2,24,2048]{2,1,0:T(8,128)(2,1)S(1)} collective-permute-done((bf16[2,24,2048]{2,1,0:T(8,128)(2,1)S(1)}, bf16[2,24,2048]{2,1,0:T(8,128)(2,1)S(1)}, u32[]{:S(2)}, u32[]{:S(2)}) %collective-permute-start.14) | collective-permute-done | bytes 196640 | tf_op jit(solution)/shard_map/ppermute | solution.py:46
  60.7 2.4 %collective-permute-done.17.last_got_ref = bf16[24,2048]{1,0:T(8,128)(2,1)S(1)} collective-permute-done((bf16[24,2048]{1,0:T(8,128)(2,1)S(1)}, bf16[24,2048]{1,0:T(8,128)(2,1)S(1)}, u32[]{:S(2)}, u32[]{:S(2)}) %collective-permute-start.17) | collective-permute-done | bytes 98336 | tf_op jit(solution)/shard_map/ppermute | solution.py:46
  (32 shorter events, 10.4 us)
Async XLA Ops:
  0.6 9.1 %collective-permute-start = (bf16[24,8192]{1,0:T(8,128)(2,1)}, bf16[24,8192]{1,0:T(8,128)(2,1)S(1)}, u32[]{:S(2)}, u32[]{:S(2)}) collective-permute-start(bf16[24,8192]{1,0:T(8,128)(2,1)} %g_ref.1), channel_id=1, source_target_pairs={{0,8},{1,17},{2,10},{3,19},{4,12},{5,21},{6,14},{7,23},{8,0},{9,25... | collective-permute-start | bytes 1179656 | tf_op jit(solution)/shard_map/ppermute | solution.py:46
  7.3 11.9 %collective-permute-start.1 = (bf16[24,8192]{1,0:T(8,128)(2,1)S(1)}, bf16[24,8192]{1,0:T(8,128)(2,1)S(1)}, u32[]{:S(2)}, u32[]{:S(2)}) collective-permute-start(bf16[24,8192]{1,0:T(8,128)(2,1)S(1)} %get-tuple-element.36.refs_0_), channel_id=1, source_target_pairs={{0,16},{1,9},{2,18},{3,11},{4,20},{5,13},{6,22},{7,15},{8,24},{9,1... | collective-permute-start | bytes 1179656 | tf_op jit(solution)/shard_map/ppermute | solution.py:46
  9.7 9.7 %collective-permute-start.2 = (bf16[24,8192]{1,0:T(8,128)(2,1)S(1)}, bf16[24,8192]{1,0:T(8,128)(2,1)S(1)}, u32[]{:S(2)}, u32[]{:S(2)}) collective-permute-start(bf16[24,8192]{1,0:T(8,128)(2,1)S(1)} %collective-permute-done.refs_1_), channel_id=1, source_target_pairs={{0,16},{1,9},{2,18},{3,11},{4,20},{5,13},{6,22},{7,15},{8,24},{9,1... | collective-permute-start | bytes 1179656 | tf_op jit(solution)/shard_map/ppermute | solution.py:46
  23.7 1.5 %collective-permute-start.3 = (bf16[4,24,1024]{2,1,0:T(8,128)(2,1)S(1)}, bf16[4,24,1024]{2,1,0:T(8,128)(2,1)S(1)}, u32[]{:S(2)}, u32[]{:S(2)}) collective-permute-start(bf16[4,24,1024]{2,1,0:T(8,128)(2,1)S(1)} %get-tuple-element.48), channel_id=1, source_target_pairs={{0,1},{1,0},{2,3},{3,2},{4,5},{5,4},{6,7},{7,6},{8,9},{9,8},{10,11... | collective-permute-start | bytes 589832 | tf_op jit(solution)/shard_map/ppermute | solution.py:38
  25.3 8.1 %collective-permute-start.4 = (bf16[24,1024]{1,0:T(8,128)(2,1)S(1)}, bf16[24,1024]{1,0:T(8,128)(2,1)S(1)}, u32[]{:S(2)}, u32[]{:S(2)}) collective-permute-start(bf16[24,1024]{1,0:T(8,128)(2,1)S(1)} %get-tuple-element.50), channel_id=1, source_target_pairs={{0,4},{1,5},{2,6},{3,7},{4,0},{5,1},{6,2},{7,3},{8,12},{9,13},{10,... | collective-permute-start | bytes 147464 | tf_op jit(solution)/shard_map/ppermute | solution.py:38
  27.9 6.2 %collective-permute-start.5 = (bf16[24,1024]{1,0:T(8,128)(2,1)S(1)}, bf16[24,1024]{1,0:T(8,128)(2,1)S(1)}, u32[]{:S(2)}, u32[]{:S(2)}) collective-permute-start(bf16[24,1024]{1,0:T(8,128)(2,1)S(1)} %get-tuple-element.51), channel_id=1, source_target_pairs={{0,6},{1,7},{2,4},{3,5},{4,2},{5,3},{6,0},{7,1},{8,14},{9,15},{10,... | collective-permute-start | bytes 147464 | tf_op jit(solution)/shard_map/ppermute | solution.py:38
  29.3 4.9 %collective-permute-start.6 = (bf16[24,1024]{1,0:T(8,128)(2,1)S(1)}, bf16[24,1024]{1,0:T(8,128)(2,1)S(1)}, u32[]{:S(2)}, u32[]{:S(2)}) collective-permute-start(bf16[24,1024]{1,0:T(8,128)(2,1)S(1)} %get-tuple-element.52), channel_id=1, source_target_pairs={{0,2},{1,3},{2,0},{3,1},{4,6},{5,7},{6,4},{7,5},{8,10},{9,11},{10,... | collective-permute-start | bytes 147464 | tf_op jit(solution)/shard_map/ppermute | solution.py:38
  29.5 3.9 %collective-permute-start.7 = (bf16[12,1024]{1,0:T(8,128)(2,1)S(1)}, bf16[12,1024]{1,0:T(8,128)(2,1)S(1)}, u32[]{:S(2)}, u32[]{:S(2)}) collective-permute-start(bf16[12,1024]{1,0:T(8,128)(2,1)S(1)} %get-tuple-element.53), channel_id=1, source_target_pairs={{0,1},{1,0},{2,3},{3,2},{4,5},{5,4},{6,7},{7,6},{8,9},{9,8},{10,11... | collective-permute-start | bytes 73736 | tf_op jit(solution)/shard_map/ppermute | solution.py:38
  34.3 7.0 %collective-permute-start.11 = (bf16[24,1024]{1,0:T(8,128)(2,1)S(1)}, bf16[24,1024]{1,0:T(8,128)(2,1)S(1)}, u32[]{:S(2)}, u32[]{:S(2)}) collective-permute-start(bf16[24,1024]{1,0:T(8,128)(2,1)S(1)} %get-tuple-element.56.refs_0_), channel_id=1, source_target_pairs={{0,6},{1,7},{2,4},{3,5},{4,2},{5,3},{6,0},{7,1},{8,14},{9,15},{10,... | collective-permute-start | bytes 147464 | tf_op jit(solution)/shard_map/ppermute | solution.py:38
  37.1 5.2 %collective-permute-start.10 = (bf16[24,1024]{1,0:T(8,128)(2,1)S(1)}, bf16[24,1024]{1,0:T(8,128)(2,1)S(1)}, u32[]{:S(2)}, u32[]{:S(2)}) collective-permute-start(bf16[24,1024]{1,0:T(8,128)(2,1)S(1)} %get-tuple-element.56.refs_0_), channel_id=1, source_target_pairs={{0,4},{1,5},{2,6},{3,7},{4,0},{5,1},{6,2},{7,3},{8,12},{9,13},{10,... | collective-permute-start | bytes 147464 | tf_op jit(solution)/shard_map/ppermute | solution.py:38
  37.1 5.2 %collective-permute-start.9 = (bf16[24,1024]{1,0:T(8,128)(2,1)S(1)}, bf16[24,1024]{1,0:T(8,128)(2,1)S(1)}, u32[]{:S(2)}, u32[]{:S(2)}) collective-permute-start(bf16[24,1024]{1,0:T(8,128)(2,1)S(1)} %get-tuple-element.56.refs_0_), channel_id=1, source_target_pairs={{0,2},{1,3},{2,0},{3,1},{4,6},{5,7},{6,4},{7,5},{8,10},{9,11},{10,... | collective-permute-start | bytes 147464 | tf_op jit(solution)/shard_map/ppermute | solution.py:38
  42.4 1.6 %collective-permute-start.12 = (bf16[4,32,1024]{2,1,0:T(8,128)(2,1)S(1)}, bf16[4,32,1024]{2,1,0:T(8,128)(2,1)S(1)}, u32[]{:S(2)}, u32[]{:S(2)}) collective-permute-start(bf16[4,32,1024]{2,1,0:T(8,128)(2,1)S(1)} %shard_map.62.mine_ref.refs_2_), channel_id=1, source_target_pairs={{0,1},{1,0},{2,3},{3,2},{4,5},{5,4},{6,7},{7,6},{8,9},{9,8},{10,11... | collective-permute-start | bytes 786440 | tf_op jit(solution)/shard_map/ppermute | solution.py:38
  45.2 10.0 %collective-permute-start.13 = (bf16[2,24,4096]{2,1,0:T(8,128)(2,1)S(1)}, bf16[2,24,4096]{2,1,0:T(8,128)(2,1)S(1)}, u32[]{:S(2)}, u32[]{:S(2)}) collective-permute-start(bf16[2,24,4096]{2,1,0:T(8,128)(2,1)S(1)} %get-tuple-element.57), channel_id=1, source_target_pairs={{0,16},{1,9},{2,18},{3,11},{4,20},{5,13},{6,22},{7,15},{8,24},{9,1... | collective-permute-start | bytes 1179656 | tf_op jit(solution)/shard_map/ppermute | solution.py:46
  48.7 6.4 %collective-permute-start.14 = (bf16[2,24,2048]{2,1,0:T(8,128)(2,1)S(1)}, bf16[2,24,2048]{2,1,0:T(8,128)(2,1)S(1)}, u32[]{:S(2)}, u32[]{:S(2)}) collective-permute-start(bf16[2,24,2048]{2,1,0:T(8,128)(2,1)S(1)} %get-tuple-element.60), channel_id=1, source_target_pairs={{0,16},{1,9},{2,18},{3,11},{4,20},{5,13},{6,22},{7,15},{8,24},{9,1... | collective-permute-start | bytes 589832 | tf_op jit(solution)/shard_map/ppermute | solution.py:46
  51.8 5.8 %collective-permute-start.16 = (bf16[2,24,2048]{2,1,0:T(8,128)(2,1)S(1)}, bf16[2,24,2048]{2,1,0:T(8,128)(2,1)S(1)}, u32[]{:S(2)}, u32[]{:S(2)}) collective-permute-start(bf16[2,24,2048]{2,1,0:T(8,128)(2,1)S(1)} %get-tuple-element.65), channel_id=1, source_target_pairs={{0,16},{1,9},{2,18},{3,11},{4,20},{5,13},{6,22},{7,15},{8,24},{9,1... | collective-permute-start | bytes 589832 | tf_op jit(solution)/shard_map/ppermute | solution.py:46
  55.3 7.8 %collective-permute-start.15 = (bf16[24,6144]{1,0:T(8,128)(2,1)S(1)}, bf16[24,6144]{1,0:T(8,128)(2,1)S(1)}, u32[]{:S(2)}, u32[]{:S(2)}) collective-permute-start(bf16[24,6144]{1,0:T(8,128)(2,1)S(1)} %get-tuple-element.64), channel_id=1, source_target_pairs={{0,8},{1,17},{2,10},{3,19},{4,12},{5,21},{6,14},{7,23},{8,0},{9,25... | collective-permute-start | bytes 884744 | tf_op jit(solution)/shard_map/ppermute | solution.py:46
  57.6 5.5 %collective-permute-start.17 = (bf16[24,2048]{1,0:T(8,128)(2,1)S(1)}, bf16[24,2048]{1,0:T(8,128)(2,1)S(1)}, u32[]{:S(2)}, u32[]{:S(2)}) collective-permute-start(bf16[24,2048]{1,0:T(8,128)(2,1)S(1)} %get-tuple-element.69), channel_id=1, source_target_pairs={{0,8},{1,17},{2,10},{3,19},{4,12},{5,21},{6,14},{7,23},{8,0},{9,25... | collective-permute-start | bytes 294920 | tf_op jit(solution)/shard_map/ppermute | solution.py:46
  58.8 1.3 %collective-permute-start.8 = (f32[12,1024]{1,0:T(8,128)S(1)}, f32[12,1024]{1,0:T(8,128)S(1)}, u32[]{:S(2)}, u32[]{:S(2)}) collective-permute-start(f32[12,1024]{1,0:T(8,128)S(1)} %get-tuple-element.55), channel_id=1, source_target_pairs={{0,1},{1,0},{2,3},{3,2},{4,5},{5,4},{6,7},{7,6},{8,9},{9,8},{10,11... | collective-permute-start | bytes 147464 | tf_op jit(solution)/shard_map/ppermute | solution.py:38

commit v6 on v5

--- a/solution.py
+++ b/solution.py
@@ -215,9 +215,13 @@
             for at, total in bias_half(all_ref, c_refs, (1 - core) * half):
                 total_ref[:, at] = total
 
-        for c in copies:
+        for c in copies[:2]:
             c.wait()
-        for at, total in bias_half(all_ref, last_refs, (1 - core) * half, here):
+        for at, total in bias_half(all_ref, last_refs[:1], (1 - core) * half, here):
+            total_ref[:, at] += total
+        for c in copies[2:]:
+            c.wait()
+        for at, total in bias_half(all_ref, last_refs[1:], (1 - core) * half, here + 1):
             total += total_ref[:, at]
             for p in range(4):
                 sent_ref[blk ^ role(p, core), :, at] = total[p * PAD : p * PAD + wb].astype(bf16)
@@ -408,12 +412,25 @@
         )
         done += [mine, cross(sent, 0)]
 
-    def final(mine_ref, got_ref, last_ref, last_got_ref, out_ref):
+    def written(start, mine_ref, got_ref, *refs):
+        out_ref, whole_ref, sem = refs[-3:]
         n = mine_ref.shape[1]
-        out_ref[:, :n] = (mine_ref[...] + got_ref[...].astype(f32)).astype(bf16)
-        out_ref[:, n:] = (last_ref[...] + last_got_ref[...].astype(f32)).astype(bf16)
-
-    result = call(final, struct((wb, depth), bf16), *done)
+        whole_ref[...] = (mine_ref[...] + got_ref[...].astype(f32)).astype(bf16)
+        run([pltpu.make_async_copy(whole_ref, out_ref.at[:, pl.ds(start, n)], sem)])
+
+    def write(start, mine, got, *old):
+        return pl.pallas_call(
+            functools.partial(written, start),
+            out_shape=struct((wb, depth), bf16),
+            in_specs=[VMEM] * 2 + [HBM] * len(old),
+            out_specs=HBM,
+            scratch_shapes=[pltpu.VMEM(mine.shape, bf16), pltpu.SemaphoreType.DMA],
+            input_output_aliases={2: 0} if old else {},
+            compiler_params=pltpu.CompilerParams(vmem_limit_bytes=3 << 20),
+        )(mine, got, *old)
+
+    result = write(0, *done[:2])
+    result = write(done[0].shape[1], *done[2:], result)
 
     def own_bias(bias_ref, got_ref, out_ref):
         _, _, core = ids()

time: 64.1 us -> 64.2 us (level)
  Pallas kernels: 30.4 us -> 31.1 us
  waiting for transfers between devices: 9.52 us -> 8.83 us
    pallas_call x0 -> x2, Pallas kernels: none -> 1.44 us  [write(): pl.pallas_call(functools.partial(written, start), out_shape=struct((wb, d...]
    pallas_call x20 -> x19, Pallas kernels: 30.4 us -> 29.7 us  [call(): pl.pallas_call(body, out_shape=outs, in_specs=ins or [VMEM] * len(args),...]
    ppermute x8, waiting for transfers between devices: 6.19 us -> 5.5 us  [cross(): return lax.ppermute(x, ('blk', 'grp'), pairs)]
  transfers between devices with their start and end apart: 18 -> 18, of which waited for: 10 -> 11; matrix products, arithmetic and copies ran while one was open for 0% -> 0% of each run, Pallas kernels for 37% -> 38%
where the time goes in v6:
time: 64.2 us; the launch traced here: 64.1 us
  Pallas kernels  31.1 us (48%)
  starting transfers between devices  23.1 us (36%)
  waiting for transfers between devices  8.83 us (14%)
  between operations  0.99 us (2%)
    pallas_call x19, Pallas kernels, call(): pl.pallas_call(body, out_shape=outs, in_specs=ins or [VMEM] * len(args),...  29.7 us
    ppermute x8, starting transfers between devices, cross(): return lax.ppermute(x, ('blk', 'grp'), pairs)  14.3 us
    ppermute x10, starting transfers between devices, swap(): return lax.ppermute(x, axis, [(i, i ^ bit) for i in range(n)])  8.84 us
    ppermute x8, waiting for transfers between devices, cross(): return lax.ppermute(x, ('blk', 'grp'), pairs)  5.5 us
    ppermute x10, waiting for transfers between devices, swap(): return lax.ppermute(x, axis, [(i, i ^ bit) for i in range(n)])  3.33 us
    pallas_call x2, Pallas kernels, write(): pl.pallas_call(functools.partial(written, start), out_shape=struct((wb, d...  1.44 us
  transfers between devices with their start and end apart: 18, of which 11 were waited for; matrix products, arithmetic and copies ran while one was open for 0% of the time, Pallas kernels for 38%

profile of v6, /device:TPU:0, one launch (start us, length us, event | category | flops | bytes accessed | tf_op | source)
XLA Modules:
  0.0 64.1 jit_solution(3907126155610929607)
XLA Ops:
  0.6 3.0 %collective-permute-start = (bf16[24,8192]{1,0:T(8,128)(2,1)}, bf16[24,8192]{1,0:T(8,128)(2,1)S(1)}, u32[]{:S(2)}, u32[]{:S(2)}) collective-permute-start(bf16[24,8192]{1,0:T(8,128)(2,1)} %g_ref.1), channel_id=1, source_target_pairs={{0,8},{1,17},{2,10},{3,19},{4,12},{5,21},{6,14},{7,23},{8,0},{9,25... | collective-permute-start | bytes 1179656 | tf_op jit(solution)/shard_map/ppermute | solution.py:46
  3.6 3.7 %shard_map.50 = (bf16[1024,2048]{1,0:T(8,128)(2,1)S(1)}, bf16[1024,2048]{1,0:T(8,128)(2,1)S(1)}, bf16[12,1024]{1,0:T(8,128)(2,1)S(1)}, bf16[12,1024]{1,0:T(8,128)(2,1)S(1)}, bf16[24,8192]{1,0:T(8,128)(2,1)S(1)}) custom-call(bf16[8192,2048]{1,0:T(8,128)(2,1)} %refs_10_.1, bf16[12,2048]{1,0:T(8,128)(2,1)} %aux_ref.1, bf16[24,8192]{1,0:T(8,128)(2,1)} %g_ref.1), custom_call_target="tpu_custom_call" | custom-call | flops 4000000000 | bytes 262144 | tf_op jit(solution)/shard_map/pallas_call | solution.py:50
  7.3 1.6 %collective-permute-start.1 = (bf16[24,8192]{1,0:T(8,128)(2,1)S(1)}, bf16[24,8192]{1,0:T(8,128)(2,1)S(1)}, u32[]{:S(2)}, u32[]{:S(2)}) collective-permute-start(bf16[24,8192]{1,0:T(8,128)(2,1)S(1)} %get-tuple-element.36.refs_0_), channel_id=1, source_target_pairs={{0,16},{1,9},{2,18},{3,11},{4,20},{5,13},{6,22},{7,15},{8,24},{9,1... | collective-permute-start | bytes 1179656 | tf_op jit(solution)/shard_map/ppermute | solution.py:46
  9.7 3.6 %collective-permute-start.2 = (bf16[24,8192]{1,0:T(8,128)(2,1)S(1)}, bf16[24,8192]{1,0:T(8,128)(2,1)S(1)}, u32[]{:S(2)}, u32[]{:S(2)}) collective-permute-start(bf16[24,8192]{1,0:T(8,128)(2,1)S(1)} %collective-permute-done.refs_1_), channel_id=1, source_target_pairs={{0,16},{1,9},{2,18},{3,11},{4,20},{5,13},{6,22},{7,15},{8,24},{9,1... | collective-permute-start | bytes 1179656 | tf_op jit(solution)/shard_map/ppermute | solution.py:46
  13.3 5.9 %shard_map.51 = (bf16[1024,2048]{1,0:T(8,128)(2,1)S(1)}, bf16[1024,2048]{1,0:T(8,128)(2,1)S(1)}, bf16[1024,2048]{1,0:T(8,128)(2,1)S(1)}, bf16[1024,2048]{1,0:T(8,128)(2,1)S(1)}) custom-call(bf16[8192,2048]{1,0:T(8,128)(2,1)} %refs_10_.1, bf16[12,1024]{1,0:T(8,128)(2,1)S(1)} %get-tuple-element.39._.aux_ref), custom_call_target="tpu_custom_call" | custom-call | flops 8000000000 | bytes 262144 | tf_op jit(solution)/shard_map/pallas_call | solution.py:50
  19.4 4.4 %shard_map.52 = (bf16[128,8192]{1,0:T(8,128)(2,1)S(1)}, bf16[4,24,1024]{2,1,0:T(8,128)(2,1)S(1)}, f32[128,1024]{1,0:T(8,128)S(1)}, bf16[1024,2048]{1,0:T(8,128)(2,1)S(1)}, bf16[1024,2048]{1,0:T(8,128)(2,1)S(1)}) custom-call(bf16[24,8192]{1,0:T(8,128)(2,1)S(1)} %get-tuple-element.36.refs_0_, bf16[24,8192]{1,0:T(8,128)(2,1)S(1)} %collective-permute-done.refs_1_, ...), custom_call_target="tpu_custom_call" | custom-call | flops 2147483648 | bytes 262144 | tf_op jit(solution)/shard_map/pallas_call | solution.py:50
  23.9 1.4 %shard_map.53.mine_ref = f32[4,24,1024]{2,1,0:T(8,128)S(1)} custom-call(bf16[128,8192]{1,0:T(8,128)(2,1)S(1)} %get-tuple-element.44.all_ref, f32[128,1024]{1,0:T(8,128)S(1)} %get-tuple-element.45.part_ref, bf16[1024,2048]{1,0:T(8,128)(2,1)S(1)} %get-tuple-element.42.refs_8_.refs_0_.refs_4_.refs_3_.refs_2_.refs_1_.c, ...), custom_call_target="tpu_custom_call" | custom-call | flops 2147483648 | bytes 262144 | tf_op jit(solution)/shard_map/pallas_call | solution.py:50
  25.4 2.7 %collective-permute-start.4 = (bf16[24,1024]{1,0:T(8,128)(2,1)S(1)}, bf16[24,1024]{1,0:T(8,128)(2,1)S(1)}, u32[]{:S(2)}, u32[]{:S(2)}) collective-permute-start(bf16[24,1024]{1,0:T(8,128)(2,1)S(1)} %get-tuple-element.50), channel_id=1, source_target_pairs={{0,4},{1,5},{2,6},{3,7},{4,0},{5,1},{6,2},{7,3},{8,12},{9,13},{10,... | collective-permute-start | bytes 147464 | tf_op jit(solution)/shard_map/ppermute | solution.py:38
  28.0 1.4 %collective-permute-start.5 = (bf16[24,1024]{1,0:T(8,128)(2,1)S(1)}, bf16[24,1024]{1,0:T(8,128)(2,1)S(1)}, u32[]{:S(2)}, u32[]{:S(2)}) collective-permute-start(bf16[24,1024]{1,0:T(8,128)(2,1)S(1)} %get-tuple-element.51), channel_id=1, source_target_pairs={{0,6},{1,7},{2,4},{3,5},{4,2},{5,3},{6,0},{7,1},{8,14},{9,15},{10,... | collective-permute-start | bytes 147464 | tf_op jit(solution)/shard_map/ppermute | solution.py:38
  29.6 1.3 %shard_map.55.refs_0_ = bf16[2048,1024]{1,0:T(8,128)(2,1)S(1)} custom-call(bf16[1024,2048]{1,0:T(8,128)(2,1)S(1)} %get-tuple-element.37.refs_4_.c, f32[24,1024]{1,0:T(8,128)S(1)} %get-tuple-element.49.refs_0_.keep_ref, bf16[1024,2048]{1,0:T(8,128)(2,1)S(1)} %get-tuple-element.38.refs_5_.refs_1_.c, ...), custom_call_target="tpu_custom_call" | custom-call | bytes 262144 | tf_op jit(solution)/shard_map/pallas_call | solution.py:50
  30.9 1.3 %shard_map.56.refs_0_.refs_1_ = bf16[2048,1024]{1,0:T(8,128)(2,1)S(1)} custom-call(bf16[1024,2048]{1,0:T(8,128)(2,1)S(1)} %get-tuple-element.38.refs_5_.refs_1_.c, bf16[2048,1024]{1,0:T(8,128)(2,1)S(1)} %shard_map.55.refs_0_, bf16[1024,2048]{1,0:T(8,128)(2,1)S(1)} %get-tuple-element.40.refs_6_.refs_2_.refs_1_.c, ...), custom_call_target="tpu_custom_call" | custom-call | bytes 262144 | tf_op jit(solution)/shard_map/pallas_call | solution.py:50
  32.2 1.3 %shard_map.57._.refs_2_ = bf16[2048,1024]{1,0:T(8,128)(2,1)S(1)} custom-call(bf16[1024,2048]{1,0:T(8,128)(2,1)S(1)} %get-tuple-element.40.refs_6_.refs_2_.refs_1_.c, bf16[2048,1024]{1,0:T(8,128)(2,1)S(1)} %shard_map.56.refs_0_.refs_1_, bf16[1024,2048]{1,0:T(8,128)(2,1)S(1)} %get-tuple-element.41.refs_7_.refs_3_.refs_2_.refs_1_.c, ...), custom_call_target="tpu_custom_call" | custom-call | bytes 262144 | tf_op jit(solution)/shard_map/pallas_call | solution.py:50
  34.4 2.9 %collective-permute-start.11 = (bf16[24,1024]{1,0:T(8,128)(2,1)S(1)}, bf16[24,1024]{1,0:T(8,128)(2,1)S(1)}, u32[]{:S(2)}, u32[]{:S(2)}) collective-permute-start(bf16[24,1024]{1,0:T(8,128)(2,1)S(1)} %get-tuple-element.56.refs_0_), channel_id=1, source_target_pairs={{0,6},{1,7},{2,4},{3,5},{4,2},{5,3},{6,0},{7,1},{8,14},{9,15},{10,... | collective-permute-start | bytes 147464 | tf_op jit(solution)/shard_map/ppermute | solution.py:38
  37.2 1.6 %collective-permute-start.9 = (bf16[24,1024]{1,0:T(8,128)(2,1)S(1)}, bf16[24,1024]{1,0:T(8,128)(2,1)S(1)}, u32[]{:S(2)}, u32[]{:S(2)}) collective-permute-start(bf16[24,1024]{1,0:T(8,128)(2,1)S(1)} %get-tuple-element.56.refs_0_), channel_id=1, source_target_pairs={{0,2},{1,3},{2,0},{3,1},{4,6},{5,7},{6,4},{7,5},{8,10},{9,11},{10,... | collective-permute-start | bytes 147464 | tf_op jit(solution)/shard_map/ppermute | solution.py:38
  38.8 1.3 %shard_map.60.refs_0_.refs_3_ = bf16[2048,1024]{1,0:T(8,128)(2,1)S(1)} custom-call(bf16[1024,2048]{1,0:T(8,128)(2,1)S(1)} %get-tuple-element.41.refs_7_.refs_3_.refs_2_.refs_1_.c, bf16[24,1024]{1,0:T(8,128)(2,1)S(1)} %get-tuple-element.56.refs_0_, bf16[1024,2048]{1,0:T(8,128)(2,1)S(1)} %get-tuple-element.42.refs_8_.refs_0_.refs_4_.refs_3_.refs_2_.refs_1_.c, ...), custom_call_target="tpu_custom_call" | custom-call | bytes 262144 | tf_op jit(solution)/shard_map/pallas_call | solution.py:50
  40.1 1.3 %shard_map.61.refs_4_.refs_0_ = bf16[2048,1024]{1,0:T(8,128)(2,1)S(1)} custom-call(bf16[1024,2048]{1,0:T(8,128)(2,1)S(1)} %get-tuple-element.42.refs_8_.refs_0_.refs_4_.refs_3_.refs_2_.refs_1_.c, bf16[2048,1024]{1,0:T(8,128)(2,1)S(1)} %shard_map.60.refs_0_.refs_3_, bf16[1024,2048]{1,0:T(8,128)(2,1)S(1)} %get-tuple-element.43.refs_9_.refs_1_.refs_5_.refs_4_.refs_3_.refs_2_, ...), custom_call_target="tpu_custom_call" | custom-call | bytes 262144 | tf_op jit(solution)/shard_map/pallas_call | solution.py:50
  42.5 1.3 %shard_map.66.part_ref = f32[128,4096]{1,0:T(8,128)S(1)} custom-call(bf16[4,32,1024]{2,1,0:T(8,128)(2,1)S(1)} %shard_map.62.mine_ref.refs_2_, bf16[2048,1024]{1,0:T(8,128)(2,1)S(1)} %shard_map.55.refs_0_, bf16[2048,1024]{1,0:T(8,128)(2,1)S(1)} %shard_map.56.refs_0_.refs_1_, bf16[2048,1024]{1,0:T(8,128)(2,1)S(1)} %shard_map.57._.refs_2_, ...), custom_call_target="tpu_custom_call" | custom-call | bytes 262144 | tf_op jit(solution)/shard_map/pallas_call | solution.py:50
  44.1 1.3 %shard_map.67 = (bf16[2,24,4096]{2,1,0:T(8,128)(2,1)S(1)}, f32[24,4096]{1,0:T(8,128)S(1)}, f32[24,4096]{1,0:T(8,128)S(1)}) custom-call(bf16[4,32,1024]{2,1,0:T(8,128)(2,1)S(1)} %collective-permute-done.12.other_ref, f32[128,4096]{1,0:T(8,128)S(1)} %shard_map.66.part_ref, bf16[2048,1024]{1,0:T(8,128)(2,1)S(1)} %shard_map.55.refs_0_, ...), custom_call_target="tpu_custom_call" | custom-call | flops 2147483648 | bytes 262144 | tf_op jit(solution)/shard_map/pallas_call | solution.py:50
  45.3 1.6 %collective-permute-start.15 = (bf16[2,24,4096]{2,1,0:T(8,128)(2,1)S(1)}, bf16[2,24,4096]{2,1,0:T(8,128)(2,1)S(1)}, u32[]{:S(2)}, u32[]{:S(2)}) collective-permute-start(bf16[2,24,4096]{2,1,0:T(8,128)(2,1)S(1)} %get-tuple-element.63), channel_id=1, source_target_pairs={{0,16},{1,9},{2,18},{3,11},{4,20},{5,13},{6,22},{7,15},{8,24},{9,1... | collective-permute-start | bytes 1179656 | tf_op jit(solution)/shard_map/ppermute | solution.py:46
  46.9 1.9 %shard_map.63 = (bf16[2,24,2048]{2,1,0:T(8,128)(2,1)S(1)}, f32[24,2048]{1,0:T(8,128)S(1)}, f32[24,2048]{1,0:T(8,128)S(1)}) custom-call(bf16[4,32,1024]{2,1,0:T(8,128)(2,1)S(1)} %shard_map.62.mine_ref.refs_2_, bf16[4,32,1024]{2,1,0:T(8,128)(2,1)S(1)} %collective-permute-done.12.other_ref, bf16[2048,1024]{1,0:T(8,128)(2,1)S(1)} %shard_map.61.refs_4_.refs_0_, ...), custom_call_target="tpu_custom_call" | custom-call | flops 2147483648 | bytes 262144 | tf_op jit(solution)/shard_map/pallas_call | solution.py:50
  49.4 2.5 %shard_map.64 = (bf16[2,24,2048]{2,1,0:T(8,128)(2,1)S(1)}, f32[24,2048]{1,0:T(8,128)S(1)}, f32[24,2048]{1,0:T(8,128)S(1)}) custom-call(bf16[4,32,1024]{2,1,0:T(8,128)(2,1)S(1)} %shard_map.62.mine_ref.refs_2_, bf16[4,32,1024]{2,1,0:T(8,128)(2,1)S(1)} %collective-permute-done.12.other_ref, ...), custom_call_target="tpu_custom_call" | custom-call | flops 2147483648 | bytes 262144 | tf_op jit(solution)/shard_map/pallas_call | solution.py:50
  51.9 1.6 %collective-permute-start.13 = (bf16[2,24,2048]{2,1,0:T(8,128)(2,1)S(1)}, bf16[2,24,2048]{2,1,0:T(8,128)(2,1)S(1)}, u32[]{:S(2)}, u32[]{:S(2)}) collective-permute-start(bf16[2,24,2048]{2,1,0:T(8,128)(2,1)S(1)} %get-tuple-element.58), channel_id=1, source_target_pairs={{0,16},{1,9},{2,18},{3,11},{4,20},{5,13},{6,22},{7,15},{8,24},{9,1... | collective-permute-start | bytes 589832 | tf_op jit(solution)/shard_map/ppermute | solution.py:46
  53.5 1.8 %collective-permute-done.16.refs_3_ = bf16[2,24,2048]{2,1,0:T(8,128)(2,1)S(1)} collective-permute-done((bf16[2,24,2048]{2,1,0:T(8,128)(2,1)S(1)}, bf16[2,24,2048]{2,1,0:T(8,128)(2,1)S(1)}, u32[]{:S(2)}, u32[]{:S(2)}) %collective-permute-start.16) | collective-permute-done | bytes 196640 | tf_op jit(solution)/shard_map/ppermute | solution.py:46
  60.8 1.4 %collective-permute-done.17.got_ref = bf16[24,6144]{1,0:T(8,128)(2,1)S(1)} collective-permute-done((bf16[24,6144]{1,0:T(8,128)(2,1)S(1)}, bf16[24,6144]{1,0:T(8,128)(2,1)S(1)}, u32[]{:S(2)}, u32[]{:S(2)}) %collective-permute-start.17) | collective-permute-done | bytes 294944 | tf_op jit(solution)/shard_map/ppermute | solution.py:46
  (33 shorter events, 11.3 us)
Async XLA Ops:
  0.6 9.1 %collective-permute-start = (bf16[24,8192]{1,0:T(8,128)(2,1)}, bf16[24,8192]{1,0:T(8,128)(2,1)S(1)}, u32[]{:S(2)}, u32[]{:S(2)}) collective-permute-start(bf16[24,8192]{1,0:T(8,128)(2,1)} %g_ref.1), channel_id=1, source_target_pairs={{0,8},{1,17},{2,10},{3,19},{4,12},{5,21},{6,14},{7,23},{8,0},{9,25... | collective-permute-start | bytes 1179656 | tf_op jit(solution)/shard_map/ppermute | solution.py:46
  7.3 11.9 %collective-permute-start.1 = (bf16[24,8192]{1,0:T(8,128)(2,1)S(1)}, bf16[24,8192]{1,0:T(8,128)(2,1)S(1)}, u32[]{:S(2)}, u32[]{:S(2)}) collective-permute-start(bf16[24,8192]{1,0:T(8,128)(2,1)S(1)} %get-tuple-element.36.refs_0_), channel_id=1, source_target_pairs={{0,16},{1,9},{2,18},{3,11},{4,20},{5,13},{6,22},{7,15},{8,24},{9,1... | collective-permute-start | bytes 1179656 | tf_op jit(solution)/shard_map/ppermute | solution.py:46
  9.7 9.7 %collective-permute-start.2 = (bf16[24,8192]{1,0:T(8,128)(2,1)S(1)}, bf16[24,8192]{1,0:T(8,128)(2,1)S(1)}, u32[]{:S(2)}, u32[]{:S(2)}) collective-permute-start(bf16[24,8192]{1,0:T(8,128)(2,1)S(1)} %collective-permute-done.refs_1_), channel_id=1, source_target_pairs={{0,16},{1,9},{2,18},{3,11},{4,20},{5,13},{6,22},{7,15},{8,24},{9,1... | collective-permute-start | bytes 1179656 | tf_op jit(solution)/shard_map/ppermute | solution.py:46
  23.8 1.5 %collective-permute-start.3 = (bf16[4,24,1024]{2,1,0:T(8,128)(2,1)S(1)}, bf16[4,24,1024]{2,1,0:T(8,128)(2,1)S(1)}, u32[]{:S(2)}, u32[]{:S(2)}) collective-permute-start(bf16[4,24,1024]{2,1,0:T(8,128)(2,1)S(1)} %get-tuple-element.48), channel_id=1, source_target_pairs={{0,1},{1,0},{2,3},{3,2},{4,5},{5,4},{6,7},{7,6},{8,9},{9,8},{10,11... | collective-permute-start | bytes 589832 | tf_op jit(solution)/shard_map/ppermute | solution.py:38
  25.4 8.1 %collective-permute-start.4 = (bf16[24,1024]{1,0:T(8,128)(2,1)S(1)}, bf16[24,1024]{1,0:T(8,128)(2,1)S(1)}, u32[]{:S(2)}, u32[]{:S(2)}) collective-permute-start(bf16[24,1024]{1,0:T(8,128)(2,1)S(1)} %get-tuple-element.50), channel_id=1, source_target_pairs={{0,4},{1,5},{2,6},{3,7},{4,0},{5,1},{6,2},{7,3},{8,12},{9,13},{10,... | collective-permute-start | bytes 147464 | tf_op jit(solution)/shard_map/ppermute | solution.py:38
  28.0 6.2 %collective-permute-start.5 = (bf16[24,1024]{1,0:T(8,128)(2,1)S(1)}, bf16[24,1024]{1,0:T(8,128)(2,1)S(1)}, u32[]{:S(2)}, u32[]{:S(2)}) collective-permute-start(bf16[24,1024]{1,0:T(8,128)(2,1)S(1)} %get-tuple-element.51), channel_id=1, source_target_pairs={{0,6},{1,7},{2,4},{3,5},{4,2},{5,3},{6,0},{7,1},{8,14},{9,15},{10,... | collective-permute-start | bytes 147464 | tf_op jit(solution)/shard_map/ppermute | solution.py:38
  29.4 4.9 %collective-permute-start.6 = (bf16[24,1024]{1,0:T(8,128)(2,1)S(1)}, bf16[24,1024]{1,0:T(8,128)(2,1)S(1)}, u32[]{:S(2)}, u32[]{:S(2)}) collective-permute-start(bf16[24,1024]{1,0:T(8,128)(2,1)S(1)} %get-tuple-element.52), channel_id=1, source_target_pairs={{0,2},{1,3},{2,0},{3,1},{4,6},{5,7},{6,4},{7,5},{8,10},{9,11},{10,... | collective-permute-start | bytes 147464 | tf_op jit(solution)/shard_map/ppermute | solution.py:38
  29.6 3.9 %collective-permute-start.7 = (bf16[12,1024]{1,0:T(8,128)(2,1)S(1)}, bf16[12,1024]{1,0:T(8,128)(2,1)S(1)}, u32[]{:S(2)}, u32[]{:S(2)}) collective-permute-start(bf16[12,1024]{1,0:T(8,128)(2,1)S(1)} %get-tuple-element.53), channel_id=1, source_target_pairs={{0,1},{1,0},{2,3},{3,2},{4,5},{5,4},{6,7},{7,6},{8,9},{9,8},{10,11... | collective-permute-start | bytes 73736 | tf_op jit(solution)/shard_map/ppermute | solution.py:38
  34.4 7.0 %collective-permute-start.11 = (bf16[24,1024]{1,0:T(8,128)(2,1)S(1)}, bf16[24,1024]{1,0:T(8,128)(2,1)S(1)}, u32[]{:S(2)}, u32[]{:S(2)}) collective-permute-start(bf16[24,1024]{1,0:T(8,128)(2,1)S(1)} %get-tuple-element.56.refs_0_), channel_id=1, source_target_pairs={{0,6},{1,7},{2,4},{3,5},{4,2},{5,3},{6,0},{7,1},{8,14},{9,15},{10,... | collective-permute-start | bytes 147464 | tf_op jit(solution)/shard_map/ppermute | solution.py:38
  37.2 5.2 %collective-permute-start.10 = (bf16[24,1024]{1,0:T(8,128)(2,1)S(1)}, bf16[24,1024]{1,0:T(8,128)(2,1)S(1)}, u32[]{:S(2)}, u32[]{:S(2)}) collective-permute-start(bf16[24,1024]{1,0:T(8,128)(2,1)S(1)} %get-tuple-element.56.refs_0_), channel_id=1, source_target_pairs={{0,4},{1,5},{2,6},{3,7},{4,0},{5,1},{6,2},{7,3},{8,12},{9,13},{10,... | collective-permute-start | bytes 147464 | tf_op jit(solution)/shard_map/ppermute | solution.py:38
  37.2 5.2 %collective-permute-start.9 = (bf16[24,1024]{1,0:T(8,128)(2,1)S(1)}, bf16[24,1024]{1,0:T(8,128)(2,1)S(1)}, u32[]{:S(2)}, u32[]{:S(2)}) collective-permute-start(bf16[24,1024]{1,0:T(8,128)(2,1)S(1)} %get-tuple-element.56.refs_0_), channel_id=1, source_target_pairs={{0,2},{1,3},{2,0},{3,1},{4,6},{5,7},{6,4},{7,5},{8,10},{9,11},{10,... | collective-permute-start | bytes 147464 | tf_op jit(solution)/shard_map/ppermute | solution.py:38
  42.5 1.6 %collective-permute-start.12 = (bf16[4,32,1024]{2,1,0:T(8,128)(2,1)S(1)}, bf16[4,32,1024]{2,1,0:T(8,128)(2,1)S(1)}, u32[]{:S(2)}, u32[]{:S(2)}) collective-permute-start(bf16[4,32,1024]{2,1,0:T(8,128)(2,1)S(1)} %shard_map.62.mine_ref.refs_2_), channel_id=1, source_target_pairs={{0,1},{1,0},{2,3},{3,2},{4,5},{5,4},{6,7},{7,6},{8,9},{9,8},{10,11... | collective-permute-start | bytes 786440 | tf_op jit(solution)/shard_map/ppermute | solution.py:38
  45.3 10.0 %collective-permute-start.15 = (bf16[2,24,4096]{2,1,0:T(8,128)(2,1)S(1)}, bf16[2,24,4096]{2,1,0:T(8,128)(2,1)S(1)}, u32[]{:S(2)}, u32[]{:S(2)}) collective-permute-start(bf16[2,24,4096]{2,1,0:T(8,128)(2,1)S(1)} %get-tuple-element.63), channel_id=1, source_target_pairs={{0,16},{1,9},{2,18},{3,11},{4,20},{5,13},{6,22},{7,15},{8,24},{9,1... | collective-permute-start | bytes 1179656 | tf_op jit(solution)/shard_map/ppermute | solution.py:46
  48.9 6.4 %collective-permute-start.16 = (bf16[2,24,2048]{2,1,0:T(8,128)(2,1)S(1)}, bf16[2,24,2048]{2,1,0:T(8,128)(2,1)S(1)}, u32[]{:S(2)}, u32[]{:S(2)}) collective-permute-start(bf16[2,24,2048]{2,1,0:T(8,128)(2,1)S(1)} %get-tuple-element.66), channel_id=1, source_target_pairs={{0,16},{1,9},{2,18},{3,11},{4,20},{5,13},{6,22},{7,15},{8,24},{9,1... | collective-permute-start | bytes 589832 | tf_op jit(solution)/shard_map/ppermute | solution.py:46
  51.9 5.8 %collective-permute-start.13 = (bf16[2,24,2048]{2,1,0:T(8,128)(2,1)S(1)}, bf16[2,24,2048]{2,1,0:T(8,128)(2,1)S(1)}, u32[]{:S(2)}, u32[]{:S(2)}) collective-permute-start(bf16[2,24,2048]{2,1,0:T(8,128)(2,1)S(1)} %get-tuple-element.58), channel_id=1, source_target_pairs={{0,16},{1,9},{2,18},{3,11},{4,20},{5,13},{6,22},{7,15},{8,24},{9,1... | collective-permute-start | bytes 589832 | tf_op jit(solution)/shard_map/ppermute | solution.py:46
  55.4 6.8 %collective-permute-start.17 = (bf16[24,6144]{1,0:T(8,128)(2,1)S(1)}, bf16[24,6144]{1,0:T(8,128)(2,1)S(1)}, u32[]{:S(2)}, u32[]{:S(2)}) collective-permute-start(bf16[24,6144]{1,0:T(8,128)(2,1)S(1)} %get-tuple-element.69), channel_id=1, source_target_pairs={{0,8},{1,17},{2,10},{3,19},{4,12},{5,21},{6,14},{7,23},{8,0},{9,25... | collective-permute-start | bytes 884744 | tf_op jit(solution)/shard_map/ppermute | solution.py:46
  57.7 5.5 %collective-permute-start.14 = (bf16[24,2048]{1,0:T(8,128)(2,1)S(1)}, bf16[24,2048]{1,0:T(8,128)(2,1)S(1)}, u32[]{:S(2)}, u32[]{:S(2)}) collective-permute-start(bf16[24,2048]{1,0:T(8,128)(2,1)S(1)} %get-tuple-element.62), channel_id=1, source_target_pairs={{0,8},{1,17},{2,10},{3,19},{4,12},{5,21},{6,14},{7,23},{8,0},{9,25... | collective-permute-start | bytes 294920 | tf_op jit(solution)/shard_map/ppermute | solution.py:46
  58.9 1.3 %collective-permute-start.8 = (f32[12,1024]{1,0:T(8,128)S(1)}, f32[12,1024]{1,0:T(8,128)S(1)}, u32[]{:S(2)}, u32[]{:S(2)}) collective-permute-start(f32[12,1024]{1,0:T(8,128)S(1)} %get-tuple-element.55), channel_id=1, source_target_pairs={{0,1},{1,0},{2,3},{3,2},{4,5},{5,4},{6,7},{7,6},{8,9},{9,8},{10,11... | collective-permute-start | bytes 147464 | tf_op jit(solution)/shard_map/ppermute | solution.py:38
